TPU v7x, 32 devices: a whole 2x2x4 slice. The times are simulated.
32 devices in a mesh: dp: 8 (over y, x, core), tensor: 4 (over z).
Axes of the slice: x: 2, y: 2, z: 4, core: 2. Of those that a mesh axis runs over, the one named last changes fastest.
Arguments:
- tokens: bfloat16 [12288, 2560], P(('dp', 'tensor')), may hold values from -6 to 6
- attention_gain: bfloat16 [2560], P('dp'), may hold values from 0.25 to 1.75
- query_weight: bfloat16 [2560, 2560], P('dp', 'tensor'), may hold values from -0.125 to 0.125
- key_weight: bfloat16 [2560, 640], P('dp', 'tensor'), may hold values from -0.125 to 0.125
- value_weight: bfloat16 [2560, 640], P('dp', 'tensor'), may hold values from -0.125 to 0.125
- output_weight: bfloat16 [2560, 2560], P('tensor', 'dp'), may hold values from -1.25 to 1.25
- feedforward_gain: bfloat16 [2560], P('dp'), may hold values from 0.25 to 1.75
- gate_weight: bfloat16 [2560, 6912], P('dp', 'tensor'), may hold values from -0.125 to 0.125
- up_weight: bfloat16 [2560, 6912], P('dp', 'tensor'), may hold values from -0.125 to 0.125
- down_weight: bfloat16 [6912, 2560], P('tensor', 'dp'), may hold values from -0.15625 to 0.15625
- cotangent: bfloat16 [12288, 2560], P(('dp', 'tensor')), may hold values from -6 to 6
- lengths: int32 [8, 3], P('dp'), may hold values from 1 to 1024, 1536 in all within a row
- storage_order: int32 [12288], P('dp'), may hold values from 0 to 1535, as said below
- sequence_order: int32 [12288], P('dp'), may hold values from 0 to 1535, as said below
- pad_mask: int32 [12288], P('dp'), may hold values 0 or 1
Outputs:
- layer_output: float32 [12288, 2560], P(('dp', 'tensor'))
- input_grad: float32 [12288, 2560], P(('dp', 'tensor'))
- attention_gain_grad: float32 [2560], P('dp')
- query_weight_grad: float32 [2560, 2560], P('dp', 'tensor')
- key_weight_grad: float32 [2560, 640], P('dp', 'tensor')
- value_weight_grad: float32 [2560, 640], P('dp', 'tensor')
- output_weight_grad: float32 [2560, 2560], P('tensor', 'dp')
- feedforward_gain_grad: float32 [2560], P('dp')
- gate_weight_grad: float32 [2560, 6912], P('dp', 'tensor')
- up_weight_grad: float32 [2560, 6912], P('dp', 'tensor')
- down_weight_grad: float32 [6912, 2560], P('tensor', 'dp')
Inputs may be any that keep to these rules, and one draw needn't show every extreme that they name: Each group's 3 lengths add up to 1536, and the longest is 1024. `storage_order`: each group's 1536 entries are a permutation of its sequence positions. `sequence_order`: each group's 1536 entries are the inverse of that group's storage_order.
All inputs are finite; a program needn't handle non-finite values. No bound on the sum of `pad_mask` on one device may be relied on, other than what follows from the above.
Results may differ from a plain program's by a relative error of at most 0.02.
Values may be sent and summed in bfloat16 or wider, within the bound.
A program may use at most 320 MiB of HBM per device.

v0:
```python
import math

import jax
import jax.numpy as jnp
from jax import lax
from jax.sharding import PartitionSpec as P

HEAD_DIM = 80


epsilon = 1e-05
rope_base = 10000.0


def inverse_root(vectors):
    return lax.rsqrt(jnp.mean(vectors * vectors, axis=-1, keepdims=True) + epsilon)


def sequence_layout(length_row, token_count):
    sequence_ends = jnp.cumsum(length_row)
    sequence_starts = sequence_ends - length_row
    places = jnp.arange(token_count, dtype=jnp.int32)
    members = jnp.sum((places[:, None] >= sequence_ends[None, :]).astype(jnp.int32), axis=1)
    chosen = members[:, None] == jnp.arange(length_row.shape[0], dtype=jnp.int32)[None, :]
    first_place = jnp.sum(jnp.where(chosen, sequence_starts[None, :], 0), axis=1)
    return (members, places - first_place)


def rotary_tables(positions, head_width):
    half_width = head_width // 2
    frequency = jnp.exp(
        jnp.arange(half_width, dtype=jnp.float32) * (-2.0 * math.log(rope_base) / head_width)
    )
    angles = positions.astype(jnp.float32)[:, None] * frequency[None, :]
    return (jnp.cos(angles), jnp.sin(angles))


def rotate(vectors, cosine_table, sine_table):
    half_width = vectors.shape[-1] // 2
    leading = vectors[..., :half_width]
    trailing = vectors[..., half_width:]
    cosine = cosine_table[:, None, :]
    sine_part = sine_table[:, None, :]
    return jnp.concatenate(
        [leading * cosine - trailing * sine_part, trailing * cosine + leading * sine_part], axis=-1
    )


def unrotate(vectors, cosine_table, sine_table):
    half_width = vectors.shape[-1] // 2
    leading = vectors[..., :half_width]
    trailing = vectors[..., half_width:]
    cosine = cosine_table[:, None, :]
    sine_part = sine_table[:, None, :]
    return jnp.concatenate(
        [leading * cosine + trailing * sine_part, trailing * cosine - leading * sine_part], axis=-1
    )


def gather_attention(attention_gain, query_weight, key_weight, value_weight, output_weight):
    return (
        lax.all_gather(attention_gain, "dp", axis=0, tiled=True),
        lax.all_gather(query_weight, "dp", axis=0, tiled=True),
        lax.all_gather(key_weight, "dp", axis=0, tiled=True),
        lax.all_gather(value_weight, "dp", axis=0, tiled=True),
        lax.all_gather(output_weight, "dp", axis=1, tiled=True),
    )


def gather_feedforward(feedforward_gain, gate_weight, up_weight, down_weight):
    return (
        lax.all_gather(feedforward_gain, "dp", axis=0, tiled=True),
        lax.all_gather(gate_weight, "dp", axis=0, tiled=True),
        lax.all_gather(up_weight, "dp", axis=0, tiled=True),
        lax.all_gather(down_weight, "dp", axis=1, tiled=True),
    )


def block_scores(query_heads, key_heads, members, pad_keys, block_start, block_rows):
    token_count = key_heads.shape[0]
    row_index = block_start + jnp.arange(block_rows, dtype=jnp.int32)
    columns = jnp.arange(token_count, dtype=jnp.int32)
    owners = lax.dynamic_slice_in_dim(members, block_start, block_rows, 0)
    allowed = (
        (owners[:, None] == members[None, :])
        & (columns[None, :] <= row_index[:, None])
        & ((pad_keys[None, :] == 1) | (columns[None, :] == row_index[:, None]))
    )
    query_block = lax.dynamic_slice_in_dim(query_heads, block_start, block_rows, 0)
    scores = jnp.einsum(
        "qkge,ske->kgqs", query_block, key_heads, preferred_element_type=jnp.float32
    ) * (1.0 / math.sqrt(query_heads.shape[-1]))
    return (query_block, jnp.where(allowed[None, None], scores, -1e30))


def attention_forward(query_heads, key_heads, value_heads, members, pad_keys):
    token_count = query_heads.shape[0]
    block_rows = math.gcd(token_count, 512)

    def one_block(block_start):
        query_block, scores = block_scores(
            query_heads, key_heads, members, pad_keys, block_start, block_rows
        )
        row_top = jnp.max(scores, axis=-1, keepdims=True)
        exponent = jnp.exp(scores - row_top)
        row_total = jnp.sum(exponent, axis=-1, keepdims=True)
        probability = (exponent / row_total).astype(jnp.bfloat16)
        attended = jnp.einsum(
            "kgqs,ske->qkge", probability, value_heads, preferred_element_type=jnp.float32
        )
        return (attended, row_top[..., 0] + jnp.log(row_total[..., 0]))

    block_starts = jnp.arange(token_count // block_rows, dtype=jnp.int32) * block_rows
    attended, log_totals = lax.map(one_block, block_starts)
    return (attended.reshape(query_heads.shape), log_totals)


def attention_backward(
    query_heads, key_heads, value_heads, members, pad_keys, log_totals, grad_attended
):
    token_count = query_heads.shape[0]
    key_count = key_heads.shape[1]
    head_width = query_heads.shape[-1]
    block_rows = math.gcd(token_count, 512)
    score_scale = 1.0 / math.sqrt(head_width)

    def one_block(carried, scan_item):
        block_start, block_totals = scan_item
        grad_keys, grad_values = carried
        query_block, scores = block_scores(
            query_heads, key_heads, members, pad_keys, block_start, block_rows
        )
        probability = jnp.exp(scores - block_totals[..., None])
        grad_block = lax.dynamic_slice_in_dim(grad_attended, block_start, block_rows, 0)
        grad_values = grad_values + jnp.einsum(
            "kgqs,qkge->ske",
            probability.astype(jnp.bfloat16),
            grad_block,
            preferred_element_type=jnp.float32,
        )
        grad_probability = jnp.einsum(
            "qkge,ske->kgqs", grad_block, value_heads, preferred_element_type=jnp.float32
        )
        row_inner = jnp.sum(probability * grad_probability, axis=-1, keepdims=True)
        grad_scores = (probability * (grad_probability - row_inner)).astype(jnp.bfloat16)
        grad_query = (
            jnp.einsum("kgqs,ske->qkge", grad_scores, key_heads, preferred_element_type=jnp.float32)
            * score_scale
        )
        grad_keys = (
            grad_keys
            + jnp.einsum(
                "kgqs,qkge->ske", grad_scores, query_block, preferred_element_type=jnp.float32
            )
            * score_scale
        )
        return ((grad_keys, grad_values), grad_query)

    blank_state = jnp.zeros((token_count, key_count, head_width), jnp.float32)
    block_starts = jnp.arange(token_count // block_rows, dtype=jnp.int32) * block_rows
    (grad_keys, grad_values), grad_query = lax.scan(
        one_block, (blank_state, blank_state), (block_starts, log_totals)
    )
    return (grad_query.reshape(query_heads.shape), grad_keys, grad_values)


def attention_sublayer(residual_in, parameters, tables):
    gain_vector, query_weight, key_weight, value_weight, output_weight = parameters
    members, pad_keys, cosine_table, sine_table, sequence_order, storage_order = tables
    scale_rows = inverse_root(residual_in)
    local_in = (residual_in * scale_rows * gain_vector.astype(jnp.float32)).astype(jnp.bfloat16)
    normed = lax.all_gather(local_in, "tensor", axis=0, tiled=True)
    token_count = normed.shape[0]
    key_count = key_weight.shape[1] // HEAD_DIM
    head_group = query_weight.shape[1] // key_weight.shape[1]
    query_rows = jnp.dot(normed, query_weight, preferred_element_type=jnp.float32)[sequence_order]
    query_heads = rotate(
        query_rows.reshape(token_count, key_count * head_group, HEAD_DIM), cosine_table, sine_table
    )
    query_heads = query_heads.astype(jnp.bfloat16).reshape(
        token_count, key_count, head_group, HEAD_DIM
    )
    key_rows = jnp.dot(normed, key_weight, preferred_element_type=jnp.float32)[sequence_order]
    key_heads = rotate(
        key_rows.reshape(token_count, key_count, HEAD_DIM), cosine_table, sine_table
    ).astype(jnp.bfloat16)
    value_rows = jnp.dot(normed, value_weight, preferred_element_type=jnp.float32)[sequence_order]
    value_heads = value_rows.reshape(token_count, key_count, HEAD_DIM).astype(jnp.bfloat16)
    attended, log_totals = attention_forward(query_heads, key_heads, value_heads, members, pad_keys)
    attended_low = attended.reshape(token_count, -1).astype(jnp.bfloat16)[storage_order]
    attention_out = lax.psum_scatter(
        jnp.dot(attended_low, output_weight, preferred_element_type=jnp.float32),
        "tensor",
        scatter_dimension=0,
        tiled=True,
    )
    saved_state = (
        scale_rows,
        normed,
        query_heads,
        key_heads,
        value_heads,
        log_totals,
        attended_low,
    )
    return (residual_in + attention_out, saved_state)


def feedforward_front(residual_in, parameters):
    gain_vector, gate_weight, up_weight, down_weight = parameters
    scale_rows = inverse_root(residual_in)
    local_in = (residual_in * scale_rows * gain_vector.astype(jnp.float32)).astype(jnp.bfloat16)
    normed = lax.all_gather(local_in, "tensor", axis=0, tiled=True)
    gate_values = jnp.dot(normed, gate_weight, preferred_element_type=jnp.float32)
    up_values = jnp.dot(normed, up_weight, preferred_element_type=jnp.float32)
    hidden = (gate_values * jax.nn.sigmoid(gate_values) * up_values).astype(jnp.bfloat16)
    return (scale_rows, normed, gate_values, up_values, hidden)


def norm_backward(residual_in, scale_rows, gain_vector, grad_normed):
    normed = residual_in * scale_rows
    scaled = grad_normed * gain_vector
    gain_grad = jnp.sum(grad_normed * normed, axis=0)
    grad_input = scale_rows * (scaled - normed * jnp.mean(scaled * normed, axis=-1, keepdims=True))
    return (grad_input, gain_grad)


def per_device(
    tokens,
    attention_gain,
    query_weight,
    key_weight,
    value_weight,
    output_weight,
    feedforward_gain,
    gate_weight,
    up_weight,
    down_weight,
    cotangent,
    lengths,
    storage_order,
    sequence_order,
    pad_mask,
):
    token_count = storage_order.shape[0]
    members, positions = sequence_layout(lengths[0], token_count)
    cosine_table, sine_table = rotary_tables(positions, HEAD_DIM)
    tables = (members, pad_mask, cosine_table, sine_table, sequence_order, storage_order)
    residual_in = tokens.astype(jnp.float32)
    attn_params = gather_attention(
        attention_gain, query_weight, key_weight, value_weight, output_weight
    )
    ffn_params = gather_feedforward(feedforward_gain, gate_weight, up_weight, down_weight)
    residual_first, state_first = attention_sublayer(residual_in, attn_params, tables)
    front_part = feedforward_front(residual_first, ffn_params)
    forward_hidden = front_part[4]
    layer_output = residual_first + lax.psum_scatter(
        jnp.dot(forward_hidden, ffn_params[3], preferred_element_type=jnp.float32).astype(
            jnp.bfloat16
        ),
        "tensor",
        scatter_dimension=0,
        tiled=True,
    ).astype(jnp.float32)
    attn_again = gather_attention(
        attention_gain, query_weight, key_weight, value_weight, output_weight
    )
    ffn_again = gather_feedforward(feedforward_gain, gate_weight, up_weight, down_weight)
    residual, saved_state = attention_sublayer(residual_in, attn_again, tables)
    scale_ffn, normed_ffn, gate_values, up_values, hidden = feedforward_front(residual, ffn_again)
    cot_rows = lax.all_gather(cotangent, "tensor", axis=0, tiled=True)
    down_grad = jnp.einsum("tf,td->fd", hidden, cot_rows, preferred_element_type=jnp.float32)
    grad_hidden = jnp.einsum(
        "td,fd->tf", cot_rows, ffn_again[3], preferred_element_type=jnp.float32
    )
    sigmoid_gate = jax.nn.sigmoid(gate_values)
    grad_gate = (
        grad_hidden * up_values * sigmoid_gate * (1.0 + gate_values * (1.0 - sigmoid_gate))
    ).astype(jnp.bfloat16)
    grad_up = (grad_hidden * gate_values * sigmoid_gate).astype(jnp.bfloat16)
    gate_grad = jnp.einsum("td,tf->df", normed_ffn, grad_gate, preferred_element_type=jnp.float32)
    up_grad = jnp.einsum("td,tf->df", normed_ffn, grad_up, preferred_element_type=jnp.float32)
    grad_normed_ffn = lax.psum_scatter(
        (
            jnp.einsum("tf,df->td", grad_gate, ffn_again[1], preferred_element_type=jnp.float32)
            + jnp.einsum("tf,df->td", grad_up, ffn_again[2], preferred_element_type=jnp.float32)
        ).astype(jnp.bfloat16),
        "tensor",
        scatter_dimension=0,
        tiled=True,
    ).astype(jnp.float32)
    grad_residual, ffn_gain_part = norm_backward(
        residual, scale_ffn, ffn_again[0].astype(jnp.float32), grad_normed_ffn
    )
    grad_residual = grad_residual + cotangent.astype(jnp.float32)
    scale_attn, normed, query_heads, key_heads, value_heads, log_totals, attended_low = saved_state
    key_count = key_heads.shape[1]
    head_group = query_heads.shape[2]
    grad_attention = grad_residual.astype(jnp.bfloat16)
    grad_rows = lax.all_gather(grad_attention, "tensor", axis=0, tiled=True)
    output_grad = jnp.einsum(
        "tc,td->cd", attended_low, grad_rows, preferred_element_type=jnp.float32
    )
    grad_attended = jnp.einsum(
        "td,cd->tc", grad_rows, attn_again[4], preferred_element_type=jnp.float32
    ).astype(jnp.bfloat16)
    grad_attended = grad_attended[sequence_order].reshape(
        token_count, key_count, head_group, HEAD_DIM
    )
    grad_query, grad_keys, grad_values = attention_backward(
        query_heads, key_heads, value_heads, members, pad_mask, log_totals, grad_attended
    )
    grad_query = unrotate(
        grad_query.reshape(token_count, key_count * head_group, HEAD_DIM), cosine_table, sine_table
    )
    grad_query = grad_query.astype(jnp.bfloat16).reshape(token_count, -1)[storage_order]
    grad_keys = (
        unrotate(grad_keys, cosine_table, sine_table)
        .astype(jnp.bfloat16)
        .reshape(token_count, -1)[storage_order]
    )
    grad_values = grad_values.astype(jnp.bfloat16).reshape(token_count, -1)[storage_order]
    query_grad = jnp.einsum("td,tc->dc", normed, grad_query, preferred_element_type=jnp.float32)
    key_grad = jnp.einsum("td,tc->dc", normed, grad_keys, preferred_element_type=jnp.float32)
    value_grad = jnp.einsum("td,tc->dc", normed, grad_values, preferred_element_type=jnp.float32)
    summed = jnp.einsum("tc,dc->td", grad_query, attn_again[1], preferred_element_type=jnp.float32)
    summed = summed + jnp.einsum(
        "tc,dc->td", grad_keys, attn_again[2], preferred_element_type=jnp.float32
    )
    grad_normed = lax.psum_scatter(
        (
            summed
            + jnp.einsum(
                "tc,dc->td", grad_values, attn_again[3], preferred_element_type=jnp.float32
            )
        ).astype(jnp.bfloat16),
        "tensor",
        scatter_dimension=0,
        tiled=True,
    ).astype(jnp.float32)
    grad_tokens, attn_gain_part = norm_backward(
        residual_in, scale_attn, attn_again[0].astype(jnp.float32), grad_normed
    )
    input_grad = grad_residual + grad_tokens
    summed_all = (
        lax.psum_scatter(
            attn_gain_part.astype(jnp.bfloat16), "dp", scatter_dimension=0, tiled=True
        ).astype(jnp.float32),
        lax.psum_scatter(
            query_grad.astype(jnp.bfloat16), "dp", scatter_dimension=0, tiled=True
        ).astype(jnp.float32),
        lax.psum_scatter(
            key_grad.astype(jnp.bfloat16), "dp", scatter_dimension=0, tiled=True
        ).astype(jnp.float32),
        lax.psum_scatter(
            value_grad.astype(jnp.bfloat16), "dp", scatter_dimension=0, tiled=True
        ).astype(jnp.float32),
        lax.psum_scatter(
            output_grad.astype(jnp.bfloat16), "dp", scatter_dimension=1, tiled=True
        ).astype(jnp.float32),
        lax.psum_scatter(
            ffn_gain_part.astype(jnp.bfloat16), "dp", scatter_dimension=0, tiled=True
        ).astype(jnp.float32),
        lax.psum_scatter(
            gate_grad.astype(jnp.bfloat16), "dp", scatter_dimension=0, tiled=True
        ).astype(jnp.float32),
        lax.psum_scatter(
            up_grad.astype(jnp.bfloat16), "dp", scatter_dimension=0, tiled=True
        ).astype(jnp.float32),
        lax.psum_scatter(
            down_grad.astype(jnp.bfloat16), "dp", scatter_dimension=1, tiled=True
        ).astype(jnp.float32),
    )
    attn_sums = summed_all[:5]
    ffn_sums = summed_all[5:]
    gain_sums = lax.psum((attn_sums[0], ffn_sums[0]), "tensor")
    return (
        layer_output,
        input_grad,
        gain_sums[0],
        attn_sums[1],
        attn_sums[2],
        attn_sums[3],
        attn_sums[4],
        gain_sums[1],
        ffn_sums[1],
        ffn_sums[2],
        ffn_sums[3],
    )


def solution(mesh):
    placed = (
        P(("dp", "tensor"), None),
        P("dp"),
        P("dp", "tensor"),
        P("dp", "tensor"),
        P("dp", "tensor"),
        P("tensor", "dp"),
        P("dp"),
        P("dp", "tensor"),
        P("dp", "tensor"),
        P("tensor", "dp"),
        P(("dp", "tensor"), None),
        P("dp", None),
        P("dp"),
        P("dp"),
        P("dp"),
    )
    return jax.shard_map(
        per_device,
        mesh=mesh,
        in_specs=placed,
        out_specs=(
            P(("dp", "tensor"), None),
            P(("dp", "tensor"), None),
            P("dp"),
            P("dp", "tensor"),
            P("dp", "tensor"),
            P("dp", "tensor"),
            P("tensor", "dp"),
            P("dp"),
            P("dp", "tensor"),
            P("dp", "tensor"),
            P("tensor", "dp"),
        ),
        check_vma=False,
    )
```

profile of v0, /device:TPU:0, one launch (start us, length us, event | category | flops | bytes accessed | tf_op | source)
XLA Modules:
  0.0 2964.4 jit_solution(16399657833730471692)
XLA Ops:
  70.9 112.7 %all-gather.13.cloned.1.call-done = bf16[1536,2560]{1,0:T(8,128)(2,1)} async-done(((bf16[384,2560]{1,0:T(8,128)(2,1)}), bf16[1536,2560]{1,0:T(8,128)(2,1)}) %all-gather.13.cloned.1.call-update) | async-done | bytes 7864336 | tf_op jit(solution)/shard_map/all_gather | solution.py:172
  245.8 121.9 %while.38 = (s32[]{:T(128)}, bf16[3,512,2,4,80]{1,4,3,2,0:T(8,128)(2,1)}, f32[3,2,4,512]{3,2,1,0:T(4,128)}, s32[3]{0:T(128)S(1)}, s32[1536]{0:T(1024)S(1)}, /*in...) while((s32[]{:T(128)}, ...), condition=%wide.region_14.15_spmd, body=%wide.region_11.14_spmd.sunk | while | flops 2093479936 | bytes 97477880 | solution.py:114
  398.5 262.1 %reduce-scatter.21.cloned.1.call-done = f32[384,2560]{1,0:T(8,128)} async-done(((f32[1536,2560]{1,0:T(8,128)}), f32[384,2560]{1,0:T(8,128)}) %reduce-scatter.21.cloned.1.call-update) | async-done | bytes 3932176 | tf_op jit(solution)/shard_map/reduce_scatter | solution.py:191
  669.9 94.9 %while.37 = (s32[]{:T(128)}, bf16[3,512,2,4,80]{1,4,3,2,0:T(8,128)(2,1)}, s32[3]{0:T(128)S(1)}, s32[1536]{0:T(1024)S(1)}, s32[1536]{0:T(1024)S(1)}, /*index=5*/b...) while((s32[]{:T(128)}, ...), condition=%wide.region_7.8_spmd, body=%wide.region_4.7_spmd.sunk | while | flops 2055736832 | bytes 54912176 | solution.py:114
  794.1 70.1 %all-gather.29.cloned.1.call-done = bf16[1536,2560]{1,0:T(8,128)(2,1)} async-done(((bf16[384,2560]{1,0:T(8,128)(2,1)}), bf16[1536,2560]{1,0:T(8,128)(2,1)}) %all-gather.29.cloned.1.call-update) | async-done | bytes 7864336 | tf_op jit(solution)/shard_map/all_gather | solution.py:213
  884.9 37.2 %all-gather.23.cloned.1.call-done = bf16[2560,1728]{1,0:T(8,128)(2,1)} async-done(((bf16[320,1728]{1,0:T(8,128)(2,1)}), bf16[2560,1728]{1,0:T(8,128)(2,1)}) %all-gather.23.cloned.1.call-update) | async-done | bytes 8847376 | tf_op jit(solution)/shard_map/all_gather | solution.py:74
  942.7 122.1 %all-gather.27.cloned.1.call-done = bf16[1536,2560]{1,0:T(8,128)(2,1)} async-done(((bf16[384,2560]{1,0:T(8,128)(2,1)}), bf16[1536,2560]{1,0:T(8,128)(2,1)}) %all-gather.27.cloned.1.call-update) | async-done | bytes 7864336 | tf_op jit(solution)/shard_map/all_gather | solution.py:271
  1064.8 57.9 %all-gather.25.cloned.1.call-done = bf16[1728,2560]{0,1:T(8,128)(2,1)} async-done(((bf16[1728,320]{0,1:T(8,128)(2,1)}), bf16[1728,2560]{0,1:T(8,128)(2,1)}) %all-gather.25.cloned.1.call-update) | async-done | bytes 8847376 | tf_op jit(solution)/shard_map/all_gather | solution.py:75
  1122.6 27.8 multiply_convert_fusion.1
  1195.9 191.6 %reduce-scatter.17.cloned.1.call-done = f32[384,2560]{1,0:T(8,128)} async-done(((f32[1536,2560]{1,0:T(8,128)}), f32[384,2560]{1,0:T(8,128)}) %reduce-scatter.17.cloned.1.call-update) | async-done | bytes 3932176 | tf_op jit(solution)/shard_map/reduce_scatter | solution.py:191
  1387.5 139.6 %reduce-scatter.23.cloned.1.call-done = bf16[384,2560]{1,0:T(8,128)(2,1)} async-done(((bf16[1536,2560]{1,0:T(8,128)(2,1)}), bf16[384,2560]{1,0:T(8,128)(2,1)}) %reduce-scatter.23.cloned.1.call-update) | async-done | bytes 1966096 | tf_op jit(solution)/shard_map/reduce_scatter | solution.py:283
  1537.7 141.6 %all-gather.31.cloned.1.call-done = bf16[1536,2560]{1,0:T(8,128)(2,1)} async-done(((bf16[384,2560]{1,0:T(8,128)(2,1)}), bf16[1536,2560]{1,0:T(8,128)(2,1)}) %all-gather.31.cloned.1.call-update) | async-done | bytes 7864336 | tf_op jit(solution)/shard_map/all_gather | solution.py:300
  1698.5 344.6 %while.39 = (s32[]{:T(128)}, f32[1536,2,80]{0,2,1:T(8,128)}, f32[1536,2,80]{0,2,1:T(8,128)}, f32[3,512,2,4,80]{1,0,4,3,2:T(4,128)}, s32[3]{0:T(128)S(1)}, /*inde...) while((s32[]{:T(128)}, f32[1536,2,80]{0,2,1:T(8,128)}, ...), condition=%wide.region_21.22_spmd.clone, body=%wide.region_19.21_spmd.clone.sunk | while | flops 5096060928 | bytes 255337744 | solution.py:161
  1902.2 26.0 dynamic_update_slice.25
  2108.9 133.2 %reduce-scatter.25.cloned.1.call-done = bf16[384,2560]{1,0:T(8,128)(2,1)} async-done(((bf16[1536,2560]{1,0:T(8,128)(2,1)}), bf16[384,2560]{1,0:T(8,128)(2,1)}) %reduce-scatter.25.cloned.1.call-update) | async-done | bytes 1966096 | tf_op jit(solution)/shard_map/reduce_scatter | solution.py:330
  2253.5 26.3 convolution_convert_fusion.2
  2356.9 38.2 %all-gather.19.cloned.1.call-done = bf16[1536,2560]{1,0:T(8,128)(2,1)} async-done(((bf16[384,2560]{1,0:T(8,128)(2,1)}), bf16[1536,2560]{1,0:T(8,128)(2,1)}) %all-gather.19.cloned.1.call-update) | async-done | bytes 7864336 | tf_op jit(solution)/shard_map/all_gather | solution.py:213
  2474.7 76.2 %reduce-scatter.33.cloned.1.call-done = bf16[320,1728]{1,0:T(8,128)(2,1)} async-done(((bf16[2560,1728]{1,0:T(8,128)(2,1)}), bf16[320,1728]{1,0:T(8,128)(2,1)}) %reduce-scatter.33.cloned.1.call-update) | async-done | bytes 1105936 | tf_op jit(solution)/shard_map/reduce_scatter | solution.py:367
  2553.8 75.7 %reduce-scatter.31.cloned.1.call-done = bf16[320,1728]{1,0:T(8,128)(2,1)} async-done(((bf16[2560,1728]{1,0:T(8,128)(2,1)}), bf16[320,1728]{1,0:T(8,128)(2,1)}) %reduce-scatter.31.cloned.1.call-update) | async-done | bytes 1105936 | tf_op jit(solution)/shard_map/reduce_scatter | solution.py:364
  2632.3 38.0 %reduce-scatter.39.cloned.1.call-done = bf16[320,160]{1,0:T(8,128)(2,1)} async-done(((bf16[2560,160]{1,0:T(8,128)(2,1)}), bf16[320,160]{1,0:T(8,128)(2,1)}) %reduce-scatter.39.cloned.1.call-update) | async-done | bytes 102416
  2672.0 39.2 %reduce-scatter.37.cloned.1.call-done = bf16[320,160]{1,0:T(8,128)(2,1)} async-done(((bf16[2560,160]{1,0:T(8,128)(2,1)}), bf16[320,160]{1,0:T(8,128)(2,1)}) %reduce-scatter.37.cloned.1.call-update) | async-done | bytes 102416
  2713.0 48.8 %reduce-scatter.29.cloned.1.call-done = bf16[640,320]{0,1:T(8,128)(2,1)} async-done(((bf16[640,2560]{0,1:T(8,128)(2,1)}), bf16[640,320]{0,1:T(8,128)(2,1)}) %reduce-scatter.29.cloned.1.call-update) | async-done | bytes 409616 | tf_op jit(solution)/shard_map/reduce_scatter | solution.py:358
  2763.7 49.3 %reduce-scatter.27.cloned.1.call-done = bf16[320,640]{1,0:T(8,128)(2,1)} async-done(((bf16[2560,640]{1,0:T(8,128)(2,1)}), bf16[320,640]{1,0:T(8,128)(2,1)}) %reduce-scatter.27.cloned.1.call-update) | async-done | bytes 409616 | tf_op jit(solution)/shard_map/reduce_scatter | solution.py:349
  2851.2 100.8 %reduce-scatter.19.cloned.1.call-done = bf16[384,2560]{1,0:T(8,128)(2,1)} async-done(((bf16[1536,2560]{1,0:T(8,128)(2,1)}), bf16[384,2560]{1,0:T(8,128)(2,1)}) %reduce-scatter.19.cloned.1.call-update) | async-done | bytes 1966096 | tf_op jit(solution)/shard_map/reduce_scatter | solution.py:257
  (373 shorter events, 1114.6 us)
Async XLA Ops:
  7.2 176.5 %all-gather.13.cloned.1.call-start = ((), (), s32[]{:S(2)}) async-start(), calls=%async_computation.12 | async-start | bytes 9830400 | tf_op jit(solution)/shard_map/all_gather | solution.py:172
  42.5 174.1 %all-gather.15.cloned.1.call-start = ((), (), s32[]{:S(2)}) async-start(), calls=%async_computation.13 | async-start | bytes 3686400 | tf_op jit(solution)/shard_map/all_gather | solution.py:63
  43.3 342.5 %all-gather.17.cloned.1.call-start = ((), (), s32[]{:S(2)}) async-start(), calls=%async_computation.14 | async-start | bytes 3686400 | tf_op jit(solution)/shard_map/all_gather | solution.py:66
  44.0 616.6 %reduce-scatter.21.cloned.1.call-start = ((), (), s32[]{:S(2)}) async-start(), calls=%async_computation.21 | async-start | bytes 19660800 | tf_op jit(solution)/shard_map/reduce_scatter | solution.py:191
  397.8 396.3 %all-gather.21.cloned.1.call-start = ((), (), s32[]{:S(2)}) async-start(), calls=%async_computation.17 | async-start | bytes 10321920 | tf_op jit(solution)/shard_map/all_gather | solution.py:73
  398.4 465.8 %all-gather.29.cloned.1.call-start = ((), (), s32[]{:S(2)}) async-start(), calls=%async_computation.23 | async-start | bytes 9830400 | tf_op jit(solution)/shard_map/all_gather | solution.py:213
  666.1 256.0 %all-gather.23.cloned.1.call-start = ((), (), s32[]{:S(2)}) async-start(), calls=%async_computation.18 | async-start | bytes 10321920 | tf_op jit(solution)/shard_map/all_gather | solution.py:74
  666.8 397.9 %all-gather.27.cloned.1.call-start = ((), (), s32[]{:S(2)}) async-start(), calls=%async_computation.22 | async-start | bytes 9830400 | tf_op jit(solution)/shard_map/all_gather | solution.py:271
  667.6 455.1 %all-gather.25.cloned.1.call-start = ((), (), s32[]{:S(2)}) async-start(), calls=%async_computation.19 | async-start | bytes 10321920 | tf_op jit(solution)/shard_map/all_gather | solution.py:75
  668.3 719.2 %reduce-scatter.17.cloned.1.call-start = ((), (), s32[]{:S(2)}) async-start(), calls=%async_computation.15 | async-start | bytes 19660800 | tf_op jit(solution)/shard_map/reduce_scatter | solution.py:191
  794.0 733.1 %reduce-scatter.23.cloned.1.call-start = ((), (), s32[]{:S(2)}) async-start(), calls=%async_computation.24 | async-start | bytes 9830400 | tf_op jit(solution)/shard_map/reduce_scatter | solution.py:283
  1195.8 331.3 %copy-start.42 = (f32[384]{0:T(512)S(1)}, f32[384]{0:T(512)}, u32[]{:S(2)}) copy-start(f32[384]{0:T(512)} %copy-done.41) | copy-start | bytes 4612
  1195.8 483.5 %all-gather.31.cloned.1.call-start = ((), (), s32[]{:S(2)}) async-start(), calls=%async_computation.25 | async-start | bytes 9830400 | tf_op jit(solution)/shard_map/all_gather | solution.py:300
  1537.6 704.4 %reduce-scatter.25.cloned.1.call-start = ((), (), s32[]{:S(2)}) async-start(), calls=%async_computation.26 | async-start | bytes 9830400 | tf_op jit(solution)/shard_map/reduce_scatter | solution.py:330
  2107.4 287.7 %all-gather.19.cloned.1.call-start = ((), (), s32[]{:S(2)}) async-start(), calls=%async_computation.16 | async-start | bytes 9830400 | tf_op jit(solution)/shard_map/all_gather | solution.py:213
  2253.4 218.5 %reduce-scatter.35.cloned.1.call-start = ((), (), s32[]{:S(2)}) async-start(), calls=%async_computation.31 | async-start | bytes 10321920 | tf_op jit(solution)/shard_map/reduce_scatter | solution.py:370
  2279.8 271.2 %reduce-scatter.33.cloned.1.call-start = ((), (), s32[]{:S(2)}) async-start(), calls=%async_computation.30 | async-start | bytes 10321920 | tf_op jit(solution)/shard_map/reduce_scatter | solution.py:367
  2300.6 328.9 %reduce-scatter.31.cloned.1.call-start = ((), (), s32[]{:S(2)}) async-start(), calls=%async_computation.29 | async-start | bytes 10321920 | tf_op jit(solution)/shard_map/reduce_scatter | solution.py:364
  2321.6 348.7 %reduce-scatter.39.cloned.1.call-start = ((), (), s32[]{:S(2)}) async-start(), calls=%async_computation.33 | async-start | bytes 1474560
  2327.9 383.3 %reduce-scatter.37.cloned.1.call-start = ((), (), s32[]{:S(2)}) async-start(), calls=%async_computation.32 | async-start | bytes 1474560
  2336.0 425.7 %reduce-scatter.29.cloned.1.call-start = ((), (), s32[]{:S(2)}) async-start(), calls=%async_computation.28 | async-start | bytes 3686400 | tf_op jit(solution)/shard_map/reduce_scatter | solution.py:358
  2346.3 466.8 %reduce-scatter.27.cloned.1.call-start = ((), (), s32[]{:S(2)}) async-start(), calls=%async_computation.27 | async-start | bytes 3686400 | tf_op jit(solution)/shard_map/reduce_scatter | solution.py:349
  2356.9 595.1 %reduce-scatter.19.cloned.1.call-start = ((), (), s32[]{:S(2)}) async-start(), calls=%async_computation.20 | async-start | bytes 9830400 | tf_op jit(solution)/shard_map/reduce_scatter | solution.py:257
  2553.7 398.2 %copy-start.4 = (bf16[384,2560]{1,0:T(8,128)(2,1)S(1)}, bf16[384,2560]{1,0:T(8,128)(2,1)}, u32[]{:S(2)}) copy-start(bf16[384,2560]{1,0:T(8,128)(2,1)} %param.21) | copy-start | bytes 5898244
  (60 other events, 3244.9 us)
Sparse Core Ops, SparseCore 0:
  42.7 140.9 all-gather.12
  185.6 31.0 all-gather.14
  218.6 32.8 all-gather.16
  397.9 262.6 reduce-scatter.20
  662.3 58.7 all-gather.20
  723.1 141.0 all-gather.28
  866.1 55.9 all-gather.22
  923.7 141.0 all-gather.26
  1066.7 55.9 all-gather.24
  1124.8 262.6 reduce-scatter.16
  1389.8 137.2 reduce-scatter.22
  1537.7 141.5 all-gather.30
  2107.5 134.4 reduce-scatter.24
  2253.6 141.5 all-gather.18
  2398.6 73.2 reduce-scatter.34
  2475.9 75.0 reduce-scatter.32
  2554.4 75.0 reduce-scatter.30
  2632.9 37.2 reduce-scatter.38
  2673.9 37.2 reduce-scatter.36
  2714.8 46.8 reduce-scatter.28
  2766.1 46.8 reduce-scatter.26
  2815.5 136.4 reduce-scatter.18
where the time goes:
time: 2970 us; the launch traced here: 2960 us
  waiting for transfers between devices  1760 us (59%)
  matrix products  712 us (24%)
  local copies, waits for them, and re-layouts  203 us (7%)
  other arithmetic  169 us (6%)
  blocking collectives  82.8 us (3%)
    reduce_scatter x2, waiting for transfers between devices, attention_sublayer(): lax.psum_scatter(jnp.dot(attended_low, output_weight, preferred_element_t...  454 us
    all_gather x1, waiting for transfers between devices, per_device(): grad_rows = lax.all_gather(grad_attention, 'tensor', axis=0, tiled=True)  142 us
    reduce_scatter x1, waiting for transfers between devices, per_device(): lax.psum_scatter((jnp.einsum('tf,df->td', grad_gate, ffn_again[1], prefer...  140 us
    reduce_scatter x1, waiting for transfers between devices, per_device(): lax.psum_scatter((summed + jnp.einsum('tc,dc->td', grad_values, attn_agai...  133 us
    all_gather x1, waiting for transfers between devices, per_device(): cot_rows = lax.all_gather(cotangent, 'tensor', axis=0, tiled=True)  122 us
    all_gather x1, waiting for transfers between devices, attention_sublayer(): normed = lax.all_gather(local_in, 'tensor', axis=0, tiled=True)  113 us
    all_gather x2, waiting for transfers between devices, feedforward_front(): normed = lax.all_gather(local_in, 'tensor', axis=0, tiled=True)  108 us
    dot_general x6, matrix products, block_scores(): jnp.einsum('qkge,ske->kgqs', query_block, key_heads, preferred_element_ty...  102 us
  transfers between devices with their start and end apart: 22, of which 20 were waited for; matrix products, arithmetic and copies ran while one was open for 21% of the time, Pallas kernels for 0%

commit v1 on v0

v1 whole, which is shorter than its diff:
```python
import functools
import math

import jax
import jax.numpy as jnp
from jax import lax
from jax.experimental import pallas as pl
from jax.experimental.pallas import tpu as pltpu
from jax.sharding import PartitionSpec as P

HEAD_DIM = 80
HALF = HEAD_DIM // 2
QUERY_BLOCK = 128
KEY_BLOCK = 256
MASKED = -1e30
VMEM_LIMIT = 48 * 1024 * 1024

epsilon = 1e-05
rope_base = 10000.0
AXES = ("dp", "tensor")


def contract(left, right, left_dim, right_dim, out_type=jnp.float32):
    product = lax.dot_general(
        left,
        right,
        (((left_dim,), (right_dim,)), ((), ())),
        preferred_element_type=jnp.float32,
    )
    return product.astype(out_type)


def inverse_root(vectors):
    return lax.rsqrt(jnp.mean(vectors * vectors, axis=-1, keepdims=True) + epsilon)


class Placement:
    def __init__(self, dp_count, tensor_count):
        self.dp_count = dp_count
        self.tensor_count = tensor_count
        self.chips = dp_count // 2
        self.low = tensor_count // 2
        dp_index = lax.axis_index("dp")
        tensor_index = lax.axis_index("tensor")
        self.p = dp_index // 2
        self.c = dp_index % 2
        self.th = tensor_index // self.low
        self.tl = tensor_index % self.low
        self.home = self.c == self.th

    def move(self, array, target):
        pairs = []
        for p in range(self.chips):
            for c in range(2):
                for th in range(2):
                    for tl in range(self.low):
                        goal = target(p, c, th, tl)
                        if goal is not None:
                            pairs.append((self.flat(p, c, th, tl), self.flat(*goal)))
        return lax.ppermute(array, AXES, pairs)

    def flat(self, p, c, th, tl):
        return (2 * p + c) * self.tensor_count + th * self.low + tl

    def to_core(self, array):
        return self.move(array, lambda p, c, th, tl: (p, 1 - c, th, tl))

    def to_chip(self, array, step):
        return self.move(array, lambda p, c, th, tl: (p ^ step, c, th, tl))

    def to_low(self, array, step):
        return self.move(array, lambda p, c, th, tl: (p, c, th, (tl + step) % self.low))

    def cross(self, array):
        return self.move(
            array, lambda p, c, th, tl: (p, 1 - c, 1 - th, tl) if c != th else None
        )

    def home_turn(self, array):
        return self.move(
            array, lambda p, c, th, tl: (p, c, 1 - th, tl) if c == th else (p, 1 - c, th, tl)
        )

    def away_turn(self, array):
        return self.move(
            array, lambda p, c, th, tl: (p, 1 - c, th, tl) if c == th else (p, c, 1 - th, tl)
        )

    def swap(self, array):
        return jnp.where(self.home, array, self.cross(array))

    def relative_features(self, array):
        width = array.shape[-1] // self.chips
        return jnp.concatenate(
            [
                lax.dynamic_slice_in_dim(array, (self.p ^ step) * width, width, array.ndim - 1)
                for step in range(self.chips)
            ],
            axis=-1,
        )

    def gather_rows(self, own):
        same = [own] + [self.to_low(own, self.low - step) for step in range(1, self.low)]
        blocks = []
        for block in same:
            blocks.append(block)
            blocks.append(self.to_core(block))
        return blocks

    def scatter_rows(self, blocks):
        total = None
        for step in list(range(1, self.low)) + [0]:
            mine, others = blocks[2 * step], blocks[2 * step + 1]
            pair = mine.astype(jnp.float32) + self.to_core(others).astype(jnp.float32)
            if step:
                pair = self.to_low(pair.astype(jnp.bfloat16), step).astype(jnp.float32)
            total = pair if total is None else total + pair
        return total

    def gather_weight(self, shard):
        turned = self.home_turn(shard)
        crossed = self.cross(shard)
        mine = jnp.where(self.home, shard, turned)
        other = jnp.where(self.home, turned, crossed)
        first = jnp.where(self.c == 0, mine, other)
        second = jnp.where(self.c == 0, other, mine)
        if self.chips == 4:
            units = [[first, second], None, None, None]
            unit = jnp.stack([first, second])
            by_x = self.to_chip(unit, 1)
            by_y = self.to_chip(unit, 2)
            diagonal_first = self.to_chip(by_y[0], 1)
            diagonal_second = self.to_chip(by_x[1], 2)
            units = [first, second, by_x[0], by_x[1], by_y[0], by_y[1], diagonal_first, diagonal_second]
        else:
            unit = jnp.stack([first, second])
            units = [first, second]
            for step in range(1, self.chips):
                arrived = self.to_chip(unit, step)
                units += [arrived[0], arrived[1]]
        return jnp.concatenate(units, axis=0)

    def scatter_weight(self, partial):
        rows = partial.shape[0] // self.dp_count
        units = partial.reshape(self.chips, 2, rows, partial.shape[1])

        def low(value):
            return value.astype(jnp.bfloat16)

        def wide(value):
            return value.astype(jnp.float32)

        if self.chips == 4:
            by_x = self.to_chip(units[3, 0], 1)
            by_y = self.to_chip(units[3, 1], 2)
            unit_x = jnp.stack([units[1, 0], low(wide(units[1, 1]) + wide(by_y))])
            unit_y = jnp.stack([low(wide(units[2, 0]) + wide(by_x)), units[2, 1]])
            total = (
                wide(units[0])
                + wide(self.to_chip(unit_x, 1))
                + wide(self.to_chip(unit_y, 2))
            )
        else:
            total = wide(units[0])
            for step in range(1, self.chips):
                total = total + wide(self.to_chip(units[step], step))
        mine = jnp.where(self.c == 0, total[0], total[1])
        other = jnp.where(self.c == 0, total[1], total[0])
        turned = self.away_turn(low(jnp.where(self.home, other, mine)))
        crossed = self.cross(low(other))
        return jnp.where(self.home, mine, wide(crossed)) + wide(turned)

    def sum_tensor(self, array):
        for bit in range(self.tensor_count.bit_length() - 1):
            step = 1 << bit

            def target(p, c, th, tl, step=step):
                moved = (th * self.low + tl) ^ step
                return (p, c, moved // self.low, moved % self.low)

            array = array + self.move(array, target)
        return array


def project_kernel(heads, tokens_ref, gain_ref, weight_ref, cosine_ref, sine_ref, normed_ref, out_ref):
    tokens = tokens_ref[...].astype(jnp.float32)
    root = lax.rsqrt(jnp.mean(tokens * tokens, axis=-1, keepdims=True) + epsilon)
    normed = (tokens * root * gain_ref[...]).astype(jnp.bfloat16)
    normed_ref[...] = normed
    rows = jnp.dot(normed, weight_ref[...], preferred_element_type=jnp.float32)
    cosine, sine = cosine_ref[...], sine_ref[...]
    pieces = []
    for head in range(heads):
        leading = rows[:, head * HEAD_DIM : head * HEAD_DIM + HALF]
        trailing = rows[:, head * HEAD_DIM + HALF : (head + 1) * HEAD_DIM]
        pieces.append(leading * cosine - trailing * sine)
        pieces.append(trailing * cosine + leading * sine)
    pieces.append(rows[:, heads * HEAD_DIM : out_ref.shape[1]])
    out_ref[...] = jnp.concatenate(pieces, axis=1).astype(jnp.bfloat16)


def project(tokens, gain, weight, cosine, sine, rotated_heads, out_columns):
    count, width = tokens.shape
    block = math.gcd(count, 256)
    return pl.pallas_call(
        functools.partial(project_kernel, rotated_heads),
        grid=(count // block,),
        in_specs=[
            pl.BlockSpec((block, width), lambda i: (i, 0)),
            pl.BlockSpec((1, width), lambda i: (0, 0)),
            pl.BlockSpec(weight.shape, lambda i: (0, 0)),
            pl.BlockSpec((block, HALF), lambda i: (i, 0)),
            pl.BlockSpec((block, HALF), lambda i: (i, 0)),
        ],
        out_specs=[
            pl.BlockSpec((block, width), lambda i: (i, 0)),
            pl.BlockSpec((block, out_columns), lambda i: (i, 0)),
        ],
        out_shape=[
            jax.ShapeDtypeStruct((count, width), jnp.bfloat16),
            jax.ShapeDtypeStruct((count, out_columns), jnp.bfloat16),
        ],
        compiler_params=pltpu.CompilerParams(vmem_limit_bytes=VMEM_LIMIT),
        cost_estimate=pl.CostEstimate(
            flops=2 * count * width * weight.shape[1],
            bytes_accessed=4 * count * width + 2 * weight.size,
            transcendentals=0,
        ),
        name="project",
    )(tokens, gain, weight, cosine, sine)


def block_bias(key_start, query_start, start_row, pad_column):
    shape = (pad_column.shape[0], start_row.shape[1])
    keys = key_start + lax.broadcasted_iota(jnp.int32, shape, 0)
    queries = query_start + lax.broadcasted_iota(jnp.int32, shape, 1)
    allowed = ((keys >= start_row) & (keys <= queries) & (pad_column == 1)) | (keys == queries)
    return jnp.where(allowed, 0.0, MASKED)


def stack_heads(rows, first, group):
    return jnp.concatenate(
        [rows[:, (first + g) * HEAD_DIM : (first + g + 1) * HEAD_DIM] for g in range(group)], axis=0
    )


def times(left, right, left_dim, right_dim):
    return lax.dot_general(
        left, right, (((left_dim,), (right_dim,)), ((), ())), preferred_element_type=jnp.float32
    )


def attend_kernel(
    kv_heads, group, first_ref, query_ref, all_ref, start_ref, pad_ref, out_ref, total_ref, key_heads, value_turned
):
    step = pl.program_id(0)
    heads = kv_heads * group
    query_rows = query_ref.shape[0]
    scale = 1.0 / math.sqrt(HEAD_DIM)

    @pl.when(step == 0)
    def _():
        for k in range(kv_heads):
            at = (heads + k) * HEAD_DIM
            key_heads[k] = all_ref[:, at : at + HEAD_DIM]
            at = (heads + kv_heads + k) * HEAD_DIM
            value_turned[k] = all_ref[:, at : at + HEAD_DIM].astype(jnp.float32).T.astype(jnp.bfloat16)

    query_start = step * query_rows
    last = (query_start + query_rows - 1) // KEY_BLOCK + 1
    pieces = []
    for k in range(kv_heads):
        queries = stack_heads(query_ref[:, : heads * HEAD_DIM], k * group, group)

        def body(block, carry, k=k, queries=queries):
            top, total, mixed = carry
            at = pl.multiple_of(block * KEY_BLOCK, KEY_BLOCK)
            bias = block_bias(at, query_start, start_ref[...], pad_ref[pl.ds(at, KEY_BLOCK), :])
            bias = jnp.concatenate([bias] * group, axis=1)
            scores = times(key_heads[k, pl.ds(at, KEY_BLOCK), :], queries, 1, 1) * scale + bias
            new_top = jnp.maximum(top, jnp.max(scores, axis=0, keepdims=True))
            weight = jnp.exp(scores - new_top)
            shrink = jnp.exp(top - new_top)
            total = total * shrink + jnp.sum(weight, axis=0, keepdims=True)
            mixed = mixed * shrink + times(
                value_turned[k, :, pl.ds(at, KEY_BLOCK)], weight.astype(jnp.bfloat16), 1, 0
            )
            return new_top, total, mixed

        columns = group * query_rows
        top, total, mixed = lax.fori_loop(
            first_ref[step],
            last,
            body,
            (
                jnp.full((1, columns), MASKED, jnp.float32),
                jnp.zeros((1, columns), jnp.float32),
                jnp.zeros((HEAD_DIM, columns), jnp.float32),
            ),
        )
        mixed = mixed / total
        log_total = top + jnp.log(total)
        for g in range(group):
            span = slice(g * query_rows, (g + 1) * query_rows)
            pieces.append(mixed[:, span].T)
            total_ref[k * group + g : k * group + g + 1, :] = log_total[:, span]
    out_ref[...] = jnp.concatenate(pieces, axis=1).astype(jnp.bfloat16)


def attend(first, heads_all, start_row, pad_column, kv_heads, group):
    count, columns = heads_all.shape
    heads = kv_heads * group
    block = math.gcd(count, QUERY_BLOCK)
    return pl.pallas_call(
        functools.partial(attend_kernel, kv_heads, group),
        grid_spec=pltpu.PrefetchScalarGridSpec(
            num_scalar_prefetch=1,
            grid=(count // block,),
            in_specs=[
                pl.BlockSpec((block, columns), lambda i, first: (i, 0)),
                pl.BlockSpec((count, columns), lambda i, first: (0, 0)),
                pl.BlockSpec((1, block), lambda i, first: (0, i)),
                pl.BlockSpec((count, 1), lambda i, first: (0, 0)),
            ],
            out_specs=[
                pl.BlockSpec((block, heads * HEAD_DIM), lambda i, first: (i, 0)),
                pl.BlockSpec((heads, block), lambda i, first: (0, i)),
            ],
            scratch_shapes=[
                pltpu.VMEM((kv_heads, count, HEAD_DIM), jnp.bfloat16),
                pltpu.VMEM((kv_heads, HEAD_DIM, count), jnp.bfloat16),
            ],
        ),
        out_shape=[
            jax.ShapeDtypeStruct((count, heads * HEAD_DIM), jnp.bfloat16),
            jax.ShapeDtypeStruct((heads, count), jnp.float32),
        ],
        compiler_params=pltpu.CompilerParams(vmem_limit_bytes=VMEM_LIMIT),
        cost_estimate=pl.CostEstimate(
            flops=60 * 10**9, bytes_accessed=count * columns * 4, transcendentals=0
        ),
        name="attend",
    )(first, heads_all, heads_all, start_row, pad_column)


def attend_back_kernel(
    kv_heads,
    group,
    first_ref,
    query_ref,
    all_ref,
    start_ref,
    pad_ref,
    total_ref,
    attended_ref,
    grad_ref,
    cosine_turned_ref,
    sine_turned_ref,
    cosine_ref,
    sine_ref,
    grad_query_ref,
    grad_rest_ref,
    key_heads,
    value_heads,
    key_turned,
    grad_keys,
    grad_values,
):
    step = pl.program_id(0)
    heads = kv_heads * group
    query_rows = query_ref.shape[0]
    scale = 1.0 / math.sqrt(HEAD_DIM)

    @pl.when(step == 0)
    def _():
        for k in range(kv_heads):
            at = (heads + k) * HEAD_DIM
            keys = all_ref[:, at : at + HEAD_DIM]
            key_heads[k] = keys
            key_turned[k] = keys.astype(jnp.float32).T.astype(jnp.bfloat16)
            at = (heads + kv_heads + k) * HEAD_DIM
            value_heads[k] = all_ref[:, at : at + HEAD_DIM]
        grad_keys[...] = jnp.zeros_like(grad_keys)
        grad_values[...] = jnp.zeros_like(grad_values)

    query_start = step * query_rows
    last = (query_start + query_rows - 1) // KEY_BLOCK + 1
    cosine = cosine_turned_ref[...]
    sine = sine_turned_ref[...]
    pieces = []
    for k in range(kv_heads):
        queries = stack_heads(query_ref[:, : heads * HEAD_DIM], k * group, group)
        grads = stack_heads(grad_ref[...], k * group, group)
        attended = stack_heads(attended_ref[...], k * group, group)
        inner = jnp.sum(
            (grads.astype(jnp.float32) * attended.astype(jnp.float32)).T, axis=0, keepdims=True
        )
        log_total = jnp.concatenate(
            [total_ref[k * group + g : k * group + g + 1, :] for g in range(group)], axis=1
        )

        def body(block, turned, k=k, queries=queries, grads=grads, inner=inner, log_total=log_total):
            at = pl.multiple_of(block * KEY_BLOCK, KEY_BLOCK)
            span = pl.ds(at, KEY_BLOCK)
            bias = block_bias(at, query_start, start_ref[...], pad_ref[span, :])
            bias = jnp.concatenate([bias] * group, axis=1)
            scores = times(key_heads[k, span, :], queries, 1, 1) * scale + bias
            weight = jnp.exp(scores - log_total)
            grad_weight = times(value_heads[k, span, :], grads, 1, 1)
            grad_scores = (weight * (grad_weight - inner)).astype(jnp.bfloat16)
            grad_values[k, span, :] += times(weight.astype(jnp.bfloat16), grads, 1, 0)
            grad_keys[k, span, :] += times(grad_scores, queries, 1, 0)
            return turned + times(key_turned[k, :, span], grad_scores, 1, 0)

        turned = lax.fori_loop(
            first_ref[step], last, body, jnp.zeros((HEAD_DIM, group * query_rows), jnp.float32)
        )
        turned = turned * scale
        for g in range(group):
            part = turned[:, g * query_rows : (g + 1) * query_rows]
            leading, trailing = part[:HALF], part[HALF:]
            back = jnp.concatenate(
                [leading * cosine + trailing * sine, trailing * cosine - leading * sine], axis=0
            )
            pieces.append(back.T)
    grad_query_ref[...] = jnp.concatenate(pieces, axis=1).astype(jnp.bfloat16)

    @pl.when(step == pl.num_programs(0) - 1)
    def _():
        rest = []
        for k in range(kv_heads):
            leading = grad_keys[k][:, :HALF] * scale
            trailing = grad_keys[k][:, HALF:] * scale
            rest.append(leading * cosine_ref[...] + trailing * sine_ref[...])
            rest.append(trailing * cosine_ref[...] - leading * sine_ref[...])
        for k in range(kv_heads):
            rest.append(grad_values[k])
        grad_rest_ref[...] = jnp.concatenate(rest, axis=1).astype(jnp.bfloat16)


def attend_back(
    first, heads_all, start_row, pad_column, log_totals, attended, grad_attended, cosine, sine, kv_heads, group
):
    count, columns = heads_all.shape
    heads = kv_heads * group
    block = math.gcd(count, QUERY_BLOCK)
    width = heads * HEAD_DIM
    rest = 2 * kv_heads * HEAD_DIM
    return pl.pallas_call(
        functools.partial(attend_back_kernel, kv_heads, group),
        grid_spec=pltpu.PrefetchScalarGridSpec(
            num_scalar_prefetch=1,
            grid=(count // block,),
            in_specs=[
                pl.BlockSpec((block, columns), lambda i, first: (i, 0)),
                pl.BlockSpec((count, columns), lambda i, first: (0, 0)),
                pl.BlockSpec((1, block), lambda i, first: (0, i)),
                pl.BlockSpec((count, 1), lambda i, first: (0, 0)),
                pl.BlockSpec((heads, block), lambda i, first: (0, i)),
                pl.BlockSpec((block, width), lambda i, first: (i, 0)),
                pl.BlockSpec((block, width), lambda i, first: (i, 0)),
                pl.BlockSpec((HALF, block), lambda i, first: (0, i)),
                pl.BlockSpec((HALF, block), lambda i, first: (0, i)),
                pl.BlockSpec((count, HALF), lambda i, first: (0, 0)),
                pl.BlockSpec((count, HALF), lambda i, first: (0, 0)),
            ],
            out_specs=[
                pl.BlockSpec((block, width), lambda i, first: (i, 0)),
                pl.BlockSpec((count, rest), lambda i, first: (0, 0)),
            ],
            scratch_shapes=[
                pltpu.VMEM((kv_heads, count, HEAD_DIM), jnp.bfloat16),
                pltpu.VMEM((kv_heads, count, HEAD_DIM), jnp.bfloat16),
                pltpu.VMEM((kv_heads, HEAD_DIM, count), jnp.bfloat16),
                pltpu.VMEM((kv_heads, count, HEAD_DIM), jnp.float32),
                pltpu.VMEM((kv_heads, count, HEAD_DIM), jnp.float32),
            ],
        ),
        out_shape=[
            jax.ShapeDtypeStruct((count, width), jnp.bfloat16),
            jax.ShapeDtypeStruct((count, rest), jnp.bfloat16),
        ],
        compiler_params=pltpu.CompilerParams(vmem_limit_bytes=VMEM_LIMIT),
        cost_estimate=pl.CostEstimate(
            flops=120 * 10**9, bytes_accessed=count * columns * 8, transcendentals=0
        ),
        name="attend_back",
    )(
        first,
        heads_all,
        heads_all,
        start_row,
        pad_column,
        log_totals,
        attended,
        grad_attended,
        cosine.T,
        sine.T,
        cosine,
        sine,
    )


def starts_of(positions, length_row):
    ends = jnp.cumsum(length_row)
    inside = positions[:, None] >= ends[None, :]
    return jnp.sum(jnp.where(inside, length_row[None, :], 0), axis=1)


def rotary_tables(positions):
    frequency = jnp.exp(
        jnp.arange(HALF, dtype=jnp.float32) * (-2.0 * math.log(rope_base) / HEAD_DIM)
    )
    angles = positions.astype(jnp.float32)[:, None] * frequency[None, :]
    return (jnp.cos(angles), jnp.sin(angles))


def per_device(
    dp_count,
    tensor_count,
    tokens,
    attention_gain,
    query_weight,
    key_weight,
    value_weight,
    output_weight,
    feedforward_gain,
    gate_weight,
    up_weight,
    down_weight,
    cotangent,
    lengths,
    storage_order,
    sequence_order,
    pad_mask,
):
    place = Placement(dp_count, tensor_count)
    count = storage_order.shape[0]
    rows = count // tensor_count
    kv_heads = key_weight.shape[1] // HEAD_DIM
    heads = query_weight.shape[1] // HEAD_DIM
    group = heads // kv_heads
    head_columns = (heads + 2 * kv_heads) * HEAD_DIM

    tokens_own = place.swap(place.relative_features(tokens))
    first_weight = place.gather_weight(
        jnp.concatenate(
            [query_weight, key_weight, value_weight, attention_gain[:, None], feedforward_gain[:, None]],
            axis=1,
        )
    )
    tokens_all = jnp.concatenate(place.gather_rows(tokens_own), axis=0)
    output_turned = place.gather_weight(output_weight.T)
    gate_full = place.gather_weight(gate_weight)
    up_full = place.gather_weight(up_weight)
    down_turned = place.gather_weight(down_weight.T)
    cot_own = place.swap(place.relative_features(cotangent))
    cot_all = jnp.concatenate(place.gather_rows(cot_own), axis=0)

    numbers = jnp.concatenate([storage_order, pad_mask, lengths[0]])
    numbers = jnp.where(place.home, numbers, place.to_core(numbers))
    pad_column = numbers[count : 2 * count][:, None]
    length_row = numbers[2 * count :]
    quarters = numbers[:count].reshape(2, place.low, rows)
    order = []
    for step in range(place.low):
        for other in range(2):
            quarter = lax.dynamic_index_in_dim(quarters, place.c ^ other, 0, keepdims=False)
            order.append(
                lax.dynamic_index_in_dim(quarter, (place.tl + step) % place.low, 0, keepdims=False)
            )
    order = jnp.concatenate(order)

    places = jnp.arange(count, dtype=jnp.int32)
    starts = starts_of(places, length_row)
    cosine, sine = rotary_tables(places - starts)
    cosine_stored, sine_stored = rotary_tables(order - starts_of(order, length_row))
    to_sequence = (places[:, None] == order[None, :]).astype(jnp.bfloat16)
    to_storage = (order[:, None] == places[None, :]).astype(jnp.bfloat16)
    first_blocks = starts[:: math.gcd(count, QUERY_BLOCK)] // KEY_BLOCK
    start_row = starts[None, :]

    attention_scale = first_weight[:, head_columns].astype(jnp.float32)[None, :]
    feedforward_scale = first_weight[:, head_columns + 1].astype(jnp.float32)[None, :]
    normed, heads_stored = project(
        tokens_all,
        attention_scale,
        first_weight,
        cosine_stored,
        sine_stored,
        heads + kv_heads,
        head_columns,
    )
    heads_all = contract(to_sequence, heads_stored, 1, 0, jnp.bfloat16)
    attended, log_totals = attend(first_blocks, heads_all, start_row, pad_column, kv_heads, group)
    attended_stored = contract(to_storage, attended, 1, 0, jnp.bfloat16)

    def split_rows(array):
        return [array[i * rows : (i + 1) * rows] for i in range(tensor_count)]

    attention_out = place.scatter_rows(
        split_rows(contract(attended_stored, output_turned, 1, 1, jnp.bfloat16))
    )
    residual = tokens_own.astype(jnp.float32) + attention_out

    root = inverse_root(residual)
    normed_ffn = jnp.concatenate(
        place.gather_rows((residual * root * feedforward_scale).astype(jnp.bfloat16)), axis=0
    )
    gate_values = contract(normed_ffn, gate_full, 1, 0)
    up_values = contract(normed_ffn, up_full, 1, 0)
    sigmoid = jax.nn.sigmoid(gate_values)
    hidden = (gate_values * sigmoid * up_values).astype(jnp.bfloat16)
    layer_own = residual + place.scatter_rows(
        split_rows(contract(hidden, down_turned, 1, 1, jnp.bfloat16))
    )

    def leave(own):
        arrived = place.cross(own.astype(jnp.bfloat16)).astype(jnp.float32)
        return place.relative_features(jnp.where(place.home, own, arrived))

    layer_output = leave(layer_own)

    grad_hidden = contract(cot_all, down_turned, 1, 0)
    grad_gate = (grad_hidden * up_values * sigmoid * (1.0 + gate_values * (1.0 - sigmoid))).astype(
        jnp.bfloat16
    )
    grad_up = (grad_hidden * gate_values * sigmoid).astype(jnp.bfloat16)
    grad_normed_ffn = place.scatter_rows(
        split_rows(
            (contract(grad_gate, gate_full, 1, 1) + contract(grad_up, up_full, 1, 1)).astype(jnp.bfloat16)
        )
    )
    down_grad = place.scatter_weight(contract(cot_all, hidden, 0, 0, jnp.bfloat16))
    gate_grad = place.scatter_weight(contract(normed_ffn, grad_gate, 0, 0, jnp.bfloat16))
    up_grad = place.scatter_weight(contract(normed_ffn, grad_up, 0, 0, jnp.bfloat16))
    unit_rows = residual * root
    scaled = grad_normed_ffn * feedforward_scale
    feedforward_part = jnp.sum(grad_normed_ffn * unit_rows, axis=0)
    grad_residual = cot_own.astype(jnp.float32) + root * (
        scaled - unit_rows * jnp.mean(scaled * unit_rows, axis=-1, keepdims=True)
    )

    grad_rows = jnp.concatenate(place.gather_rows(grad_residual.astype(jnp.bfloat16)), axis=0)
    grad_attended = contract(grad_rows, output_turned, 1, 0, jnp.bfloat16)
    grad_attended = contract(to_sequence, grad_attended, 1, 0, jnp.bfloat16)
    output_grad = place.scatter_weight(contract(grad_rows, attended_stored, 0, 0, jnp.bfloat16))
    grad_query, grad_rest = attend_back(
        first_blocks,
        heads_all,
        start_row,
        pad_column,
        log_totals,
        attended,
        grad_attended,
        cosine,
        sine,
        kv_heads,
        group,
    )
    grad_heads = contract(
        to_storage, jnp.concatenate([grad_query, grad_rest], axis=1), 1, 0, jnp.bfloat16
    )
    grad_normed_part = contract(grad_heads, first_weight[:, :head_columns], 1, 1)
    grad_normed = place.scatter_rows(split_rows(grad_normed_part.astype(jnp.bfloat16)))
    tokens_wide = tokens_all.astype(jnp.float32)
    attention_part = jnp.sum(grad_normed_part * (tokens_wide * inverse_root(tokens_wide)), axis=0)
    first_grad = place.scatter_weight(
        jnp.concatenate(
            [
                contract(normed, grad_heads, 0, 0, jnp.bfloat16),
                attention_part.astype(jnp.bfloat16)[:, None],
                feedforward_part.astype(jnp.bfloat16)[:, None],
            ],
            axis=1,
        )
    )
    gain_grads = place.sum_tensor(first_grad[:, head_columns:])
    own_wide = tokens_own.astype(jnp.float32)
    root_own = inverse_root(own_wide)
    unit_rows = own_wide * root_own
    scaled = grad_normed * attention_scale
    input_grad = grad_residual + root_own * (
        scaled - unit_rows * jnp.mean(scaled * unit_rows, axis=-1, keepdims=True)
    )
    query_columns = heads * HEAD_DIM
    key_columns = kv_heads * HEAD_DIM
    return (
        layer_output,
        leave(input_grad),
        gain_grads[:, 0],
        first_grad[:, :query_columns],
        first_grad[:, query_columns : query_columns + key_columns],
        first_grad[:, query_columns + key_columns : head_columns],
        output_grad.T,
        gain_grads[:, 1],
        gate_grad,
        up_grad,
        down_grad.T,
    )


def solution(mesh):
    placed = (
        P(("dp", "tensor"), None),
        P("dp"),
        P("dp", "tensor"),
        P("dp", "tensor"),
        P("dp", "tensor"),
        P("tensor", "dp"),
        P("dp"),
        P("dp", "tensor"),
        P("dp", "tensor"),
        P("tensor", "dp"),
        P(("dp", "tensor"), None),
        P("dp", None),
        P("dp"),
        P("dp"),
        P("dp"),
    )
    return jax.shard_map(
        functools.partial(per_device, mesh.shape["dp"], mesh.shape["tensor"]),
        mesh=mesh,
        in_specs=placed,
        out_specs=(
            P(("dp", "tensor"), None),
            P(("dp", "tensor"), None),
            P("dp"),
            P("dp", "tensor"),
            P("dp", "tensor"),
            P("dp", "tensor"),
            P("tensor", "dp"),
            P("dp"),
            P("dp", "tensor"),
            P("dp", "tensor"),
            P("tensor", "dp"),
        ),
        check_vma=False,
    )
```

time: 2970 us -> 1590 us (0.54)
  waiting for transfers between devices: 1760 us -> 479 us
  matrix products: 712 us -> 282 us
  starting transfers between devices: 0.89 us -> 385 us
  Pallas kernels: 0 us -> 103 us
  blocking collectives: 82.8 us -> 0 us
  local copies, waits for them, and re-layouts: 203 us -> 165 us
    reduce_scatter x10 -> x0, waiting for transfers between devices: 1090 us -> none  [the longest x2 454 us: attention_sublayer(): lax.psum_scatter(jnp.dot(attended_low, output_weight, preferred_element_t...]
    all_gather x10 -> x0, waiting for transfers between devices: 592 us -> none  [the longest x1 142 us: per_device(): grad_rows = lax.all_gather(grad_attention, 'tensor', axis=0, tiled=True)]
    ppermute x0 -> x91, waiting for transfers between devices: none -> 479 us  [move(): return lax.ppermute(array, AXES, pairs)]
    ppermute x0 -> x91, starting transfers between devices: none -> 385 us  [move(): return lax.ppermute(array, AXES, pairs)]
    dot_general x48 -> x17, matrix products: 666 us -> 282 us  [contract(): lax.dot_general(left, right, (((left_dim,), (right_dim,)), ((), ())), pre...]
    pallas_call x0 -> x3, Pallas kernels: none -> 103 us  [the longest x1 46.8 us: attend_back(): pl.pallas_call(functools.partial(attend_back_kernel, kv_heads, group), gr...]
    dynamic_update_slice x6 -> x0, local copies, waits for them, and re-layouts: 82.1 us -> none  [attention_forward(): attended, log_totals = lax.map(one_block, block_starts)]
    unnamed x24 -> x0, waiting for transfers between devices: 81.4 us -> none
  transfers between devices with their start and end apart: 22 -> 91, of which waited for: 20 -> 29; matrix products, arithmetic and copies ran while one was open for 21% -> 22% of each run, Pallas kernels for 0% -> 7%
where the time goes in v1:
time: 1590 us; the launch traced here: 1570 us
  waiting for transfers between devices  479 us (30%)
  starting transfers between devices  385 us (24%)
  matrix products  282 us (18%)
  local copies, waits for them, and re-layouts  165 us (10%)
  other arithmetic  158 us (10%)
  Pallas kernels  103 us (6%)
    ppermute x91, waiting for transfers between devices, move(): return lax.ppermute(array, AXES, pairs)  479 us
    ppermute x91, starting transfers between devices, move(): return lax.ppermute(array, AXES, pairs)  385 us
    dot_general x17, matrix products, contract(): lax.dot_general(left, right, (((left_dim,), (right_dim,)), ((), ())), pre...  282 us
    unnamed x219, local copies, waits for them, and re-layouts  49.2 us
    pallas_call x1, Pallas kernels, attend_back(): pl.pallas_call(functools.partial(attend_back_kernel, kv_heads, group), gr...  46.8 us
    convert_element_type x4, local copies, waits for them, and re-layouts, contract(): return product.astype(out_type)  46.2 us
    pallas_call x1, Pallas kernels, attend(): pl.pallas_call(functools.partial(attend_kernel, kv_heads, group), grid_sp...  34.3 us
  transfers between devices with their start and end apart: 91, of which 29 were waited for; matrix products, arithmetic and copies ran while one was open for 22% of the time, Pallas kernels for 7%

profile of v1, /device:TPU:0, one launch (start us, length us, event | category | flops | bytes accessed | tf_op | source)
XLA Modules:
  0.0 1574.7 jit_solution(14836753582175457110)
XLA Ops:
  33.9 38.4 %collective-permute-start.23 = (bf16[320,1728]{1,0:T(8,128)(2,1)}, bf16[320,1728]{1,0:T(8,128)(2,1)S(1)}, u32[]{:S(2)}, u32[]{:S(2)}) collective-permute-start(bf16[320,1728]{1,0:T(8,128)(2,1)} %param.22), channel_id=1, source_target_pairs={{0,2},{1,3},{2,6},{3,7},{4,0},{5,1},{6,4},{7,5},{8,10},{9,11},{10,... | collective-permute-start | bytes 3317768 | tf_op jit(solution)/shard_map/ppermute | solution.py:60
  157.3 55.6 %collective-permute-done.9 = bf16[320,962]{1,0:T(8,128)(2,1)S(1)} collective-permute-done((bf16[320,962]{1,0:T(8,128)(2,1)S(1)}, bf16[320,962]{1,0:T(8,128)(2,1)S(1)}, u32[]{:S(2)}, u32[]{:S(2)}) %collective-permute-start.9) | collective-permute-done | bytes 615712 | tf_op jit(solution)/shard_map/ppermute | solution.py:60
  219.6 170.0 %collective-permute-start.3 = (bf16[384,2560]{1,0:T(8,128)(2,1)S(1)}, bf16[384,2560]{1,0:T(8,128)(2,1)S(1)}, u32[]{:S(2)}, u32[]{:S(2)}) collective-permute-start(bf16[384,2560]{1,0:T(8,128)(2,1)S(1)} %get-tuple-element.84), channel_id=1, source_target_pairs={{0,1},{1,0},{2,3},{3,2},{4,5},{5,4},{6,7},{7,6},{8,9},{9,8},{10,11... | collective-permute-start | bytes 5898248 | tf_op jit(solution)/shard_map/ppermute | solution.py:60
  394.1 36.4 %collective-permute-done.3 = bf16[384,2560]{1,0:T(8,128)(2,1)S(1)} collective-permute-done((bf16[384,2560]{1,0:T(8,128)(2,1)S(1)}, bf16[384,2560]{1,0:T(8,128)(2,1)S(1)}, u32[]{:S(2)}, u32[]{:S(2)}) %collective-permute-start.3) | collective-permute-done | bytes 1966112 | tf_op jit(solution)/shard_map/ppermute | solution.py:60
  441.8 21.5 %project.1 = (bf16[1536,2560]{1,0:T(8,128)(2,1)}, bf16[1536,960]{1,0:T(8,128)(2,1)S(1)}) custom-call(bf16[1536,2560]{1,0:T(8,128)(2,1)} %get-tuple-element.80.tokens_ref, f32[1,2560]{1,0:T(1,128)S(1)} %reshape.283.gain_ref, bf16[2560,962]{1,0:T(8,128)(2,1)} %constant_dynamic-update-slice_fusion.weight_ref, f32[1536,40]{1,0:T(8,128)S(1)} %get-tuple-element.186.cosine_ref, ...), custom_call_target="tpu_custom_call" | custom-call | flops 7565475840 | bytes 20654080 | tf_op jit(solution)/shard_map/project/pallas_call | solution.py:205
  468.6 34.3 %attend.1 = (bf16[1536,640]{1,0:T(8,128)(2,1)S(1)}, f32[8,1536]{1,0:T(8,128)S(1)}) custom-call(s32[12]{0:T(128)S(1)} %and_select_fusion.first_ref, bf16[1536,960]{1,0:T(8,128)(2,1)S(1)} %fusion.20.query_ref.all_ref, bf16[1536,960]{1,0:T(8,128)(2,1)S(1)} %fusion.20.query_ref.all_ref, s32[1,1536]{1,0:T(1,128)S(1)} %broadcast_in_dim.28.start_ref, ...), custom_call_target="tpu_custom_call" | custom-call | flops 60000002048 | bytes 5898240 | tf_op jit(solution)/shard_map/attend/pallas_call | solution.py:314
  544.3 23.3 %collective-permute-done.18 = bf16[384,2560]{1,0:T(8,128)(2,1)S(1)} collective-permute-done((bf16[384,2560]{1,0:T(8,128)(2,1)S(1)}, bf16[384,2560]{1,0:T(8,128)(2,1)S(1)}, u32[]{:S(2)}, u32[]{:S(2)}) %collective-permute-start.18) | collective-permute-done | bytes 1966112 | tf_op jit(solution)/shard_map/ppermute | solution.py:60
  631.6 22.9 %fusion.41 = f32[1536,1728]{0,1:T(8,128)} fusion(bf16[2560,1728]{1,0:T(8,128)(2,1)} %constant_dynamic-update-slice_fusion.16, bf16[384,2560]{1,0:T(8,128)(2,1)} %collective-permute-done.48, bf16[384,2560]{1,0:T(8,128)(2,1)} %collective-permute-done.47, bf16[384,2560]{1,0:T(8,128)(2,1)} %copy-done.74, bf16[384,2560]{1,0:T(8,128)(2,1)} %copy-done.20), kind=kOutput, calls=%fused_computation.123 | convolution fusion | flops 13621002240 | bytes 27328512 | tf_op jit(solution)/shard_map/dot_general | solution.py:24
  654.4 22.7 %fusion.104 = f32[1536,1728]{0,1:T(8,128)} fusion(bf16[2560,1728]{1,0:T(8,128)(2,1)} %constant_dynamic-update-slice_fusion.12, bf16[384,2560]{1,0:T(8,128)(2,1)} %collective-permute-done.22, bf16[384,2560]{1,0:T(8,128)(2,1)} %collective-permute-done.21, bf16[384,2560]{1,0:T(8,128)(2,1)} %collective-permute-done.20, ...), kind=kOutput, calls=%fused_computation.348 | convolution fusion | flops 13621002240 | bytes 27328512 | tf_op jit(solution)/shard_map/dot_general | solution.py:24
  677.1 37.0 %multiply_convert_fusion.1 = (bf16[1536,1728]{0,1:T(8,128)(2,1)}, bf16[1536,1728]{0,1:T(8,128)(2,1)}, bf16[1536,1728]{0,1:T(8,128)(2,1)}) fusion(f32[1536,1728]{0,1:T(8,128)} %fusion.41, f32[1536,1728]{0,1:T(8,128)} %fusion.104, bf16[2560,1728]{1,0:T(8,128)(2,1)} %constant_dynamic-update-slice_fusion.8, bf16[384,2560]{1,0:T(8,128)(2,1)} %collective-permute-done.22, ...), kind=kOutput, calls=%fused_computation.12 | convolution fusion | flops 13663469568 | bytes 53870592 | tf_op jit(solution)/shard_map/dot_general | solution.py:24
  714.1 20.1 %convolution_convert_fusion.3 = bf16[2560,1728]{0,1:T(8,128)(2,1)} fusion(bf16[1536,1728]{0,1:T(8,128)(2,1)} %get-tuple-element.104, bf16[384,2560]{1,0:T(8,128)(2,1)} %collective-permute-done.22, bf16[384,2560]{1,0:T(8,128)(2,1)} %collective-permute-done.21, bf16[384,2560]{1,0:T(8,128)(2,1)} %collective-permute-done.20, ...), kind=kOutput, calls=%fused_computation.9 | convolution fusion | flops 13625425920 | bytes 22020096 | tf_op jit(solution)/shard_map/dot_general | solution.py:24
  751.1 21.1 %fusion.115 = f32[1536,2560]{1,0:T(8,128)} fusion(bf16[1536,1728]{0,1:T(8,128)(2,1)S(1)} %copy-done.78, bf16[2560,1728]{1,0:T(8,128)(2,1)} %constant_dynamic-update-slice_fusion.12), kind=kOutput, calls=%fused_computation.358 | convolution fusion | flops 13589544960 | bytes 29884416 | tf_op jit(solution)/shard_map/dot_general | solution.py:24
  772.2 20.2 %convolution_convert_fusion.2 = bf16[2560,1728]{0,1:T(8,128)(2,1)} fusion(bf16[1536,1728]{0,1:T(8,128)(2,1)} %get-tuple-element.106, bf16[384,2560]{1,0:T(8,128)(2,1)} %collective-permute-done.22, bf16[384,2560]{1,0:T(8,128)(2,1)} %collective-permute-done.21, bf16[384,2560]{1,0:T(8,128)(2,1)} %collective-permute-done.20, ...), kind=kOutput, calls=%fused_computation.8 | convolution fusion | flops 13625425920 | bytes 22020096 | tf_op jit(solution)/shard_map/dot_general | solution.py:24
  809.1 20.8 %convolution_convert_fusion.4 = bf16[1536,2560]{1,0:T(8,128)(2,1)} fusion(bf16[1536,1728]{0,1:T(8,128)(2,1)} %get-tuple-element.105, bf16[2560,1728]{1,0:T(8,128)(2,1)} %constant_dynamic-update-slice_fusion.16), kind=kOutput, calls=%fused_computation.10 | convolution fusion | flops 13593477120 | bytes 22020096 | tf_op jit(solution)/shard_map/dot_general | solution.py:24
  829.8 19.9 %convolution_convert_fusion.1 = bf16[2560,1728]{0,1:T(8,128)(2,1)} fusion(bf16[1536,1728]{0,1:T(8,128)(2,1)} %get-tuple-element.105, bf16[384,2560]{1,0:T(8,128)(2,1)} %collective-permute-done.48, bf16[384,2560]{1,0:T(8,128)(2,1)} %collective-permute-done.47, bf16[384,2560]{1,0:T(8,128)(2,1)S(1)} %copy-done.75, bf16[384,2560]{1,0:T(8,128)(2,1)S(1)} %copy-done.21), kind=kOutput, calls=%fused_computation.7 | convolution fusion | flops 13625425920 | bytes 22020096 | tf_op jit(solution)/shard_map/dot_general | solution.py:24
  866.7 23.1 %add_convert_fusion = bf16[1536,2560]{1,0:T(8,128)(2,1)} fusion(f32[1536,2560]{1,0:T(8,128)} %fusion.115, bf16[1536,1728]{0,1:T(8,128)(2,1)} %get-tuple-element.104, bf16[2560,1728]{1,0:T(8,128)(2,1)} %constant_dynamic-update-slice_fusion.8), kind=kOutput, calls=%fused_computation.5 | convolution fusion | flops 13597409280 | bytes 37748736 | tf_op jit(solution)/shard_map/dot_general | solution.py:24
  992.9 34.3 %collective-permute-done.76 = bf16[2,320,1728]{2,1,0:T(8,128)(2,1)S(1)} collective-permute-done((bf16[2,320,1728]{2,1,0:T(8,128)(2,1)S(1)}, bf16[2,320,1728]{2,1,0:T(8,128)(2,1)S(1)}, u32[]{:S(2)}, u32[]{:S(2)}) %collective-permute-start.76) | collective-permute-done | bytes 2211872 | tf_op jit(solution)/shard_map/ppermute | solution.py:60
  1045.4 31.5 %collective-permute-done.42 = bf16[384,2560]{1,0:T(8,128)(2,1)} collective-permute-done((bf16[384,2560]{1,0:T(8,128)(2,1)}, bf16[384,2560]{1,0:T(8,128)(2,1)}, u32[]{:S(2)}, u32[]{:S(2)}) %collective-permute-start.42) | collective-permute-done | bytes 1966112 | tf_op jit(solution)/shard_map/ppermute | solution.py:60
  1098.3 27.4 %collective-permute-done.88 = bf16[2,320,1728]{2,1,0:T(8,128)(2,1)} collective-permute-done((bf16[2,320,1728]{2,1,0:T(8,128)(2,1)}, bf16[2,320,1728]{2,1,0:T(8,128)(2,1)}, u32[]{:S(2)}, u32[]{:S(2)}) %collective-permute-start.88) | collective-permute-done | bytes 2211872 | tf_op jit(solution)/shard_map/ppermute | solution.py:60
  1142.9 25.5 %collective-permute-done.53 = bf16[384,2560]{1,0:T(8,128)(2,1)} collective-permute-done((bf16[384,2560]{1,0:T(8,128)(2,1)}, bf16[384,2560]{1,0:T(8,128)(2,1)}, u32[]{:S(2)}, u32[]{:S(2)}) %collective-permute-start.53) | collective-permute-done | bytes 1966112 | tf_op jit(solution)/shard_map/ppermute | solution.py:60
  1201.3 46.8 %attend_back.1 = (bf16[1536,640]{1,0:T(8,128)(2,1)S(1)}, bf16[1536,320]{1,0:T(8,128)(2,1)S(1)}) custom-call(s32[12]{0:T(128)S(1)} %copy-done.5, bf16[1536,960]{1,0:T(8,128)(2,1)} %copy-done.7, bf16[1536,960]{1,0:T(8,128)(2,1)} %copy-done.7, s32[1,1536]{1,0:T(1,128)S(1)} %copy-done.3, s32[1536,1]{1,0:T(8,128)S(1)} %copy-done.1, ...), custom_call_target="tpu_custom_call" | custom-call | flops 120000004096 | bytes 11796480 | tf_op jit(solution)/shard_map/attend_back/pallas_call | solution.py:449
  1273.3 42.0 %collective-permute-start.55 = (bf16[384,2560]{1,0:T(8,128)(2,1)}, bf16[384,2560]{1,0:T(8,128)(2,1)}, u32[]{:S(2)}, u32[]{:S(2)}) collective-permute-start(bf16[384,2560]{1,0:T(8,128)(2,1)} %get-tuple-element.127), channel_id=1, source_target_pairs={{0,4},{1,5},{2,6},{3,7},{4,0},{5,1},{6,2},{7,3},{8,12},{9,13},{10,... | collective-permute-start | bytes 5898248 | tf_op jit(solution)/shard_map/ppermute | solution.py:60
  1408.1 21.9 %collective-permute-start.72 = (bf16[320,640]{1,0:T(8,128)(2,1)S(1)}, bf16[320,640]{1,0:T(8,128)(2,1)S(1)}, u32[]{:S(2)}, u32[]{:S(2)}) collective-permute-start(bf16[320,640]{1,0:T(8,128)(2,1)S(1)} %fusion.61), channel_id=1, source_target_pairs={{0,4},{1,5},{2,0},{3,1},{4,6},{5,7},{6,2},{7,3},{8,12},{9,13},{10,... | collective-permute-start | bytes 1228808 | tf_op jit(solution)/shard_map/ppermute | solution.py:60
  1475.5 67.0 %collective-permute-done.64 = bf16[320,962]{1,0:T(8,128)(2,1)S(1)} collective-permute-done((bf16[320,962]{1,0:T(8,128)(2,1)S(1)}, bf16[320,962]{1,0:T(8,128)(2,1)S(1)}, u32[]{:S(2)}, u32[]{:S(2)}) %collective-permute-start.64) | collective-permute-done | bytes 615712 | tf_op jit(solution)/shard_map/ppermute | solution.py:60
  (555 shorter events, 688.3 us)
Async XLA Ops:
  6.2 69.2 %collective-permute-start.5 = (bf16[320,962]{1,0:T(8,128)(2,1)}, bf16[320,962]{1,0:T(8,128)(2,1)}, u32[]{:S(2)}, u32[]{:S(2)}) collective-permute-start(bf16[320,962]{1,0:T(8,128)(2,1)} %concatenate.67), channel_id=1, source_target_pairs={{0,2},{1,3},{2,6},{3,7},{4,0},{5,1},{6,4},{7,5},{8,10},{9,11},{10,... | collective-permute-start | bytes 1847048 | tf_op jit(solution)/shard_map/ppermute | solution.py:60
  144.4 75.2 %collective-permute-start.37 = (bf16[2,320,1728]{2,1,0:T(8,128)(2,1)S(1)}, bf16[2,320,1728]{2,1,0:T(8,128)(2,1)S(1)}, u32[]{:S(2)}, u32[]{:S(2)}) collective-permute-start(bf16[2,320,1728]{2,1,0:T(8,128)(2,1)S(1)} %pad_maximum_fusion.8), channel_id=1, source_target_pairs={{0,8},{1,9},{2,10},{3,11},{4,12},{5,13},{6,14},{7,15},{8,0},{9,1},... | collective-permute-start | bytes 6635528 | tf_op jit(solution)/shard_map/ppermute | solution.py:60
  146.2 245.7 %collective-permute-start.38 = (bf16[2,320,1728]{2,1,0:T(8,128)(2,1)S(1)}, bf16[2,320,1728]{2,1,0:T(8,128)(2,1)S(1)}, u32[]{:S(2)}, u32[]{:S(2)}) collective-permute-start(bf16[2,320,1728]{2,1,0:T(8,128)(2,1)S(1)} %pad_maximum_fusion.8), channel_id=1, source_target_pairs={{0,16},{1,17},{2,18},{3,19},{4,20},{5,21},{6,22},{7,23},{8,24},{9,... | collective-permute-start | bytes 6635528 | tf_op jit(solution)/shard_map/ppermute | solution.py:60
  149.5 282.1 %collective-permute-start.31 = (bf16[2,320,1728]{2,1,0:T(8,128)(2,1)}, bf16[2,320,1728]{2,1,0:T(8,128)(2,1)S(1)}, u32[]{:S(2)}, u32[]{:S(2)}) collective-permute-start(bf16[2,320,1728]{2,1,0:T(8,128)(2,1)} %pad_maximum_fusion.7), channel_id=1, source_target_pairs={{0,8},{1,9},{2,10},{3,11},{4,12},{5,13},{6,14},{7,15},{8,0},{9,1},... | collective-permute-start | bytes 6635528 | tf_op jit(solution)/shard_map/ppermute | solution.py:60
  212.9 301.4 %collective-permute-start.32 = (bf16[2,320,1728]{2,1,0:T(8,128)(2,1)}, bf16[2,320,1728]{2,1,0:T(8,128)(2,1)}, u32[]{:S(2)}, u32[]{:S(2)}) collective-permute-start(bf16[2,320,1728]{2,1,0:T(8,128)(2,1)} %pad_maximum_fusion.7), channel_id=1, source_target_pairs={{0,16},{1,17},{2,18},{3,19},{4,20},{5,21},{6,22},{7,23},{8,24},{9,... | collective-permute-start | bytes 6635528 | tf_op jit(solution)/shard_map/ppermute | solution.py:60
  215.3 305.2 %collective-permute-start.25 = (bf16[2,320,1728]{2,1,0:T(8,128)(2,1)}, bf16[2,320,1728]{2,1,0:T(8,128)(2,1)}, u32[]{:S(2)}, u32[]{:S(2)}) collective-permute-start(bf16[2,320,1728]{2,1,0:T(8,128)(2,1)} %pad_maximum_fusion.6), channel_id=1, source_target_pairs={{0,8},{1,9},{2,10},{3,11},{4,12},{5,13},{6,14},{7,15},{8,0},{9,1},... | collective-permute-start | bytes 6635528 | tf_op jit(solution)/shard_map/ppermute | solution.py:60
  219.6 210.9 %collective-permute-start.3 = (bf16[384,2560]{1,0:T(8,128)(2,1)S(1)}, bf16[384,2560]{1,0:T(8,128)(2,1)S(1)}, u32[]{:S(2)}, u32[]{:S(2)}) collective-permute-start(bf16[384,2560]{1,0:T(8,128)(2,1)S(1)} %get-tuple-element.84), channel_id=1, source_target_pairs={{0,1},{1,0},{2,3},{3,2},{4,5},{5,4},{6,7},{7,6},{8,9},{9,8},{10,11... | collective-permute-start | bytes 5898248 | tf_op jit(solution)/shard_map/ppermute | solution.py:60
  431.6 96.3 %collective-permute-start.26 = (bf16[2,320,1728]{2,1,0:T(8,128)(2,1)}, bf16[2,320,1728]{2,1,0:T(8,128)(2,1)}, u32[]{:S(2)}, u32[]{:S(2)}) collective-permute-start(bf16[2,320,1728]{2,1,0:T(8,128)(2,1)} %pad_maximum_fusion.6), channel_id=1, source_target_pairs={{0,16},{1,17},{2,18},{3,19},{4,20},{5,21},{6,22},{7,23},{8,24},{9,... | collective-permute-start | bytes 6635528 | tf_op jit(solution)/shard_map/ppermute | solution.py:60
  435.4 139.0 %collective-permute-start.47 = (bf16[384,2560]{1,0:T(8,128)(2,1)S(1)}, bf16[384,2560]{1,0:T(8,128)(2,1)}, u32[]{:S(2)}, u32[]{:S(2)}) collective-permute-start(bf16[384,2560]{1,0:T(8,128)(2,1)S(1)} %broadcast_select_fusion), channel_id=1, source_target_pairs={{0,1},{1,0},{2,3},{3,2},{4,5},{5,4},{6,7},{7,6},{8,9},{9,8},{10,11... | collective-permute-start | bytes 5898248 | tf_op jit(solution)/shard_map/ppermute | solution.py:60
  437.1 137.3 %collective-permute-start.39 = (bf16[320,1728]{1,0:T(8,128)(2,1)}, bf16[320,1728]{1,0:T(8,128)(2,1)}, u32[]{:S(2)}, u32[]{:S(2)}) collective-permute-start(bf16[320,1728]{1,0:T(8,128)(2,1)} %slice_bitcast_fusion.19), channel_id=1, source_target_pairs={{0,8},{1,9},{2,10},{3,11},{4,12},{5,13},{6,14},{7,15},{8,0},{9,1},... | collective-permute-start | bytes 3317768 | tf_op jit(solution)/shard_map/ppermute | solution.py:60
  894.1 143.6 %collective-permute-start.51 = (bf16[384,2560]{1,0:T(8,128)(2,1)}, bf16[384,2560]{1,0:T(8,128)(2,1)}, u32[]{:S(2)}, u32[]{:S(2)}) collective-permute-start(bf16[384,2560]{1,0:T(8,128)(2,1)} %get-tuple-element.130), channel_id=1, source_target_pairs={{0,4},{1,5},{2,6},{3,7},{4,0},{5,1},{6,2},{7,3},{8,12},{9,13},{10,... | collective-permute-start | bytes 5898248 | tf_op jit(solution)/shard_map/ppermute | solution.py:60
  1041.5 84.2 %collective-permute-start.88 = (bf16[2,320,1728]{2,1,0:T(8,128)(2,1)}, bf16[2,320,1728]{2,1,0:T(8,128)(2,1)}, u32[]{:S(2)}, u32[]{:S(2)}) collective-permute-start(bf16[2,320,1728]{2,1,0:T(8,128)(2,1)} %pad_maximum_fusion.14), channel_id=1, source_target_pairs={{0,16},{1,17},{2,18},{3,19},{4,20},{5,21},{6,22},{7,23},{8,24},{9,... | collective-permute-start | bytes 6635528 | tf_op jit(solution)/shard_map/ppermute | solution.py:60
  1045.3 93.1 %collective-permute-start.86 = (bf16[2,320,1728]{2,1,0:T(8,128)(2,1)}, bf16[2,320,1728]{2,1,0:T(8,128)(2,1)}, u32[]{:S(2)}, u32[]{:S(2)}) collective-permute-start(bf16[2,320,1728]{2,1,0:T(8,128)(2,1)} %pad_maximum_fusion.13), channel_id=1, source_target_pairs={{0,8},{1,9},{2,10},{3,11},{4,12},{5,13},{6,14},{7,15},{8,0},{9,1},... | collective-permute-start | bytes 6635528 | tf_op jit(solution)/shard_map/ppermute | solution.py:60
  1076.9 92.6 %collective-permute-start.78 = (bf16[320,1728]{1,0:T(8,128)(2,1)}, bf16[320,1728]{1,0:T(8,128)(2,1)S(1)}, u32[]{:S(2)}, u32[]{:S(2)}) collective-permute-start(bf16[320,1728]{1,0:T(8,128)(2,1)} %fusion.38), channel_id=1, source_target_pairs={{0,4},{1,5},{2,0},{3,1},{4,6},{5,7},{6,2},{7,3},{8,12},{9,13},{10,... | collective-permute-start | bytes 3317768 | tf_op jit(solution)/shard_map/ppermute | solution.py:60
  1084.1 91.1 %collective-permute-start.77 = (bf16[320,1728]{1,0:T(8,128)(2,1)}, bf16[320,1728]{1,0:T(8,128)(2,1)}, u32[]{:S(2)}, u32[]{:S(2)}) collective-permute-start(bf16[320,1728]{1,0:T(8,128)(2,1)} %bitcast_convert_fusion.2), channel_id=1, source_target_pairs={{2,4},{3,5},{4,2},{5,3},{10,12},{11,13},{12,10},{13,11},{18,20},{1... | collective-permute-start | bytes 3317768 | tf_op jit(solution)/shard_map/ppermute | solution.py:60
  1092.3 76.1 %collective-permute-start.53 = (bf16[384,2560]{1,0:T(8,128)(2,1)}, bf16[384,2560]{1,0:T(8,128)(2,1)}, u32[]{:S(2)}, u32[]{:S(2)}) collective-permute-start(bf16[384,2560]{1,0:T(8,128)(2,1)} %get-tuple-element.85), channel_id=1, source_target_pairs={{0,1},{1,0},{2,3},{3,2},{4,5},{5,4},{6,7},{7,6},{8,9},{9,8},{10,11... | collective-permute-start | bytes 5898248 | tf_op jit(solution)/shard_map/ppermute | solution.py:60
  1175.2 183.5 %collective-permute-start.90 = (bf16[320,1728]{1,0:T(8,128)(2,1)}, bf16[320,1728]{1,0:T(8,128)(2,1)}, u32[]{:S(2)}, u32[]{:S(2)}) collective-permute-start(bf16[320,1728]{1,0:T(8,128)(2,1)} %fusion.33), channel_id=1, source_target_pairs={{0,4},{1,5},{2,0},{3,1},{4,6},{5,7},{6,2},{7,3},{8,12},{9,13},{10,... | collective-permute-start | bytes 3317768 | tf_op jit(solution)/shard_map/ppermute | solution.py:60
  1180.4 178.4 %collective-permute-start.89 = (bf16[320,1728]{1,0:T(8,128)(2,1)}, bf16[320,1728]{1,0:T(8,128)(2,1)}, u32[]{:S(2)}, u32[]{:S(2)}) collective-permute-start(bf16[320,1728]{1,0:T(8,128)(2,1)} %bitcast_convert_fusion), channel_id=1, source_target_pairs={{2,4},{3,5},{4,2},{5,3},{10,12},{11,13},{12,10},{13,11},{18,20},{1... | collective-permute-start | bytes 3317768 | tf_op jit(solution)/shard_map/ppermute | solution.py:60
  1273.3 107.3 %collective-permute-start.55 = (bf16[384,2560]{1,0:T(8,128)(2,1)}, bf16[384,2560]{1,0:T(8,128)(2,1)}, u32[]{:S(2)}, u32[]{:S(2)}) collective-permute-start(bf16[384,2560]{1,0:T(8,128)(2,1)} %get-tuple-element.127), channel_id=1, source_target_pairs={{0,4},{1,5},{2,6},{3,7},{4,0},{5,1},{6,2},{7,3},{8,12},{9,13},{10,... | collective-permute-start | bytes 5898248 | tf_op jit(solution)/shard_map/ppermute | solution.py:60
  1408.1 135.0 %collective-permute-start.72 = (bf16[320,640]{1,0:T(8,128)(2,1)S(1)}, bf16[320,640]{1,0:T(8,128)(2,1)S(1)}, u32[]{:S(2)}, u32[]{:S(2)}) collective-permute-start(bf16[320,640]{1,0:T(8,128)(2,1)S(1)} %fusion.61), channel_id=1, source_target_pairs={{0,4},{1,5},{2,0},{3,1},{4,6},{5,7},{6,2},{7,3},{8,12},{9,13},{10,... | collective-permute-start | bytes 1228808 | tf_op jit(solution)/shard_map/ppermute | solution.py:60
  1461.3 106.9 %collective-permute-start.58 = (bf16[384,2560]{1,0:T(8,128)(2,1)}, bf16[384,2560]{1,0:T(8,128)(2,1)}, u32[]{:S(2)}, u32[]{:S(2)}) collective-permute-start(bf16[384,2560]{1,0:T(8,128)(2,1)} %get-tuple-element.81), channel_id=1, source_target_pairs={{2,4},{3,5},{4,2},{5,3},{10,12},{11,13},{12,10},{13,11},{18,20},{1... | collective-permute-start | bytes 5898248 | tf_op jit(solution)/shard_map/ppermute | solution.py:60
  1463.5 79.0 %collective-permute-start.64 = (bf16[320,962]{1,0:T(8,128)(2,1)S(1)}, bf16[320,962]{1,0:T(8,128)(2,1)S(1)}, u32[]{:S(2)}, u32[]{:S(2)}) collective-permute-start(bf16[320,962]{1,0:T(8,128)(2,1)S(1)} %fusion.44), channel_id=1, source_target_pairs={{0,4},{1,5},{2,0},{3,1},{4,6},{5,7},{6,2},{7,3},{8,12},{9,13},{10,... | collective-permute-start | bytes 1847048 | tf_op jit(solution)/shard_map/ppermute | solution.py:60
  1471.6 70.9 %collective-permute-start.63 = (bf16[320,962]{1,0:T(8,128)(2,1)S(1)}, bf16[320,962]{1,0:T(8,128)(2,1)S(1)}, u32[]{:S(2)}, u32[]{:S(2)}) collective-permute-start(bf16[320,962]{1,0:T(8,128)(2,1)S(1)} %bitcast_convert_fusion.3), channel_id=1, source_target_pairs={{2,4},{3,5},{4,2},{5,3},{10,12},{11,13},{12,10},{13,11},{18,20},{1... | collective-permute-start | bytes 1847048 | tf_op jit(solution)/shard_map/ppermute | solution.py:60
  1472.4 70.7 %collective-permute-start.71 = (bf16[320,640]{1,0:T(8,128)(2,1)S(1)}, bf16[320,640]{1,0:T(8,128)(2,1)S(1)}, u32[]{:S(2)}, u32[]{:S(2)}) collective-permute-start(bf16[320,640]{1,0:T(8,128)(2,1)S(1)} %bitcast_convert_fusion.4), channel_id=1, source_target_pairs={{2,4},{3,5},{4,2},{5,3},{10,12},{11,13},{12,10},{13,11},{18,20},{1... | collective-permute-start | bytes 1228808 | tf_op jit(solution)/shard_map/ppermute | solution.py:60
  (162 other events, 6776.5 us)

commit v2 on v1

--- a/solution.py
+++ b/solution.py
@@ -14,6 +14,7 @@
 KEY_BLOCK = 256
 MASKED = -1e30
 VMEM_LIMIT = 48 * 1024 * 1024
+LINK_VMEM_LIMIT = 60 * 1024 * 1024
 
 epsilon = 1e-05
 rope_base = 10000.0
@@ -28,6 +29,10 @@
         preferred_element_type=jnp.float32,
     )
     return product.astype(out_type)
+
+
+def after(value, *earlier):
+    return lax.optimization_barrier((value,) + earlier)[0]
 
 
 def inverse_root(vectors):
@@ -89,97 +94,21 @@
     def swap(self, array):
         return jnp.where(self.home, array, self.cross(array))
 
-    def relative_features(self, array):
-        width = array.shape[-1] // self.chips
-        return jnp.concatenate(
-            [
-                lax.dynamic_slice_in_dim(array, (self.p ^ step) * width, width, array.ndim - 1)
-                for step in range(self.chips)
-            ],
-            axis=-1,
-        )
-
-    def gather_rows(self, own):
-        same = [own] + [self.to_low(own, self.low - step) for step in range(1, self.low)]
-        blocks = []
-        for block in same:
-            blocks.append(block)
-            blocks.append(self.to_core(block))
-        return blocks
-
-    def scatter_rows(self, blocks):
+    def quarter_rows(self, array, step, other):
+        rows = array.shape[0] // self.tensor_count
+        index = (self.c ^ other) * self.low + (self.tl + step) % self.low
+        return lax.dynamic_slice_in_dim(array, index * rows, rows, 0)
+
+    def scatter_rows(self, partial):
         total = None
         for step in list(range(1, self.low)) + [0]:
-            mine, others = blocks[2 * step], blocks[2 * step + 1]
+            mine = self.quarter_rows(partial, step, 0)
+            others = self.quarter_rows(partial, step, 1)
             pair = mine.astype(jnp.float32) + self.to_core(others).astype(jnp.float32)
             if step:
                 pair = self.to_low(pair.astype(jnp.bfloat16), step).astype(jnp.float32)
             total = pair if total is None else total + pair
         return total
-
-    def gather_weight(self, shard):
-        turned = self.home_turn(shard)
-        crossed = self.cross(shard)
-        mine = jnp.where(self.home, shard, turned)
-        other = jnp.where(self.home, turned, crossed)
-        first = jnp.where(self.c == 0, mine, other)
-        second = jnp.where(self.c == 0, other, mine)
-        if self.chips == 4:
-            units = [[first, second], None, None, None]
-            unit = jnp.stack([first, second])
-            by_x = self.to_chip(unit, 1)
-            by_y = self.to_chip(unit, 2)
-            diagonal_first = self.to_chip(by_y[0], 1)
-            diagonal_second = self.to_chip(by_x[1], 2)
-            units = [first, second, by_x[0], by_x[1], by_y[0], by_y[1], diagonal_first, diagonal_second]
-        else:
-            unit = jnp.stack([first, second])
-            units = [first, second]
-            for step in range(1, self.chips):
-                arrived = self.to_chip(unit, step)
-                units += [arrived[0], arrived[1]]
-        return jnp.concatenate(units, axis=0)
-
-    def scatter_weight(self, partial):
-        rows = partial.shape[0] // self.dp_count
-        units = partial.reshape(self.chips, 2, rows, partial.shape[1])
-
-        def low(value):
-            return value.astype(jnp.bfloat16)
-
-        def wide(value):
-            return value.astype(jnp.float32)
-
-        if self.chips == 4:
-            by_x = self.to_chip(units[3, 0], 1)
-            by_y = self.to_chip(units[3, 1], 2)
-            unit_x = jnp.stack([units[1, 0], low(wide(units[1, 1]) + wide(by_y))])
-            unit_y = jnp.stack([low(wide(units[2, 0]) + wide(by_x)), units[2, 1]])
-            total = (
-                wide(units[0])
-                + wide(self.to_chip(unit_x, 1))
-                + wide(self.to_chip(unit_y, 2))
-            )
-        else:
-            total = wide(units[0])
-            for step in range(1, self.chips):
-                total = total + wide(self.to_chip(units[step], step))
-        mine = jnp.where(self.c == 0, total[0], total[1])
-        other = jnp.where(self.c == 0, total[1], total[0])
-        turned = self.away_turn(low(jnp.where(self.home, other, mine)))
-        crossed = self.cross(low(other))
-        return jnp.where(self.home, mine, wide(crossed)) + wide(turned)
-
-    def sum_tensor(self, array):
-        for bit in range(self.tensor_count.bit_length() - 1):
-            step = 1 << bit
-
-            def target(p, c, th, tl, step=step):
-                moved = (th * self.low + tl) ^ step
-                return (p, c, moved // self.low, moved % self.low)
-
-            array = array + self.move(array, target)
-        return array
 
 
 def project_kernel(heads, tokens_ref, gain_ref, weight_ref, cosine_ref, sine_ref, normed_ref, out_ref):
@@ -501,6 +430,912 @@
     )
 
 
+MESH = pl.DeviceIdType.MESH
+CHUNK = 64
+
+
+class Links:
+    def __init__(self, dp_count, tensor_count, send, recv, local):
+        self.chips, self.low = dp_count // 2, tensor_count // 2
+        self.send, self.recv, self.local = send, recv, local
+        self.used = 0
+        self.used_local = 0
+        self.unsent = []
+        self.all_low = False
+        dp_index, tensor_index = lax.axis_index("dp"), lax.axis_index("tensor")
+        self.dp_index, self.tensor_index = dp_index, tensor_index
+        self.p, self.c = dp_index // 2, dp_index % 2
+        self.th, self.tl = tensor_index // self.low, tensor_index % self.low
+        self.home = self.c == self.th
+        self.away = self.c != self.th
+        self.quarter = self.c * self.low + self.tl
+
+    def at(self, p, c, th, tl):
+        return (2 * p + c, th * self.low + tl)
+
+    def chip(self, step):
+        p = self.p
+        moved = p
+        for bit in (1, 2, 4):
+            if step & bit:
+                moved = moved + bit * (1 - 2 * ((p // bit) % 2))
+        return moved
+
+    def chip_peer(self, step):
+        return self.at(self.chip(step), self.c, self.th, self.tl)
+
+    def core_peer(self):
+        return self.at(self.p, 1 - self.c, self.th, self.tl)
+
+    def low_peer(self, step):
+        return self.at(self.p, self.c, self.th, (self.tl + step) % self.low)
+
+    def cross_peer(self):
+        return self.at(self.p, 1 - self.c, 1 - self.th, self.tl)
+
+    def partner(self):
+        return self.at(self.p, self.c, 1 - self.th, self.tl)
+
+    def chip_steps(self):
+        return (1, 2) if self.chips == 4 else tuple(range(1, self.chips))
+
+    def enter(self):
+        peers = [self.core_peer(), self.cross_peer(), self.partner()]
+        peers += [self.chip_peer(step) for step in self.chip_steps()]
+        peers += [self.low_peer(step) for step in range(1, self.low)]
+        if self.all_low:
+            peers += [
+                self.at(self.p, self.c, 1 - self.th, (self.tl + step) % self.low)
+                for step in range(1, self.low)
+            ]
+        barrier = pltpu.get_barrier_semaphore()
+        for peer in peers:
+            pl.semaphore_signal(barrier, inc=1, device_id=peer, device_id_type=MESH)
+        pl.semaphore_wait(barrier, len(peers))
+
+    def copy(self, source, target, peer, when=None):
+        slot = self.used
+        self.used += 1
+
+        def make():
+            return pltpu.make_async_remote_copy(
+                src_ref=source,
+                dst_ref=target,
+                send_sem=self.send.at[slot],
+                recv_sem=self.recv.at[slot],
+                device_id=peer,
+                device_id_type=MESH,
+            )
+
+        item = Item(make, when)
+        self.unsent.append(item)
+        return item
+
+    def local_slot(self):
+        self.used_local += 1
+        return self.used_local - 1
+
+    def keep(self, source, target, when=None):
+        slot = self.used_local
+        self.used_local += 1
+        return Item(lambda: pltpu.make_async_copy(source, target, self.local.at[slot]), when)
+
+    def drop(self, items):
+        self.unsent = [item for item in self.unsent if item not in items]
+
+    def leave(self):
+        for item in self.unsent:
+            item.sent()
+
+
+class Item:
+    def __init__(self, make, when):
+        self.make, self.when = make, when
+
+    def run(self, action):
+        if self.when is None:
+            action(self.make())
+        else:
+            pl.when(self.when)(lambda: action(self.make()))
+
+    def start(self):
+        self.run(lambda copy: copy.start())
+
+    def arrived(self):
+        self.run(lambda copy: copy.wait_recv())
+
+    def sent(self):
+        self.run(lambda copy: copy.wait_send())
+
+    def done(self):
+        self.run(lambda copy: copy.wait())
+
+
+class WeightGather:
+    def __init__(self, links, shard, full):
+        self.links, self.shard, self.full = links, shard, full
+        rows = shard.shape[0]
+        self.rows = rows
+        mine = full.at[pl.ds(links.dp_index * rows, rows)]
+        home_int = links.home.astype(jnp.int32)
+        self.first = links.copy(
+            shard,
+            mine,
+            links.at(
+                links.p,
+                home_int * links.c + (1 - home_int) * (1 - links.c),
+                home_int * (1 - links.th) + (1 - home_int) * links.th,
+                links.tl,
+            ),
+        )
+        self.second = links.copy(shard, mine, links.cross_peer(), links.away)
+        self.own = links.keep(shard, mine, links.home)
+        unit = 2 * rows
+        self.direct = []
+        self.forward = []
+        here = full.at[pl.ds(links.p * unit, unit)]
+        for step in links.chip_steps():
+            self.direct.append(links.copy(here, here, links.chip_peer(step)))
+        if links.chips == 4:
+            top = full.at[pl.ds(links.chip(2) * unit, rows)]
+            bottom = full.at[pl.ds(links.chip(1) * unit + rows, rows)]
+            self.forward.append(links.copy(top, top, links.chip_peer(1)))
+            self.forward.append(links.copy(bottom, bottom, links.chip_peer(2)))
+
+    def turn(self):
+        self.first.start()
+        self.second.start()
+        self.own.start()
+
+    def settle_unit(self):
+        self.first.arrived()
+        self.second.arrived()
+        self.own.done()
+
+    def spread(self):
+        self.settle_unit()
+        self.spread_unit()
+
+    def spread_unit(self):
+        for item in self.direct:
+            item.start()
+
+    def pass_on(self):
+        for item in self.direct:
+            item.arrived()
+        for item in self.forward:
+            item.start()
+
+    def finish(self):
+        for item in self.forward:
+            item.arrived()
+
+
+class RowGather:
+    def __init__(self, links, full, rows):
+        self.links = links
+        mine = full.at[pl.ds(links.quarter * rows, rows)]
+        self.to_core = links.copy(mine, mine, links.core_peer())
+        self.to_low = []
+        self.onward = []
+        for step in range(1, links.low):
+            self.to_low.append(links.copy(mine, mine, links.low_peer(step)))
+            came = (links.tl + links.low - step) % links.low
+            block = full.at[pl.ds((links.c * links.low + came) * rows, rows)]
+            self.onward.append(links.copy(block, block, links.core_peer()))
+
+    def start(self):
+        for item in self.to_low:
+            item.start()
+        self.to_core.start()
+
+    def pass_on(self):
+        for arriving, item in zip(self.to_low, self.onward):
+            arriving.arrived()
+            item.start()
+
+    def finish(self):
+        self.to_core.arrived()
+        for item in self.onward:
+            item.arrived()
+
+
+class RowScatter:
+    def __init__(self, links, partial, mine, others, sums, arrivals, rows):
+        self.links, self.rows = links, rows
+        self.mine, self.others, self.sums, self.arrivals = mine, others, sums, arrivals
+        low = links.low
+        self.load = links.keep(partial.at[pl.ds(links.c * low * rows, low * rows)], mine)
+        self.swap = links.copy(
+            partial.at[pl.ds((1 - links.c) * low * rows, low * rows)], others, links.core_peer()
+        )
+        self.sends = [
+            links.copy(sums.at[step - 1], arrivals.at[step - 1], links.low_peer(step))
+            for step in range(1, low)
+        ]
+
+    def start(self):
+        self.swap.start()
+        self.load.start()
+
+    def send_sums(self):
+        self.load.done()
+        self.swap.arrived()
+        for step in range(1, self.links.low):
+            base = ((self.links.tl + step) % self.links.low) * self.rows
+
+            @pl.loop(0, self.rows // CHUNK)
+            def _(i, base=base, step=step):
+                span = pl.ds(pl.multiple_of(base + i * CHUNK, CHUNK), CHUNK)
+                total = self.mine[span].astype(jnp.float32) + self.others[span].astype(jnp.float32)
+                self.sums[step - 1, pl.ds(pl.multiple_of(i * CHUNK, CHUNK), CHUNK)] = total.astype(jnp.bfloat16)
+
+            self.sends[step - 1].start()
+
+    def collect(self, use):
+        for item in self.sends:
+            item.arrived()
+        base = self.links.tl * self.rows
+
+        @pl.loop(0, self.rows // CHUNK)
+        def _(i):
+            at = pl.multiple_of(i * CHUNK, CHUNK)
+            span = pl.ds(pl.multiple_of(base + at, CHUNK), CHUNK)
+            total = self.mine[span].astype(jnp.float32) + self.others[span].astype(jnp.float32)
+            for step in range(1, self.links.low):
+                total = total + self.arrivals[step - 1, pl.ds(at, CHUNK)].astype(jnp.float32)
+            use(pl.ds(at, CHUNK), total)
+
+
+def scatter_scratch(low, rows, width):
+    return [
+        pltpu.VMEM((low * rows, width), jnp.bfloat16),
+        pltpu.VMEM((low * rows, width), jnp.bfloat16),
+        pltpu.VMEM((low - 1, rows, width), jnp.bfloat16),
+        pltpu.VMEM((low - 1, rows, width), jnp.bfloat16),
+    ]
+
+
+def semaphores(count, local_count):
+    return [
+        pltpu.SemaphoreType.DMA((count,)),
+        pltpu.SemaphoreType.DMA((count,)),
+        pltpu.SemaphoreType.DMA((local_count,)),
+    ]
+
+
+def anywhere(count):
+    return [pl.BlockSpec(memory_space=pl.ANY)] * count
+
+
+def in_vmem(count):
+    return [pl.BlockSpec(memory_space=pltpu.VMEM)] * count
+
+
+def link_params(number):
+    return pltpu.CompilerParams(
+        collective_id=number, has_side_effects=True, vmem_limit_bytes=LINK_VMEM_LIMIT
+    )
+
+
+ADD_ROWS = 32
+
+
+def row_loop(rows, body):
+    @pl.loop(0, rows // ADD_ROWS)
+    def _(i):
+        body(pl.ds(pl.multiple_of(i * ADD_ROWS, ADD_ROWS), ADD_ROWS))
+
+
+class WeightScatter:
+    def __init__(self, links, partial, result, inbox, turned, sums, leaving, stage):
+        self.links, self.partial, self.result = links, partial, result
+        self.inbox, self.turned, self.sums, self.leaving = inbox, turned, sums, leaving
+        rows = partial.shape[0] // (2 * links.chips)
+        self.rows = rows
+        width = partial.shape[1]
+        self.stage = [stage.at[i, pl.ds(0, rows), pl.ds(0, width)] for i in range(3)]
+        self.both = links.chips == 4
+        self.loads = [
+            links.local_slot() for _ in range(3)
+        ]
+        if self.both:
+            x_peer, y_peer = links.chip_peer(1), links.chip_peer(2)
+            self.before = [
+                links.copy(self.part(3, 0), inbox.at[0], x_peer),
+                links.copy(self.part(3, 1), inbox.at[1], y_peer),
+            ]
+            self.direct = [
+                links.copy(self.part(1, 0), inbox.at[2], x_peer),
+                links.copy(self.part(2, 1), inbox.at[3], y_peer),
+            ]
+            self.summed = [
+                links.copy(sums.at[0], inbox.at[4], y_peer),
+                links.copy(sums.at[1], inbox.at[5], x_peer),
+            ]
+            self.arrivals = ((2, 4), (5, 3))
+        else:
+            self.before, self.summed, self.direct = [], [], []
+            for step in links.chip_steps():
+                for half in range(2):
+                    at = 2 * (step - 1) + half
+                    self.direct.append(
+                        links.copy(self.part(step, half), inbox.at[at], links.chip_peer(step))
+                    )
+            self.arrivals = tuple(
+                tuple(2 * (step - 1) + half for step in links.chip_steps()) for half in range(2)
+            )
+        home_int = links.home.astype(jnp.int32)
+        self.first = links.copy(
+            leaving.at[0],
+            turned.at[0],
+            links.at(
+                links.p,
+                home_int * (1 - links.c) + (1 - home_int) * links.c,
+                home_int * links.th + (1 - home_int) * (1 - links.th),
+                links.tl,
+            ),
+        )
+        self.second = links.copy(leaving.at[1], turned.at[1], links.cross_peer(), links.away)
+
+    def part(self, step, half):
+        start = (2 * self.links.chip(step) + half) * self.rows
+        return self.partial.at[pl.ds(start, self.rows)]
+
+    def load(self, sources):
+        copies = [
+            pltpu.make_async_copy(source, stage, self.links.local.at[slot])
+            for source, stage, slot in zip(sources, self.stage, self.loads)
+        ]
+        for copy in copies:
+            copy.start()
+        for copy in copies:
+            copy.wait()
+
+    def start(self, which):
+        for item in getattr(self, which):
+            item.start()
+
+    def arrived(self, which):
+        for item in getattr(self, which):
+            item.arrived()
+
+    def add_before(self):
+        if not self.both:
+            return
+        self.arrived("before")
+        for index, part in ((0, self.part(2, 0)), (1, self.part(1, 1))):
+            self.load([part, self.inbox.at[index]])
+
+            def body(span, index=index):
+                total = self.stage[0][span].astype(jnp.float32) + self.stage[1][span].astype(jnp.float32)
+                self.sums[index, span] = total.astype(jnp.bfloat16)
+
+            row_loop(self.rows, body)
+            self.summed[index].start()
+
+    def turn(self):
+        links = self.links
+        for half in range(2):
+            sources = [self.part(0, half)] + [self.inbox.at[at] for at in self.arrivals[half]]
+            kept = links.c == half
+            if len(sources) == 3:
+                self.load(sources)
+
+                def body(span, half=half, kept=kept):
+                    total = self.stage[0][span].astype(jnp.float32)
+                    total = total + self.stage[1][span].astype(jnp.float32)
+                    self.settle(span, total + self.stage[2][span].astype(jnp.float32), kept)
+
+                row_loop(self.rows, body)
+            else:
+                self.fold(sources, kept)
+        self.first.start()
+        self.second.start()
+
+    def fold(self, sources, kept):
+        rows = self.rows
+        total = self.total
+        self.load(sources[:1])
+        row_loop(rows, lambda span: total.__setitem__(span, self.stage[0][span].astype(jnp.float32)))
+        for source in sources[1:]:
+            self.load([source])
+
+            def body(span):
+                total[span] = total[span] + self.stage[0][span].astype(jnp.float32)
+
+            row_loop(rows, body)
+        row_loop(rows, lambda span: self.settle(span, total[span], kept))
+
+    def settle(self, span, total, kept):
+        low = total.astype(jnp.bfloat16)
+        links = self.links
+
+        @pl.when(kept & links.home)
+        def _():
+            self.result[span] = total
+
+        @pl.when(kept & links.away)
+        def _():
+            self.leaving[0, span] = low
+
+        @pl.when(jnp.logical_not(kept) & links.home)
+        def _():
+            self.leaving[0, span] = low
+
+        @pl.when(jnp.logical_not(kept) & links.away)
+        def _():
+            self.leaving[1, span] = low
+
+    def finish(self):
+        links = self.links
+        self.first.arrived()
+        self.second.arrived()
+
+        @pl.when(links.home)
+        def _():
+            def body(span):
+                self.result[span] = self.result[span] + self.turned[0, span].astype(jnp.float32)
+
+            row_loop(self.rows, body)
+
+        @pl.when(links.away)
+        def _():
+            def body(span):
+                self.result[span] = self.turned[1, span].astype(jnp.float32) + self.turned[0, span].astype(
+                    jnp.float32
+                )
+
+            row_loop(self.rows, body)
+
+
+def weight_scatter_scratch(chips, rows, width):
+    return [pltpu.VMEM((2, rows, width), jnp.bfloat16)] * 3
+
+
+def inbox_shape(chips, rows, width):
+    count = 6 if chips == 4 else 2 * (chips - 1)
+    return jax.ShapeDtypeStruct((count, rows, width), jnp.bfloat16)
+
+
+def scatter_shapes(chips, partial):
+    rows = partial.shape[0] // (2 * chips)
+    width = partial.shape[1]
+    return rows, width
+
+
+def tail_kernel(
+    dp_count,
+    tensor_count,
+    gain_column,
+    partial,
+    grad_gate,
+    grad_up,
+    grad_output,
+    grad_first,
+    own_ref,
+    grad_residual_ref,
+    gain_ref,
+    input_ref,
+    gate_ref,
+    up_ref,
+    output_ref,
+    first_ref,
+    gate_in,
+    up_in,
+    output_in,
+    first_in,
+    *scratch,
+):
+    gate_work, up_work, output_work, first_work = (scratch[3 * i : 3 * i + 3] for i in range(4))
+    stage, leaving, crossed, mine, others, sums, arrivals, gains_out, gains_in, total = scratch[12:22]
+    links = Links(dp_count, tensor_count, *scratch[22:])
+    links.all_low = True
+    rows = own_ref.shape[0]
+    scatter = RowScatter(links, partial, mine, others, sums, arrivals, rows)
+    crossing = links.copy(leaving, crossed, links.cross_peer(), links.away)
+    weights = []
+    for grad, result, inbox, work in (
+        (grad_gate, gate_ref, gate_in, gate_work),
+        (grad_up, up_ref, up_in, up_work),
+        (grad_output, output_ref, output_in, output_work),
+        (grad_first, first_ref, first_in, first_work),
+    ):
+        turned, added, turning = work
+        made = WeightScatter(links, grad, result, inbox, turned, added, turning, stage)
+        made.total = None if made.both else total.at[pl.ds(0, made.rows), pl.ds(0, grad.shape[1])]
+        weights.append(made)
+    gate, up, output, first = weights
+    gain_sends = []
+    for step in range(1, tensor_count):
+        other = (links.tensor_index + step) % tensor_count
+        gain_sends.append(
+            links.copy(gains_out, gains_in.at[step - 1], links.at(links.p, links.c, other // links.low, other % links.low))
+        )
+
+    links.enter()
+    gate.start("before")
+    scatter.start()
+    gate.start("direct")
+    scatter.send_sums()
+    gate.add_before()
+
+    def use(span, grad_normed):
+        own = own_ref[span].astype(jnp.float32)
+        root = lax.rsqrt(jnp.mean(own * own, axis=-1, keepdims=True) + epsilon)
+        unit = own * root
+        scaled = grad_normed * gain_ref[...]
+        grad = grad_residual_ref[span] + root * (
+            scaled - unit * jnp.mean(scaled * unit, axis=-1, keepdims=True)
+        )
+        input_ref[span] = grad
+        leaving[span] = grad.astype(jnp.bfloat16)
+
+    gate.arrived("direct")
+    up.start("before")
+    scatter.collect(use)
+    crossing.start()
+    gate.arrived("summed")
+    up.start("direct")
+    gate.turn()
+    up.add_before()
+    up.arrived("direct")
+    output.start("before")
+    output.start("direct")
+    up.arrived("summed")
+    first.start("before")
+    up.turn()
+    output.add_before()
+    gate.finish()
+    output.arrived("direct")
+    first.start("direct")
+    first.add_before()
+    output.arrived("summed")
+    output.turn()
+    crossing.arrived()
+
+    @pl.when(links.away)
+    def _():
+        def body(span):
+            input_ref[span] = crossed[span].astype(jnp.float32)
+
+        row_loop(rows, body)
+
+    first.arrived("direct")
+    first.arrived("summed")
+    first.turn()
+    up.finish()
+    output.finish()
+    first.finish()
+    width = first_ref.shape[1]
+    gains_out[...] = first_ref[:, width - 128 :]
+    for item in gain_sends:
+        item.start()
+    for item in gain_sends:
+        item.arrived()
+    summed = gains_out[...]
+    for step in range(1, tensor_count):
+        summed = summed + gains_in[step - 1]
+    column = width - 128 + lax.broadcasted_iota(jnp.int32, summed.shape, 1)
+    first_ref[:, width - 128 :] = jnp.where(column >= gain_column, summed, gains_out[...])
+    links.leave()
+
+
+def tail(dp_count, tensor_count, gain_column, partial, grads, own, grad_residual, gain):
+    rows, width = own.shape
+    low, chips = tensor_count // 2, dp_count // 2
+    shapes = [scatter_shapes(chips, grad) for grad in grads]
+    widest = max(columns for _, columns in shapes)
+    most = shapes[0][0]
+    scratch = []
+    for block, columns in shapes:
+        scratch += weight_scatter_scratch(chips, block, columns)
+    scratch += [
+        pltpu.VMEM((3, most, widest), jnp.bfloat16),
+        pltpu.VMEM((rows, width), jnp.bfloat16),
+        pltpu.VMEM((rows, width), jnp.bfloat16),
+    ]
+    scratch += scatter_scratch(low, rows, width)
+    scratch += [
+        pltpu.VMEM((most, 128), jnp.float32),
+        pltpu.VMEM((tensor_count - 1, most, 128), jnp.float32),
+        pltpu.VMEM((most, widest) if chips != 4 else (8, 128), jnp.float32),
+    ]
+    results = pl.pallas_call(
+        functools.partial(tail_kernel, dp_count, tensor_count, gain_column),
+        out_shape=[jax.ShapeDtypeStruct((rows, width), jnp.float32)]
+        + [jax.ShapeDtypeStruct(shape, jnp.float32) for shape in shapes]
+        + [inbox_shape(chips, *shape) for shape in shapes],
+        in_specs=anywhere(5) + in_vmem(3),
+        out_specs=in_vmem(5) + anywhere(4),
+        scratch_shapes=scratch + semaphores(96, 24),
+        compiler_params=link_params(3),
+        name="tail",
+    )(partial, *grads, own, grad_residual, gain)
+    return results[:5]
+
+
+def gather_first_kernel(
+    dp_count, tensor_count, tokens, first, output, gate, tokens_all, first_full, output_full, gate_full, *sems
+):
+    links = Links(dp_count, tensor_count, *sems)
+    rows = tokens.shape[0]
+    mine = tokens_all.at[pl.ds(links.tensor_index * rows, rows)]
+    crossing = links.copy(tokens, mine, links.cross_peer(), links.away)
+    staying = links.keep(tokens, mine, links.home)
+    gather_tokens = RowGather(links, tokens_all, rows)
+    weights = [
+        WeightGather(links, shard, full)
+        for shard, full in ((first, first_full), (output, output_full), (gate, gate_full))
+    ]
+    links.enter()
+    weights[0].turn()
+    crossing.start()
+    staying.start()
+
+    @pl.when(links.home)
+    def _():
+        staying.make().wait()
+        gather_tokens.start()
+
+    weights[0].spread()
+    weights[1].turn()
+
+    @pl.when(links.away)
+    def _():
+        crossing.make().wait_recv()
+        gather_tokens.start()
+
+    weights[1].spread()
+    weights[2].turn()
+    weights[0].pass_on()
+    gather_tokens.pass_on()
+    weights[1].pass_on()
+    weights[0].finish()
+    gather_tokens.finish()
+    weights[1].finish()
+    weights[2].settle_unit()
+    links.drop(weights[2].direct + weights[2].forward)
+    links.leave()
+
+
+def gather_first(dp_count, tensor_count, tokens, first, output, gate):
+    def full(shard, times):
+        return jax.ShapeDtypeStruct((shard.shape[0] * times, shard.shape[1]), shard.dtype)
+
+    return pl.pallas_call(
+        functools.partial(gather_first_kernel, dp_count, tensor_count),
+        out_shape=[
+            full(tokens, tensor_count),
+            full(first, dp_count),
+            full(output, dp_count),
+            full(gate, dp_count),
+        ],
+        in_specs=in_vmem(4),
+        out_specs=anywhere(4),
+        scratch_shapes=semaphores(64, 8),
+        compiler_params=link_params(0),
+        name="gather_first",
+    )(tokens, first, output, gate)
+
+
+def middle_kernel(
+    dp_count,
+    tensor_count,
+    moved_units,
+    partial,
+    tokens_all,
+    cot,
+    up,
+    up_turned,
+    up_crossed,
+    down,
+    gate_part,
+    *rest,
+):
+    gate_units, rest = rest[:moved_units], rest[moved_units:]
+    gain_ref, residual_ref, normed_all, cot_all, up_full, down_full, gate_full = rest[:7]
+    own, normed, mine, others, sums, arrivals = rest[7:13]
+    links = Links(dp_count, tensor_count, *rest[13:])
+    rows = cot.shape[0]
+    scatter = RowScatter(links, partial, mine, others, sums, arrivals, rows)
+    gather_normed = RowGather(links, normed_all, rows)
+    gather_cot = RowGather(links, cot_all, rows)
+    gate_gather = WeightGather(links, up, gate_full)
+    up_gather = WeightGather(links, up, up_full)
+    down_gather = WeightGather(links, down, down_full)
+    shard = up.shape[0]
+    here = up_full.at[pl.ds(links.dp_index * shard, shard)]
+    beside = up_full.at[pl.ds((2 * links.p + 1 - links.c) * shard, shard)]
+    quarter = pl.ds(links.quarter * rows, rows)
+    placements = [
+        links.keep(up, here, links.home),
+        links.keep(up_turned, beside, links.home),
+        links.keep(up_turned, here, links.away),
+        links.keep(up_crossed, beside, links.away),
+    ]
+    gate_placements = [
+        links.keep(unit, gate_full.at[pl.ds(links.chip(step) * 2 * shard, 2 * shard)])
+        for step, unit in zip(links.chip_steps(), gate_units)
+    ]
+    cot_crossing = links.copy(cot, cot_all.at[pl.ds(links.tensor_index * rows, rows)], links.cross_peer(), links.away)
+    cot_staying = links.keep(cot, cot_all.at[quarter], links.home)
+    load = links.keep(tokens_all.at[quarter], own)
+    store = links.keep(normed, normed_all.at[quarter])
+    links.drop([up_gather.first, up_gather.second, gate_gather.first, gate_gather.second] + gate_gather.direct)
+    links.enter()
+    scatter.start()
+    load.start()
+    for item in gate_placements + placements:
+        item.start()
+    for item in gate_placements:
+        item.done()
+    for item in gate_gather.forward:
+        item.start()
+    for item in placements:
+        item.done()
+    scatter.send_sums()
+    up_gather.spread_unit()
+    down_gather.turn()
+    cot_staying.start()
+    load.done()
+
+    def use(span, total):
+        residual = own[span].astype(jnp.float32) + total
+        residual_ref[span] = residual
+        root = lax.rsqrt(jnp.mean(residual * residual, axis=-1, keepdims=True) + epsilon)
+        normed[span] = (residual * root * gain_ref[...]).astype(jnp.bfloat16)
+
+    scatter.collect(use)
+    store.start()
+    store.done()
+    gather_normed.start()
+    down_gather.settle_unit()
+    cot_crossing.start()
+    up_gather.pass_on()
+    down_gather.spread_unit()
+    gate_gather.finish()
+    gather_normed.pass_on()
+    cot_staying.done()
+    cot_crossing.arrived()
+    gather_cot.start()
+    up_gather.finish()
+    down_gather.pass_on()
+    gather_normed.finish()
+    gather_cot.pass_on()
+    down_gather.finish()
+    gather_cot.finish()
+    links.leave()
+
+
+def middle(
+    dp_count, tensor_count, partial, tokens_all, cot, up, up_turned, up_crossed, down, gate_part, gate_units, gain
+):
+    rows, width = cot.shape
+    low = tensor_count // 2
+
+    def full(shard, times):
+        return jax.ShapeDtypeStruct((shard.shape[0] * times, shard.shape[1]), shard.dtype)
+
+    return pl.pallas_call(
+        functools.partial(middle_kernel, dp_count, tensor_count, len(gate_units)),
+        out_shape=[
+            jax.ShapeDtypeStruct((rows, width), jnp.float32),
+            full(cot, tensor_count),
+            full(cot, tensor_count),
+            full(up, dp_count),
+            full(down, dp_count),
+            jax.ShapeDtypeStruct(gate_part.shape, gate_part.dtype),
+        ],
+        in_specs=anywhere(2) + in_vmem(5) + anywhere(1) + in_vmem(len(gate_units) + 1),
+        out_specs=in_vmem(1) + anywhere(5),
+        scratch_shapes=[pltpu.VMEM((rows, width), jnp.bfloat16)] * 2
+        + scatter_scratch(low, rows, width)
+        + semaphores(64, 24),
+        input_output_aliases={7: 5},
+        compiler_params=link_params(1),
+        name="middle",
+    )(partial, tokens_all, cot, up, up_turned, up_crossed, down, gate_part, *gate_units, gain)
+
+
+def turn_back_kernel(
+    dp_count,
+    tensor_count,
+    partial,
+    cot_all,
+    grad_down,
+    residual_ref,
+    gain_ref,
+    grad_residual_ref,
+    gain_part_ref,
+    down_ref,
+    grad_rows,
+    down_in,
+    own,
+    low_grad,
+    turned,
+    added,
+    turning,
+    stage,
+    total_ref,
+    mine,
+    others,
+    sums,
+    arrivals,
+    *sems,
+):
+    links = Links(dp_count, tensor_count, *sems)
+    rows = residual_ref.shape[0]
+    down = WeightScatter(links, grad_down, down_ref, down_in, turned, added, turning, stage)
+    down.total = total_ref
+    scatter = RowScatter(links, partial, mine, others, sums, arrivals, rows)
+    gather = RowGather(links, grad_rows, rows)
+    quarter = pl.ds(links.quarter * rows, rows)
+    load = links.keep(cot_all.at[quarter], own)
+    store = links.keep(low_grad, grad_rows.at[quarter])
+    links.enter()
+    scatter.start()
+    load.start()
+    down.start("before")
+    down.start("direct")
+    scatter.send_sums()
+    load.done()
+    down.add_before()
+    gain_part_ref[...] = jnp.zeros_like(gain_part_ref)
+
+    def use(span, grad_normed):
+        residual = residual_ref[span]
+        root = lax.rsqrt(jnp.mean(residual * residual, axis=-1, keepdims=True) + epsilon)
+        unit = residual * root
+        gain_part_ref[...] += jnp.sum(grad_normed * unit, axis=0, keepdims=True)
+        scaled = grad_normed * gain_ref[...]
+        grad = own[span].astype(jnp.float32) + root * (
+            scaled - unit * jnp.mean(scaled * unit, axis=-1, keepdims=True)
+        )
+        grad_residual_ref[span] = grad
+        low_grad[span] = grad.astype(jnp.bfloat16)
+
+    scatter.collect(use)
+    store.start()
+    store.done()
+    gather.start()
+    down.arrived("direct")
+    down.arrived("summed")
+    down.turn()
+    gather.pass_on()
+    down.finish()
+    gather.finish()
+    links.leave()
+
+
+def turn_back(dp_count, tensor_count, partial, cot_all, grad_down, residual, gain):
+    rows, width = residual.shape
+    low, chips = tensor_count // 2, dp_count // 2
+    block, columns = scatter_shapes(chips, grad_down)
+    return pl.pallas_call(
+        functools.partial(turn_back_kernel, dp_count, tensor_count),
+        out_shape=[
+            jax.ShapeDtypeStruct((rows, width), jnp.float32),
+            jax.ShapeDtypeStruct((1, width), jnp.float32),
+            jax.ShapeDtypeStruct((block, columns), jnp.float32),
+            jax.ShapeDtypeStruct((rows * tensor_count, width), jnp.bfloat16),
+            inbox_shape(chips, block, columns),
+        ],
+        in_specs=anywhere(3) + in_vmem(2),
+        out_specs=in_vmem(3) + anywhere(2),
+        scratch_shapes=[pltpu.VMEM((rows, width), jnp.bfloat16)] * 2
+        + weight_scatter_scratch(chips, block, columns)
+        + [
+            pltpu.VMEM((3, block, columns), jnp.bfloat16),
+            pltpu.VMEM((block, columns) if chips != 4 else (8, 128), jnp.float32),
+        ]
+        + scatter_scratch(low, rows, width)
+        + semaphores(48, 16),
+        compiler_params=link_params(2),
+        name="turn_back",
+    )(partial, cot_all, grad_down, residual, gain)[:4]
+
+
 def starts_of(positions, length_row):
     ends = jnp.cumsum(length_row)
     inside = positions[:, None] >= ends[None, :]
@@ -542,34 +1377,45 @@
     group = heads // kv_heads
     head_columns = (heads + 2 * kv_heads) * HEAD_DIM
 
-    tokens_own = place.swap(place.relative_features(tokens))
-    first_weight = place.gather_weight(
-        jnp.concatenate(
-            [query_weight, key_weight, value_weight, attention_gain[:, None], feedforward_gain[:, None]],
-            axis=1,
-        )
-    )
-    tokens_all = jnp.concatenate(place.gather_rows(tokens_own), axis=0)
-    output_turned = place.gather_weight(output_weight.T)
-    gate_full = place.gather_weight(gate_weight)
-    up_full = place.gather_weight(up_weight)
-    down_turned = place.gather_weight(down_weight.T)
-    cot_own = place.swap(place.relative_features(cotangent))
-    cot_all = jnp.concatenate(place.gather_rows(cot_own), axis=0)
+    hidden_units = gate_weight.shape[1]
+    hidden_padded = -(-hidden_units // 128) * 128
+    output_padded = -(-heads * HEAD_DIM // 128) * 128
+    first_padded = -(-(head_columns + 2) // 128) * 128
+
+    def wide(array, columns):
+        return jnp.pad(array, ((0, 0), (0, columns - array.shape[1])))
+
+    gate_shard = wide(gate_weight, hidden_padded)
+    up_shard = wide(up_weight, hidden_padded)
+    down_shard = wide(down_weight.T, hidden_padded)
+    tokens_all, first_weight, output_turned, gate_part = gather_first(
+        dp_count,
+        tensor_count,
+        tokens,
+        wide(
+            jnp.concatenate(
+                [query_weight, key_weight, value_weight, attention_gain[:, None], feedforward_gain[:, None]],
+                axis=1,
+            ),
+            first_padded,
+        ),
+        wide(output_weight.T, output_padded),
+        gate_shard,
+    )
+    output_turned = output_turned[:, : heads * HEAD_DIM]
+    late_up = after(up_shard, tokens_all)
+    up_turned = place.home_turn(late_up)
+    up_crossed = place.cross(late_up)
+    unit = gate_part.shape[0] // place.chips
+    gate_unit = lax.dynamic_slice_in_dim(gate_part, place.p * unit, unit, 0)
+    steps = (1, 2) if place.chips == 4 else tuple(range(1, place.chips))
+    gate_units = [place.to_chip(gate_unit, step) for step in steps]
 
     numbers = jnp.concatenate([storage_order, pad_mask, lengths[0]])
     numbers = jnp.where(place.home, numbers, place.to_core(numbers))
     pad_column = numbers[count : 2 * count][:, None]
     length_row = numbers[2 * count :]
-    quarters = numbers[:count].reshape(2, place.low, rows)
-    order = []
-    for step in range(place.low):
-        for other in range(2):
-            quarter = lax.dynamic_index_in_dim(quarters, place.c ^ other, 0, keepdims=False)
-            order.append(
-                lax.dynamic_index_in_dim(quarter, (place.tl + step) % place.low, 0, keepdims=False)
-            )
-    order = jnp.concatenate(order)
+    order = numbers[:count]
 
     places = jnp.arange(count, dtype=jnp.int32)
     starts = starts_of(places, length_row)
@@ -595,56 +1441,54 @@
     attended, log_totals = attend(first_blocks, heads_all, start_row, pad_column, kv_heads, group)
     attended_stored = contract(to_storage, attended, 1, 0, jnp.bfloat16)
 
-    def split_rows(array):
-        return [array[i * rows : (i + 1) * rows] for i in range(tensor_count)]
-
-    attention_out = place.scatter_rows(
-        split_rows(contract(attended_stored, output_turned, 1, 1, jnp.bfloat16))
-    )
-    residual = tokens_own.astype(jnp.float32) + attention_out
-
-    root = inverse_root(residual)
-    normed_ffn = jnp.concatenate(
-        place.gather_rows((residual * root * feedforward_scale).astype(jnp.bfloat16)), axis=0
+    residual, normed_ffn, cot_all, up_full, down_turned, gate_full = middle(
+        dp_count,
+        tensor_count,
+        contract(attended_stored, output_turned, 1, 1, jnp.bfloat16),
+        tokens_all,
+        cotangent,
+        up_shard,
+        up_turned,
+        up_crossed,
+        down_shard,
+        gate_part,
+        gate_units,
+        feedforward_scale,
     )
     gate_values = contract(normed_ffn, gate_full, 1, 0)
     up_values = contract(normed_ffn, up_full, 1, 0)
     sigmoid = jax.nn.sigmoid(gate_values)
     hidden = (gate_values * sigmoid * up_values).astype(jnp.bfloat16)
-    layer_own = residual + place.scatter_rows(
-        split_rows(contract(hidden, down_turned, 1, 1, jnp.bfloat16))
-    )
 
     def leave(own):
         arrived = place.cross(own.astype(jnp.bfloat16)).astype(jnp.float32)
-        return place.relative_features(jnp.where(place.home, own, arrived))
-
-    layer_output = leave(layer_own)
+        return jnp.where(place.home, own, arrived)
 
     grad_hidden = contract(cot_all, down_turned, 1, 0)
     grad_gate = (grad_hidden * up_values * sigmoid * (1.0 + gate_values * (1.0 - sigmoid))).astype(
         jnp.bfloat16
     )
     grad_up = (grad_hidden * gate_values * sigmoid).astype(jnp.bfloat16)
-    grad_normed_ffn = place.scatter_rows(
-        split_rows(
-            (contract(grad_gate, gate_full, 1, 1) + contract(grad_up, up_full, 1, 1)).astype(jnp.bfloat16)
-        )
-    )
-    down_grad = place.scatter_weight(contract(cot_all, hidden, 0, 0, jnp.bfloat16))
-    gate_grad = place.scatter_weight(contract(normed_ffn, grad_gate, 0, 0, jnp.bfloat16))
-    up_grad = place.scatter_weight(contract(normed_ffn, grad_up, 0, 0, jnp.bfloat16))
-    unit_rows = residual * root
-    scaled = grad_normed_ffn * feedforward_scale
-    feedforward_part = jnp.sum(grad_normed_ffn * unit_rows, axis=0)
-    grad_residual = cot_own.astype(jnp.float32) + root * (
-        scaled - unit_rows * jnp.mean(scaled * unit_rows, axis=-1, keepdims=True)
-    )
-
-    grad_rows = jnp.concatenate(place.gather_rows(grad_residual.astype(jnp.bfloat16)), axis=0)
+    grad_part = (contract(grad_gate, gate_full, 1, 1) + contract(grad_up, up_full, 1, 1)).astype(
+        jnp.bfloat16
+    )
+    down_part_grad = contract(cot_all, hidden, 0, 0, jnp.bfloat16)
+    grad_residual, feedforward_part, down_grad, grad_rows = turn_back(
+        dp_count, tensor_count, grad_part, cot_all, down_part_grad, residual, feedforward_scale
+    )
+    late_hidden = after(hidden, grad_rows)
+    down_part = contract(late_hidden, down_turned, 1, 1, jnp.bfloat16)
+
+    layer_own = residual + place.scatter_rows(down_part)
+    layer_output = leave(layer_own)
     grad_attended = contract(grad_rows, output_turned, 1, 0, jnp.bfloat16)
     grad_attended = contract(to_sequence, grad_attended, 1, 0, jnp.bfloat16)
-    output_grad = place.scatter_weight(contract(grad_rows, attended_stored, 0, 0, jnp.bfloat16))
+    late_rows, late_gate, late_up_grad = lax.optimization_barrier((normed_ffn, grad_gate, grad_up, grad_rows))[:3]
+    grads = [
+        contract(late_rows, late_gate, 0, 0, jnp.bfloat16),
+        contract(late_rows, late_up_grad, 0, 0, jnp.bfloat16),
+        wide(contract(grad_rows, attended_stored, 0, 0, jnp.bfloat16), output_padded),
+    ]
     grad_query, grad_rest = attend_back(
         first_blocks,
         heads_all,
@@ -662,41 +1506,45 @@
         to_storage, jnp.concatenate([grad_query, grad_rest], axis=1), 1, 0, jnp.bfloat16
     )
     grad_normed_part = contract(grad_heads, first_weight[:, :head_columns], 1, 1)
-    grad_normed = place.scatter_rows(split_rows(grad_normed_part.astype(jnp.bfloat16)))
     tokens_wide = tokens_all.astype(jnp.float32)
     attention_part = jnp.sum(grad_normed_part * (tokens_wide * inverse_root(tokens_wide)), axis=0)
-    first_grad = place.scatter_weight(
-        jnp.concatenate(
-            [
-                contract(normed, grad_heads, 0, 0, jnp.bfloat16),
-                attention_part.astype(jnp.bfloat16)[:, None],
-                feedforward_part.astype(jnp.bfloat16)[:, None],
-            ],
-            axis=1,
+    grads.append(
+        wide(
+            jnp.concatenate(
+                [
+                    contract(normed, grad_heads, 0, 0, jnp.bfloat16),
+                    attention_part.astype(jnp.bfloat16)[:, None],
+                    feedforward_part[0].astype(jnp.bfloat16)[:, None],
+                ],
+                axis=1,
+            ),
+            first_padded,
         )
     )
-    gain_grads = place.sum_tensor(first_grad[:, head_columns:])
-    own_wide = tokens_own.astype(jnp.float32)
-    root_own = inverse_root(own_wide)
-    unit_rows = own_wide * root_own
-    scaled = grad_normed * attention_scale
-    input_grad = grad_residual + root_own * (
-        scaled - unit_rows * jnp.mean(scaled * unit_rows, axis=-1, keepdims=True)
+    input_grad, gate_grad, up_grad, output_grad, first_grad = tail(
+        dp_count,
+        tensor_count,
+        head_columns,
+        grad_normed_part.astype(jnp.bfloat16),
+        grads,
+        place.quarter_rows(tokens_all, 0, 0),
+        grad_residual,
+        attention_scale,
     )
     query_columns = heads * HEAD_DIM
     key_columns = kv_heads * HEAD_DIM
     return (
         layer_output,
-        leave(input_grad),
-        gain_grads[:, 0],
+        input_grad,
+        first_grad[:, head_columns],
         first_grad[:, :query_columns],
         first_grad[:, query_columns : query_columns + key_columns],
         first_grad[:, query_columns + key_columns : head_columns],
-        output_grad.T,
-        gain_grads[:, 1],
-        gate_grad,
-        up_grad,
-        down_grad.T,
+        output_grad[:, :query_columns].T,
+        first_grad[:, head_columns + 1],
+        gate_grad[:, :hidden_units],
+        up_grad[:, :hidden_units],
+        down_grad[:, :hidden_units].T,
     )
 
 

time: 1590 us -> 1280 us (0.81)
  Pallas kernels: 103 us -> 857 us
  waiting for transfers between devices: 479 us -> 19.3 us
  starting transfers between devices: 385 us -> 41.6 us
  other arithmetic: 158 us -> 35 us
  local copies, waits for them, and re-layouts: 165 us -> 44.2 us
  matrix products: 282 us -> 263 us
    pallas_call x0 -> x4, Pallas kernels: none -> 752 us  [the longest x1 283 us: tail(): pl.pallas_call(functools.partial(tail_kernel, dp_count, tensor_count, gai...]
    ppermute x91 -> x9, waiting for transfers between devices: 479 us -> 19.3 us  [move(): return lax.ppermute(array, AXES, pairs)]
    ppermute x91 -> x9, starting transfers between devices: 385 us -> 41.6 us  [move(): return lax.ppermute(array, AXES, pairs)]
    unnamed x219 -> x92, local copies, waits for them, and re-layouts: 49.2 us -> 10.4 us
    another operation x31 -> x1, other arithmetic: 38.9 us -> 0.18 us  [the longest x14 17.3 us: gather_weight(): unit = jnp.stack([first, second])]
    convert_element_type x4 -> x1, local copies, waits for them, and re-layouts: 46.2 us -> 7.86 us  [contract(): return product.astype(out_type)]
    convert_element_type x17 -> x1, other arithmetic: 30.8 us -> 0.01 us  [per_device(): feedforward_part[0].astype(jnp.bfloat16)[:, None]]
    convert_element_type x6 -> x2, local copies, waits for them, and re-layouts: 23.4 us -> 1.01 us  [the longest x1 0.61 us: per_device(): first_weight[:, head_columns + 1].astype(jnp.float32)[None, :]]
  transfers between devices with their start and end apart: 91 -> 9, of which waited for: 29 -> 1; matrix products, arithmetic and copies ran while one was open for 22% -> 12% of each run, Pallas kernels for 7% -> 31%
where the time goes in v2:
time: 1280 us; the launch traced here: 1260 us
  Pallas kernels  857 us (67%)
  matrix products  263 us (21%)
  local copies, waits for them, and re-layouts  44.2 us (3%)
  starting transfers between devices  41.6 us (3%)
  other arithmetic  35 us (3%)
  waiting for transfers between devices  19.3 us (2%)
    pallas_call x1, Pallas kernels, tail(): pl.pallas_call(functools.partial(tail_kernel, dp_count, tensor_count, gai...  283 us
    dot_general x17, matrix products, contract(): lax.dot_general(left, right, (((left_dim,), (right_dim,)), ((), ())), pre...  263 us
    pallas_call x1, Pallas kernels, middle(): pl.pallas_call(functools.partial(middle_kernel, dp_count, tensor_count, l...  197 us
    pallas_call x1, Pallas kernels, gather_first(): pl.pallas_call(functools.partial(gather_first_kernel, dp_count, tensor_co...  141 us
    pallas_call x1, Pallas kernels, turn_back(): pl.pallas_call(functools.partial(turn_back_kernel, dp_count, tensor_count...  131 us
    pallas_call x1, Pallas kernels, attend_back(): pl.pallas_call(functools.partial(attend_back_kernel, kv_heads, group), gr...  48 us
    ppermute x9, starting transfers between devices, move(): return lax.ppermute(array, AXES, pairs)  41.6 us
    pallas_call x1, Pallas kernels, attend(): pl.pallas_call(functools.partial(attend_kernel, kv_heads, group), grid_sp...  35.2 us
  transfers between devices with their start and end apart: 9, of which 1 were waited for; matrix products, arithmetic and copies ran while one was open for 12% of the time, Pallas kernels for 31%

profile of v2, /device:TPU:0, one launch (start us, length us, event | category | flops | bytes accessed | tf_op | source)
XLA Modules:
  0.0 1262.1 jit_solution(17788277714946455657)
XLA Ops:
  9.0 140.9 %gather_first.1 = (bf16[1536,2560]{1,0:T(8,128)(2,1)}, bf16[2560,1024]{1,0:T(8,128)(2,1)}, bf16[2560,640]{1,0:T(8,128)(2,1)}, bf16[2560,1792]{1,0:T(8,128)(2,1)}) custom-call(bf16[384,2560]{1,0:T(8,128)(2,1)} %tokens.1, bf16[320,1024]{1,0:T(8,128)(2,1)} %pad.18.first, bf16[320,640]{1,0:T(8,128)(2,1)} %bitcast.57, bf16[320,1792]{1,0:T(8,128)(2,1)} %pad.19.gate), custom_call_target="tpu_custom_call" | custom-call | tf_op jit(solution)/shard_map/gather_first/pallas_call | solution.py:1106
  149.9 14.5 %collective-permute-start.1 = (bf16[320,1792]{1,0:T(8,128)(2,1)S(1)}, bf16[320,1792]{1,0:T(8,128)(2,1)}, u32[]{:S(2)}, u32[]{:S(2)}) collective-permute-start(bf16[320,1792]{1,0:T(8,128)(2,1)S(1)} %pad.20.up), channel_id=1, source_target_pairs={{0,2},{1,3},{2,6},{3,7},{4,0},{5,1},{6,4},{7,5},{8,10},{9,11},{10,... | collective-permute-start | bytes 3440648 | tf_op jit(solution)/shard_map/ppermute | solution.py:65
  191.9 21.7 %project.1 = (bf16[1536,2560]{1,0:T(8,128)(2,1)}, bf16[1536,960]{1,0:T(8,128)(2,1)S(1)}) custom-call(bf16[1536,2560]{1,0:T(8,128)(2,1)} %get-tuple-element.41.tokens_ref.tokens_all, f32[1,2560]{1,0:T(1,128)S(1)} %reshape.115.gain_ref, bf16[2560,1024]{1,0:T(8,128)(2,1)} %get-tuple-element.42.weight_ref, f32[1536,40]{1,0:T(8,128)S(1)} %get-tuple-element.140.cosine_ref, ...), custom_call_target="tpu_custom_call" | custom-call | flops 8053063680 | bytes 20971520 | tf_op jit(solution)/shard_map/project/pallas_call | solution.py:134
  219.2 35.2 %attend.1 = (bf16[1536,640]{1,0:T(8,128)(2,1)S(1)}, f32[8,1536]{1,0:T(8,128)S(1)}) custom-call(s32[12]{0:T(128)S(1)} %and_select_fusion.first_ref, bf16[1536,960]{1,0:T(8,128)(2,1)S(1)} %fusion.18.query_ref.all_ref, bf16[1536,960]{1,0:T(8,128)(2,1)S(1)} %fusion.18.query_ref.all_ref, s32[1,1536]{1,0:T(1,128)S(1)} %broadcast_in_dim.28.start_ref, ...), custom_call_target="tpu_custom_call" | custom-call | flops 60000002048 | bytes 5898240 | tf_op jit(solution)/shard_map/attend/pallas_call | solution.py:243
  258.7 8.9 convolution_convert_fusion.partial
  267.6 197.1 %middle.1 = (f32[384,2560]{1,0:T(8,128)}, bf16[1536,2560]{1,0:T(8,128)(2,1)}, bf16[1536,2560]{1,0:T(8,128)(2,1)}, bf16[2560,1792]{1,0:T(8,128)(2,1)}, bf16[2560,...) custom-call(bf16[1536,2560]{1,0:T(8,128)(2,1)} %convolution_convert_fusion.partial, ...), custom_call_target="tpu_custom_call", output_to_operand_aliasing={{5}: (7, {})} | custom-call | tf_op jit(solution)/shard_map/middle/pallas_call | solution.py:1220
  464.8 21.2 %fusion.30 = f32[1536,1792]{1,0:T(8,128)} fusion(bf16[1536,2560]{1,0:T(8,128)(2,1)} %get-tuple-element.52.cot_all, bf16[2560,1792]{1,0:T(8,128)(2,1)} %get-tuple-element.53), kind=kOutput, calls=%fused_computation.81 | convolution fusion | flops 14092861440 | bytes 28049408 | tf_op jit(solution)/shard_map/dot_general | solution.py:25
  486.0 16.9 %fusion.29 = f32[1536,1792]{1,0:T(8,128)} fusion(bf16[1536,2560]{1,0:T(8,128)(2,1)S(1)} %copy-done.28, bf16[2560,1792]{1,0:T(8,128)(2,1)S(1)} %copy-done.27), kind=kOutput, calls=%fused_computation.80 | convolution fusion | flops 14092861440 | bytes 28049408 | tf_op jit(solution)/shard_map/dot_general | solution.py:25
  502.9 28.4 %multiply_convert_fusion.1 = (bf16[1536,1792]{1,0:T(8,128)(2,1)}, bf16[1536,1792]{1,0:T(8,128)(2,1)}, bf16[1536,1792]{1,0:T(8,128)(2,1)S(1)}) fusion(f32[1536,1792]{1,0:T(8,128)} %fusion.30, f32[1536,1792]{1,0:T(8,128)} %fusion.29, bf16[1536,2560]{1,0:T(8,128)(2,1)} %get-tuple-element.59, bf16[2560,1792]{1,0:T(8,128)(2,1)} %get-tuple-element.50), kind=kOutput, calls=%fused_computation.12 | convolution fusion | flops 14136901632 | bytes 55574528 | tf_op jit(solution)/shard_map/dot_general | solution.py:25
  531.3 22.6 %fusion.31 = f32[1536,2560]{1,0:T(8,128)} fusion(bf16[1536,1792]{1,0:T(8,128)(2,1)S(1)} %get-tuple-element.61, bf16[2560,1792]{1,0:T(8,128)(2,1)} %get-tuple-element.51), kind=kOutput, calls=%fused_computation.82 | convolution fusion | flops 14092861440 | bytes 30408704 | tf_op jit(solution)/shard_map/dot_general | solution.py:25
  553.9 19.3 %convolution_convert_fusion.4.grad_down = bf16[2560,1792]{1,0:T(8,128)(2,1)} fusion(bf16[1536,2560]{1,0:T(8,128)(2,1)} %get-tuple-element.52.cot_all, bf16[1536,1792]{1,0:T(8,128)(2,1)S(1)} %copy-done.35), kind=kOutput, calls=%fused_computation.10 | convolution fusion | flops 14097448960 | bytes 22544384 | tf_op jit(solution)/shard_map/dot_general | solution.py:25
  573.2 23.1 %add_convert_fusion.partial = bf16[1536,2560]{1,0:T(8,128)(2,1)} fusion(f32[1536,2560]{1,0:T(8,128)} %fusion.31, bf16[1536,1792]{1,0:T(8,128)(2,1)} %get-tuple-element.60, bf16[2560,1792]{1,0:T(8,128)(2,1)} %get-tuple-element.50), kind=kOutput, calls=%fused_computation.5 | convolution fusion | flops 14100725760 | bytes 38273024 | tf_op jit(solution)/shard_map/dot_general | solution.py:25
  596.2 131.0 %turn_back.1 = (f32[384,2560]{1,0:T(8,128)}, f32[1,2560]{1,0:T(1,128)}, f32[320,1792]{1,0:T(8,128)}, bf16[1536,2560]{1,0:T(8,128)(2,1)}, bf16[6,320,1792]{2,1,0:T(8,128)(2,1)}) custom-call(bf16[1536,2560]{1,0:T(8,128)(2,1)} %add_convert_fusion.partial, bf16[1536,2560]{1,0:T(8,128)(2,1)} %get-tuple-element.52.cot_all, ...), custom_call_target="tpu_custom_call" | custom-call | tf_op jit(solution)/shard_map/turn_back/pallas_call | solution.py:1315
  727.2 15.4 %fusion.21.grad_ref = bf16[1536,640]{1,0:T(8,128)(2,1)} fusion(s32[1536]{0:T(1024)S(1)} %copy-done.20, bf16[1536,2560]{1,0:T(8,128)(2,1)} %get-tuple-element.54, bf16[2560,640]{1,0:T(8,128)(2,1)} %get-tuple-element.45), kind=kOutput, calls=%fused_computation.42 | convolution fusion | flops 8057389056 | bytes 13113344 | tf_op jit(solution)/shard_map/dot_general | solution.py:25
  742.6 19.2 %convolution_convert_fusion.3 = bf16[1536,2560]{1,0:T(8,128)(2,1)S(1)} fusion(bf16[1536,1792]{1,0:T(8,128)(2,1)} %get-tuple-element.55, bf16[2560,1792]{1,0:T(8,128)(2,1)} %get-tuple-element.53), kind=kOutput, calls=%fused_computation.9 | convolution fusion | flops 14096793600 | bytes 22544384 | tf_op jit(solution)/shard_map/dot_general | solution.py:25
  764.1 20.1 %collective-permute-start.7 = (bf16[384,2560]{1,0:T(8,128)(2,1)}, bf16[384,2560]{1,0:T(8,128)(2,1)}, u32[]{:S(2)}, u32[]{:S(2)}) collective-permute-start(bf16[384,2560]{1,0:T(8,128)(2,1)} %get-tuple-element.127), channel_id=1, source_target_pairs={{0,4},{1,5},{2,6},{3,7},{4,0},{5,1},{6,2},{7,3},{8,12},{9,13},{10,... | collective-permute-start | bytes 5898248 | tf_op jit(solution)/shard_map/ppermute | solution.py:65
  784.3 20.9 %convolution_convert_fusion.2.grad_gate = bf16[2560,1792]{1,0:T(8,128)(2,1)} fusion(bf16[1536,2560]{1,0:T(8,128)(2,1)} %get-tuple-element.59, bf16[1536,1792]{1,0:T(8,128)(2,1)} %get-tuple-element.60), kind=kOutput, calls=%fused_computation.8 | convolution fusion | flops 14097448960 | bytes 22544384 | tf_op jit(solution)/shard_map/dot_general | solution.py:25
  805.3 19.4 %convolution_convert_fusion.1.grad_up = bf16[2560,1792]{1,0:T(8,128)(2,1)} fusion(bf16[1536,2560]{1,0:T(8,128)(2,1)} %get-tuple-element.59, bf16[1536,1792]{1,0:T(8,128)(2,1)S(1)} %bitcast.64), kind=kOutput, calls=%fused_computation.7 | convolution fusion | flops 14097448960 | bytes 22544384 | tf_op jit(solution)/shard_map/dot_general | solution.py:25
  824.7 48.0 %attend_back.1 = (bf16[1536,640]{1,0:T(8,128)(2,1)S(1)}, bf16[1536,320]{1,0:T(8,128)(2,1)S(1)}) custom-call(s32[12]{0:T(128)S(1)} %copy-done.6, bf16[1536,960]{1,0:T(8,128)(2,1)} %copy-done.8, bf16[1536,960]{1,0:T(8,128)(2,1)} %copy-done.8, s32[1,1536]{1,0:T(1,128)S(1)} %copy-done.4, s32[1536,1]{1,0:T(8,128)S(1)} %copy-done.1, ...), custom_call_target="tpu_custom_call" | custom-call | flops 120000004096 | bytes 11796480 | tf_op jit(solution)/shard_map/attend_back/pallas_call | solution.py:378
  878.2 8.0 convolution_convert_fusion.6.grad_output
  889.1 9.3 convolution_convert_fusion.5
  898.4 15.7 %fusion.2 = (bf16[2560]{0:T(1024)(128)(2,1)S(1)}, bf16[1536,2560]{1,0:T(8,128)(2,1)}) fusion(bf16[1536,2560]{1,0:T(8,128)(2,1)S(1)} %bitcast.52, f32[1536]{0:T(1024)S(1)} %copy-done.25, bf16[1536,960]{0,1:T(8,128)(2,1)} %copy-done.31, bf16[2560,1024]{1,0:T(8,128)(2,1)} %get-tuple-element.42.weight_ref), kind=kOutput, calls=%fused_computation.4 | convolution fusion | flops 7569405440 | bytes 23931904 | tf_op jit(solution)/shard_map/dot_general | solution.py:25
  914.2 19.3 %collective-permute-done.6 = bf16[384,2560]{1,0:T(8,128)(2,1)S(1)} collective-permute-done((bf16[384,2560]{1,0:T(8,128)(2,1)S(1)}, bf16[384,2560]{1,0:T(8,128)(2,1)S(1)}, u32[]{:S(2)}, u32[]{:S(2)}) %collective-permute-start.6) | collective-permute-done | bytes 1966112 | tf_op jit(solution)/shard_map/ppermute | solution.py:65
  956.0 283.2 %tail.1 = (f32[384,2560]{1,0:T(8,128)}, f32[320,1792]{1,0:T(8,128)}, f32[320,1792]{1,0:T(8,128)}, f32[320,640]{1,0:T(8,128)}, f32[320,1024]{1,0:T(8,128)}, /*ind...) custom-call(bf16[1536,2560]{1,0:T(8,128)(2,1)} %get-tuple-element.12, ...), custom_call_target="tpu_custom_call" | custom-call | tf_op jit(solution)/shard_map/tail/pallas_call | solution.py:1044
  (154 shorter events, 101.3 us)
Async XLA Ops:
  8.9 163.4 %copy-start.22 = (s32[1536]{0:T(1024)S(1)}, s32[1536]{0:T(1024)}, u32[]{:S(2)}) copy-start(s32[1536]{0:T(1024)} %param.28) | copy-start | bytes 18436
  8.9 163.4 %copy-start.23 = (s32[1536]{0:T(1024)S(1)}, s32[1536]{0:T(1024)}, u32[]{:S(2)}) copy-start(s32[1536]{0:T(1024)} %param.27) | copy-start | bytes 18436
  8.9 163.4 %copy-start.26 = (s32[1,3]{1,0:T(1,128)S(1)}, s32[1,3]{1,0:T(1,128)}, u32[]{:S(2)}) copy-start(s32[1,3]{1,0:T(1,128)} %param.26) | copy-start | bytes 40
  9.0 168.3 %copy-start.12 = (bf16[320,1792]{1,0:T(8,128)(2,1)}, bf16[320,1792]{1,0:T(8,128)(2,1)S(1)}, u32[]{:S(2)}) copy-start(bf16[320,1792]{1,0:T(8,128)(2,1)S(1)} %pad.20.up) | copy-start | bytes 3440644
  149.9 117.7 %collective-permute-start.1 = (bf16[320,1792]{1,0:T(8,128)(2,1)S(1)}, bf16[320,1792]{1,0:T(8,128)(2,1)}, u32[]{:S(2)}, u32[]{:S(2)}) collective-permute-start(bf16[320,1792]{1,0:T(8,128)(2,1)S(1)} %pad.20.up), channel_id=1, source_target_pairs={{0,2},{1,3},{2,6},{3,7},{4,0},{5,1},{6,4},{7,5},{8,10},{9,11},{10,... | collective-permute-start | bytes 3440648 | tf_op jit(solution)/shard_map/ppermute | solution.py:65
  164.4 103.2 %collective-permute-start.2 = (bf16[320,1792]{1,0:T(8,128)(2,1)S(1)}, bf16[320,1792]{1,0:T(8,128)(2,1)}, u32[]{:S(2)}, u32[]{:S(2)}) collective-permute-start(bf16[320,1792]{1,0:T(8,128)(2,1)S(1)} %pad.20.up), channel_id=1, source_target_pairs={{2,4},{3,5},{4,2},{5,3},{10,12},{11,13},{12,10},{13,11},{18,20},{1... | collective-permute-start | bytes 3440648 | tf_op jit(solution)/shard_map/ppermute | solution.py:65
  169.2 98.4 %collective-permute-start.3 = (bf16[640,1792]{1,0:T(8,128)(2,1)}, bf16[640,1792]{1,0:T(8,128)(2,1)}, u32[]{:S(2)}, u32[]{:S(2)}) collective-permute-start(bf16[640,1792]{1,0:T(8,128)(2,1)} %constant_dynamic-slice_fusion.3), channel_id=1, source_target_pairs={{0,8},{1,9},{2,10},{3,11},{4,12},{5,13},{6,14},{7,15},{8,0},{9,1},... | collective-permute-start | bytes 6881288 | tf_op jit(solution)/shard_map/ppermute | solution.py:65
  170.7 96.9 %collective-permute-start.4 = (bf16[640,1792]{1,0:T(8,128)(2,1)}, bf16[640,1792]{1,0:T(8,128)(2,1)}, u32[]{:S(2)}, u32[]{:S(2)}) collective-permute-start(bf16[640,1792]{1,0:T(8,128)(2,1)} %constant_dynamic-slice_fusion.3), channel_id=1, source_target_pairs={{0,16},{1,17},{2,18},{3,19},{4,20},{5,21},{6,22},{7,23},{8,24},{9,... | collective-permute-start | bytes 6881288 | tf_op jit(solution)/shard_map/ppermute | solution.py:65
  172.3 12.7 %collective-permute-start = (s32[3075]{0:T(1024)S(1)}, s32[3075]{0:T(1024)S(1)}, u32[]{:S(2)}, u32[]{:S(2)}) collective-permute-start(s32[3075]{0:T(1024)S(1)} %pad_add_fusion), channel_id=1, source_target_pairs={{0,4},{1,5},{2,6},{3,7},{4,0},{5,1},{6,2},{7,3},{8,12},{9,13},{10,... | collective-permute-start | bytes 36908 | tf_op jit(solution)/shard_map/ppermute | solution.py:65
  183.3 30.3 %copy-start.2 = (f32[1,2560]{1,0:T(1,128)}, f32[1,2560]{1,0:T(1,128)S(1)}, u32[]{:S(2)}) copy-start(f32[1,2560]{1,0:T(1,128)S(1)} %reshape.115.gain_ref) | copy-start | bytes 30724
  185.0 69.4 %copy-start.19 = (s32[1536]{0:T(1024)}, s32[1536]{0:T(1024)S(1)}, u32[]{:S(2)}) copy-start(s32[1536]{0:T(1024)S(1)} %slice.60) | copy-start | bytes 18436
  185.4 33.7 %copy-start.3 = (s32[1,1536]{1,0:T(1,128)}, s32[1,1536]{1,0:T(1,128)S(1)}, u32[]{:S(2)}) copy-start(s32[1,1536]{1,0:T(1,128)S(1)} %broadcast_in_dim.28.start_ref) | copy-start | bytes 18436
  185.5 33.7 %copy-start.5 = (s32[12]{0:T(128)}, s32[12]{0:T(128)S(1)}, u32[]{:S(2)}) copy-start(s32[12]{0:T(128)S(1)} %and_select_fusion.first_ref) | copy-start | bytes 148
  218.9 35.5 %copy-start.8 = (bf16[1536,960]{1,0:T(8,128)(2,1)}, bf16[1536,960]{1,0:T(8,128)(2,1)S(1)}, u32[]{:S(2)}) copy-start(bf16[1536,960]{1,0:T(8,128)(2,1)S(1)} %fusion.18.query_ref.all_ref) | copy-start | bytes 8847364
  219.2 35.2 %copy-start = (s32[1536,1]{1,0:T(8,128)}, s32[1536,1]{1,0:T(8,128)S(1)}, u32[]{:S(2)}) copy-start(s32[1536,1]{1,0:T(8,128)S(1)} %broadcast_in_dim.55.pad_ref) | copy-start | bytes 18436
  596.2 131.0 %copy-start.20 = (s32[1536]{0:T(1024)S(1)}, s32[1536]{0:T(1024)}, u32[]{:S(2)}) copy-start(s32[1536]{0:T(1024)} %copy-done.19) | copy-start | bytes 18436
  761.8 43.5 %copy-start.11 = (bf16[1536,2560]{1,0:T(8,128)(2,1)}, bf16[1536,2560]{1,0:T(8,128)(2,1)S(1)}, u32[]{:S(2)}) copy-start(bf16[1536,2560]{1,0:T(8,128)(2,1)S(1)} %convolution_convert_fusion.3) | copy-start | bytes 23592964
  764.1 150.0 %collective-permute-start.7 = (bf16[384,2560]{1,0:T(8,128)(2,1)}, bf16[384,2560]{1,0:T(8,128)(2,1)}, u32[]{:S(2)}, u32[]{:S(2)}) collective-permute-start(bf16[384,2560]{1,0:T(8,128)(2,1)} %get-tuple-element.127), channel_id=1, source_target_pairs={{0,4},{1,5},{2,6},{3,7},{4,0},{5,1},{6,2},{7,3},{8,12},{9,13},{10,... | collective-permute-start | bytes 5898248 | tf_op jit(solution)/shard_map/ppermute | solution.py:65
  784.2 102.0 %collective-permute-start.5 = (bf16[384,2560]{1,0:T(8,128)(2,1)}, bf16[384,2560]{1,0:T(8,128)(2,1)}, u32[]{:S(2)}, u32[]{:S(2)}) collective-permute-start(bf16[384,2560]{1,0:T(8,128)(2,1)} %get-tuple-element.126), channel_id=1, source_target_pairs={{0,4},{1,5},{2,6},{3,7},{4,0},{5,1},{6,2},{7,3},{8,12},{9,13},{10,... | collective-permute-start | bytes 5898248 | tf_op jit(solution)/shard_map/ppermute | solution.py:65
  824.7 48.0 %copy-start.21 = (s32[1536]{0:T(1024)S(1)}, s32[1536]{0:T(1024)}, u32[]{:S(2)}) copy-start(s32[1536]{0:T(1024)} %copy-done.19) | copy-start | bytes 18436
  889.0 44.5 %collective-permute-start.6 = (bf16[384,2560]{1,0:T(8,128)(2,1)S(1)}, bf16[384,2560]{1,0:T(8,128)(2,1)S(1)}, u32[]{:S(2)}, u32[]{:S(2)}) collective-permute-start(bf16[384,2560]{1,0:T(8,128)(2,1)S(1)} %add_convert_fusion.1), channel_id=1, source_target_pairs={{0,1},{1,0},{2,3},{3,2},{4,5},{5,4},{6,7},{7,6},{8,9},{9,8},{10,11... | collective-permute-start | bytes 5898248 | tf_op jit(solution)/shard_map/ppermute | solution.py:65
  898.4 35.1 %copy-start.9 = (f32[384,2560]{1,0:T(8,128)S(1)}, f32[384,2560]{1,0:T(8,128)}, u32[]{:S(2)}) copy-start(f32[384,2560]{1,0:T(8,128)} %get-tuple-element.48.residual_ref) | copy-start | bytes 11796484
  914.2 26.1 %copy-start.24 = (f32[1,2560]{1,0:T(1,128)S(1)}, f32[1,2560]{1,0:T(1,128)}, u32[]{:S(2)}) copy-start(f32[1,2560]{1,0:T(1,128)} %get-tuple-element.63) | copy-start | bytes 30724
  938.1 311.3 %collective-permute-start.8 = (bf16[384,2560]{1,0:T(8,128)(2,1)}, bf16[384,2560]{1,0:T(8,128)(2,1)}, u32[]{:S(2)}, u32[]{:S(2)}) collective-permute-start(bf16[384,2560]{1,0:T(8,128)(2,1)} %fusion.25), channel_id=1, source_target_pairs={{2,4},{3,5},{4,2},{5,3},{10,12},{11,13},{12,10},{13,11},{18,20},{1... | collective-permute-start | bytes 5898248 | tf_op jit(solution)/shard_map/ppermute | solution.py:65
  (27 other events, 326.3 us)

commit v3 on v2

--- a/solution.py
+++ b/solution.py
@@ -99,25 +99,28 @@
         index = (self.c ^ other) * self.low + (self.tl + step) % self.low
         return lax.dynamic_slice_in_dim(array, index * rows, rows, 0)
 
-    def scatter_rows(self, partial):
-        total = None
-        for step in list(range(1, self.low)) + [0]:
-            mine = self.quarter_rows(partial, step, 0)
-            others = self.quarter_rows(partial, step, 1)
-            pair = mine.astype(jnp.float32) + self.to_core(others).astype(jnp.float32)
-            if step:
-                pair = self.to_low(pair.astype(jnp.bfloat16), step).astype(jnp.float32)
-            total = pair if total is None else total + pair
+    def pair_rows(self, partial):
+        return [
+            self.quarter_rows(partial, step, 0).astype(jnp.float32)
+            + self.to_core(self.quarter_rows(partial, step, 1)).astype(jnp.float32)
+            for step in range(self.low)
+        ]
+
+    def sum_rows(self, pairs):
+        total = pairs[0]
+        for step in range(1, self.low):
+            total = total + self.to_low(pairs[step].astype(jnp.bfloat16), step).astype(jnp.float32)
         return total
 
 
-def project_kernel(heads, tokens_ref, gain_ref, weight_ref, cosine_ref, sine_ref, normed_ref, out_ref):
+def project_kernel(heads, tokens_ref, gain_ref, weight_ref, cosine_ref, sine_ref, normed_ref, out_ref, root_ref):
     tokens = tokens_ref[...].astype(jnp.float32)
     root = lax.rsqrt(jnp.mean(tokens * tokens, axis=-1, keepdims=True) + epsilon)
+    root_ref[...] = root
     normed = (tokens * root * gain_ref[...]).astype(jnp.bfloat16)
     normed_ref[...] = normed
     rows = jnp.dot(normed, weight_ref[...], preferred_element_type=jnp.float32)
-    cosine, sine = cosine_ref[...], sine_ref[...]
+    cosine, sine = cosine_ref[...].T, sine_ref[...].T
     pieces = []
     for head in range(heads):
         leading = rows[:, head * HEAD_DIM : head * HEAD_DIM + HALF]
@@ -138,16 +141,18 @@
             pl.BlockSpec((block, width), lambda i: (i, 0)),
             pl.BlockSpec((1, width), lambda i: (0, 0)),
             pl.BlockSpec(weight.shape, lambda i: (0, 0)),
-            pl.BlockSpec((block, HALF), lambda i: (i, 0)),
-            pl.BlockSpec((block, HALF), lambda i: (i, 0)),
+            pl.BlockSpec((HALF, block), lambda i: (0, i)),
+            pl.BlockSpec((HALF, block), lambda i: (0, i)),
         ],
         out_specs=[
             pl.BlockSpec((block, width), lambda i: (i, 0)),
             pl.BlockSpec((block, out_columns), lambda i: (i, 0)),
+            pl.BlockSpec((block, 1), lambda i: (i, 0)),
         ],
         out_shape=[
             jax.ShapeDtypeStruct((count, width), jnp.bfloat16),
             jax.ShapeDtypeStruct((count, out_columns), jnp.bfloat16),
+            jax.ShapeDtypeStruct((count, 1), jnp.float32),
         ],
         compiler_params=pltpu.CompilerParams(vmem_limit_bytes=VMEM_LIMIT),
         cost_estimate=pl.CostEstimate(
@@ -266,7 +271,7 @@
         ],
         compiler_params=pltpu.CompilerParams(vmem_limit_bytes=VMEM_LIMIT),
         cost_estimate=pl.CostEstimate(
-            flops=60 * 10**9, bytes_accessed=count * columns * 4, transcendentals=0
+            flops=50 * 10**9, bytes_accessed=count * columns, transcendentals=0
         ),
         name="attend",
     )(first, heads_all, heads_all, start_row, pad_column)
@@ -285,8 +290,8 @@
     grad_ref,
     cosine_turned_ref,
     sine_turned_ref,
-    cosine_ref,
-    sine_ref,
+    cosine_all_ref,
+    sine_all_ref,
     grad_query_ref,
     grad_rest_ref,
     key_heads,
@@ -357,11 +362,12 @@
     @pl.when(step == pl.num_programs(0) - 1)
     def _():
         rest = []
+        cosine_all, sine_all = cosine_all_ref[...].T, sine_all_ref[...].T
         for k in range(kv_heads):
             leading = grad_keys[k][:, :HALF] * scale
             trailing = grad_keys[k][:, HALF:] * scale
-            rest.append(leading * cosine_ref[...] + trailing * sine_ref[...])
-            rest.append(trailing * cosine_ref[...] - leading * sine_ref[...])
+            rest.append(leading * cosine_all + trailing * sine_all)
+            rest.append(trailing * cosine_all - leading * sine_all)
         for k in range(kv_heads):
             rest.append(grad_values[k])
         grad_rest_ref[...] = jnp.concatenate(rest, axis=1).astype(jnp.bfloat16)
@@ -390,8 +396,8 @@
                 pl.BlockSpec((block, width), lambda i, first: (i, 0)),
                 pl.BlockSpec((HALF, block), lambda i, first: (0, i)),
                 pl.BlockSpec((HALF, block), lambda i, first: (0, i)),
-                pl.BlockSpec((count, HALF), lambda i, first: (0, 0)),
-                pl.BlockSpec((count, HALF), lambda i, first: (0, 0)),
+                pl.BlockSpec((HALF, count), lambda i, first: (0, 0)),
+                pl.BlockSpec((HALF, count), lambda i, first: (0, 0)),
             ],
             out_specs=[
                 pl.BlockSpec((block, width), lambda i, first: (i, 0)),
@@ -411,7 +417,7 @@
         ],
         compiler_params=pltpu.CompilerParams(vmem_limit_bytes=VMEM_LIMIT),
         cost_estimate=pl.CostEstimate(
-            flops=120 * 10**9, bytes_accessed=count * columns * 8, transcendentals=0
+            flops=50 * 10**9, bytes_accessed=count * columns, transcendentals=0
         ),
         name="attend_back",
     )(
@@ -423,8 +429,8 @@
         log_totals,
         attended,
         grad_attended,
-        cosine.T,
-        sine.T,
+        cosine,
+        sine,
         cosine,
         sine,
     )
@@ -473,6 +479,15 @@
     def cross_peer(self):
         return self.at(self.p, 1 - self.c, 1 - self.th, self.tl)
 
+    def turn_peer(self):
+        home = self.home.astype(jnp.int32)
+        return self.at(
+            self.p,
+            home * self.c + (1 - home) * (1 - self.c),
+            home * (1 - self.th) + (1 - home) * self.th,
+            self.tl,
+        )
+
     def partner(self):
         return self.at(self.p, self.c, 1 - self.th, self.tl)
 
@@ -551,23 +566,32 @@
         self.run(lambda copy: copy.wait())
 
 
+class UnitGather:
+    def __init__(self, links, shard, unit):
+        rows = shard.shape[0]
+        mine = unit.at[pl.ds(links.c * rows, rows)]
+        self.first = links.copy(shard, mine, links.turn_peer())
+        self.second = links.copy(shard, mine, links.cross_peer(), links.away)
+        self.own = links.keep(shard, mine, links.home)
+
+    def turn(self):
+        self.first.start()
+        self.second.start()
+        self.own.start()
+
+    def settle_unit(self):
+        self.first.arrived()
+        self.second.arrived()
+        self.own.done()
+
+
 class WeightGather:
     def __init__(self, links, shard, full):
         self.links, self.shard, self.full = links, shard, full
         rows = shard.shape[0]
         self.rows = rows
         mine = full.at[pl.ds(links.dp_index * rows, rows)]
-        home_int = links.home.astype(jnp.int32)
-        self.first = links.copy(
-            shard,
-            mine,
-            links.at(
-                links.p,
-                home_int * links.c + (1 - home_int) * (1 - links.c),
-                home_int * (1 - links.th) + (1 - home_int) * links.th,
-                links.tl,
-            ),
-        )
+        self.first = links.copy(shard, mine, links.turn_peer())
         self.second = links.copy(shard, mine, links.cross_peer(), links.away)
         self.own = links.keep(shard, mine, links.home)
         unit = 2 * rows
@@ -719,6 +743,46 @@
 
 
 ADD_ROWS = 32
+
+
+def cut(columns, most):
+    half = columns // 2
+    return half if columns > most and half % 128 == 0 else columns
+
+
+def product(left, right, out, left_dim, right_dim, rows, columns, finish=None, extra=(), extra_out=()):
+    depth = left.shape[left_dim]
+    count, width = out.shape
+    rows, columns = math.gcd(count, rows), cut(width, columns)
+
+    def body(left_ref, right_ref, *refs):
+        value = times(left_ref[...], right_ref[...], left_dim, right_dim)
+        if finish is None:
+            refs[0][...] = value.astype(refs[0].dtype)
+        else:
+            finish(value, *refs)
+
+    def block(shape, index):
+        return pl.BlockSpec(shape, index)
+
+    left_spec = (
+        block((rows, depth), lambda j, i: (i, 0)) if left_dim == 1 else block((depth, rows), lambda j, i: (0, i))
+    )
+    right_spec = (
+        block((columns, depth), lambda j, i: (j, 0))
+        if right_dim == 1
+        else block((depth, columns), lambda j, i: (0, j))
+    )
+    whole = block((rows, columns), lambda j, i: (i, j))
+    extra_specs = [
+        whole if ref.shape[1] == width else block((rows, ref.shape[1]), lambda j, i: (i, 0)) for ref in extra
+    ]
+    pltpu.emit_pipeline(
+        body,
+        grid=(width // columns, count // rows),
+        in_specs=[left_spec, right_spec] + extra_specs,
+        out_specs=[whole] * (1 + len(extra_out)),
+    )(left, right, *extra, out, *extra_out)
 
 
 def row_loop(rows, body):
@@ -802,8 +866,10 @@
 
     def add_before(self):
         if not self.both:
+            self.start("direct")
             return
         self.arrived("before")
+        self.start("direct")
         for index, part in ((0, self.part(2, 0)), (1, self.part(1, 1))):
             self.load([part, self.inbox.at[index]])
 
@@ -815,6 +881,14 @@
             self.summed[index].start()
 
     def turn(self):
+        self.reduce()
+        self.send_turned()
+
+    def send_turned(self):
+        self.first.start()
+        self.second.start()
+
+    def reduce(self):
         links = self.links
         for half in range(2):
             sources = [self.part(0, half)] + [self.inbox.at[at] for at in self.arrivals[half]]
@@ -830,8 +904,6 @@
                 row_loop(self.rows, body)
             else:
                 self.fold(sources, kept)
-        self.first.start()
-        self.second.start()
 
     def fold(self, sources, kept):
         rows = self.rows
@@ -909,34 +981,36 @@
     tensor_count,
     gain_column,
     partial,
-    grad_gate,
+    tokens_all,
     grad_up,
-    grad_output,
-    grad_first,
-    own_ref,
+    grad_rows,
+    attended,
+    normed,
+    grad_heads,
+    gain_parts,
     grad_residual_ref,
     gain_ref,
     input_ref,
-    gate_ref,
     up_ref,
     output_ref,
     first_ref,
-    gate_in,
     up_in,
     output_in,
     first_in,
+    grad_output,
+    grad_first,
     *scratch,
 ):
-    gate_work, up_work, output_work, first_work = (scratch[3 * i : 3 * i + 3] for i in range(4))
-    stage, leaving, crossed, mine, others, sums, arrivals, gains_out, gains_in, total = scratch[12:22]
-    links = Links(dp_count, tensor_count, *scratch[22:])
+    up_work, output_work, first_work = (scratch[3 * i : 3 * i + 3] for i in range(3))
+    stage, own_ref, leaving, crossed, mine, others, sums, arrivals, gains_out, gains_in, total = scratch[9:20]
+    links = Links(dp_count, tensor_count, *scratch[20:])
     links.all_low = True
     rows = own_ref.shape[0]
+    load_own = links.keep(tokens_all.at[pl.ds(links.quarter * rows, rows)], own_ref)
     scatter = RowScatter(links, partial, mine, others, sums, arrivals, rows)
     crossing = links.copy(leaving, crossed, links.cross_peer(), links.away)
     weights = []
     for grad, result, inbox, work in (
-        (grad_gate, gate_ref, gate_in, gate_work),
         (grad_up, up_ref, up_in, up_work),
         (grad_output, output_ref, output_in, output_work),
         (grad_first, first_ref, first_in, first_work),
@@ -945,7 +1019,7 @@
         made = WeightScatter(links, grad, result, inbox, turned, added, turning, stage)
         made.total = None if made.both else total.at[pl.ds(0, made.rows), pl.ds(0, grad.shape[1])]
         weights.append(made)
-    gate, up, output, first = weights
+    up, output, first = weights
     gain_sends = []
     for step in range(1, tensor_count):
         other = (links.tensor_index + step) % tensor_count
@@ -954,11 +1028,20 @@
         )
 
     links.enter()
-    gate.start("before")
     scatter.start()
-    gate.start("direct")
+    load_own.start()
+    up.start("before")
     scatter.send_sums()
-    gate.add_before()
+    load_own.done()
+
+    def finish(value, parts_ref, out_ref):
+        columns = value.shape[1]
+        out_ref[:, : columns - 128] = value[:, : columns - 128].astype(jnp.bfloat16)
+        out_ref[:, columns - 128 :] = (value[:, columns - 128 :] + parts_ref[...]).astype(jnp.bfloat16)
+
+    product(normed, grad_heads, grad_first, 0, 0, 512, 1024, finish, (gain_parts,))
+    up.add_before()
+    product(grad_rows, attended, grad_output, 0, 0, 512, 1024)
 
     def use(span, grad_normed):
         own = own_ref[span].astype(jnp.float32)
@@ -971,27 +1054,18 @@
         input_ref[span] = grad
         leaving[span] = grad.astype(jnp.bfloat16)
 
-    gate.arrived("direct")
-    up.start("before")
     scatter.collect(use)
     crossing.start()
-    gate.arrived("summed")
-    up.start("direct")
-    gate.turn()
-    up.add_before()
     up.arrived("direct")
-    output.start("before")
-    output.start("direct")
     up.arrived("summed")
     first.start("before")
     up.turn()
+    first.add_before()
+    output.start("before")
+    first.arrived("direct")
+    first.arrived("summed")
+    first.turn()
     output.add_before()
-    gate.finish()
-    output.arrived("direct")
-    first.start("direct")
-    first.add_before()
-    output.arrived("summed")
-    output.turn()
     crossing.arrived()
 
     @pl.when(links.away)
@@ -1001,16 +1075,16 @@
 
         row_loop(rows, body)
 
-    first.arrived("direct")
-    first.arrived("summed")
-    first.turn()
+    output.arrived("direct")
+    output.arrived("summed")
+    output.turn()
     up.finish()
-    output.finish()
     first.finish()
     width = first_ref.shape[1]
     gains_out[...] = first_ref[:, width - 128 :]
     for item in gain_sends:
         item.start()
+    output.finish()
     for item in gain_sends:
         item.arrived()
     summed = gains_out[...]
@@ -1021,42 +1095,70 @@
     links.leave()
 
 
-def tail(dp_count, tensor_count, gain_column, partial, grads, own, grad_residual, gain):
-    rows, width = own.shape
+def tail(
+    dp_count,
+    tensor_count,
+    gain_column,
+    partial,
+    tokens_all,
+    grad_up,
+    grad_rows,
+    attended,
+    normed,
+    grad_heads,
+    gain_parts,
+    grad_residual,
+    gain,
+):
+    rows, width = grad_residual.shape
     low, chips = tensor_count // 2, dp_count // 2
-    shapes = [scatter_shapes(chips, grad) for grad in grads]
+    features = grad_up.shape[0]
+    partials = [
+        grad_up,
+        jax.ShapeDtypeStruct((features, attended.shape[1]), jnp.bfloat16),
+        jax.ShapeDtypeStruct((features, grad_heads.shape[1]), jnp.bfloat16),
+    ]
+    shapes = [scatter_shapes(chips, grad) for grad in partials]
     widest = max(columns for _, columns in shapes)
     most = shapes[0][0]
     scratch = []
     for block, columns in shapes:
         scratch += weight_scatter_scratch(chips, block, columns)
-    scratch += [
-        pltpu.VMEM((3, most, widest), jnp.bfloat16),
-        pltpu.VMEM((rows, width), jnp.bfloat16),
-        pltpu.VMEM((rows, width), jnp.bfloat16),
-    ]
+    scratch += [pltpu.VMEM((3, most, widest), jnp.bfloat16)]
+    scratch += [pltpu.VMEM((rows, width), jnp.bfloat16)] * 3
     scratch += scatter_scratch(low, rows, width)
     scratch += [
         pltpu.VMEM((most, 128), jnp.float32),
         pltpu.VMEM((tensor_count - 1, most, 128), jnp.float32),
         pltpu.VMEM((most, widest) if chips != 4 else (8, 128), jnp.float32),
     ]
-    results = pl.pallas_call(
+    return pl.pallas_call(
         functools.partial(tail_kernel, dp_count, tensor_count, gain_column),
         out_shape=[jax.ShapeDtypeStruct((rows, width), jnp.float32)]
         + [jax.ShapeDtypeStruct(shape, jnp.float32) for shape in shapes]
-        + [inbox_shape(chips, *shape) for shape in shapes],
-        in_specs=anywhere(5) + in_vmem(3),
-        out_specs=in_vmem(5) + anywhere(4),
+        + [inbox_shape(chips, *shape) for shape in shapes]
+        + partials[1:],
+        in_specs=anywhere(8) + in_vmem(2),
+        out_specs=in_vmem(4) + anywhere(5),
         scratch_shapes=scratch + semaphores(96, 24),
         compiler_params=link_params(3),
         name="tail",
-    )(partial, *grads, own, grad_residual, gain)
-    return results[:5]
+    )(
+        partial,
+        tokens_all,
+        grad_up,
+        grad_rows,
+        attended,
+        normed,
+        grad_heads,
+        gain_parts,
+        grad_residual,
+        gain,
+    )[:4]
 
 
 def gather_first_kernel(
-    dp_count, tensor_count, tokens, first, output, gate, tokens_all, first_full, output_full, gate_full, *sems
+    dp_count, tensor_count, tokens, first, output, gate, tokens_all, first_full, output_full, gate_unit, *sems
 ):
     links = Links(dp_count, tensor_count, *sems)
     rows = tokens.shape[0]
@@ -1066,8 +1168,9 @@
     gather_tokens = RowGather(links, tokens_all, rows)
     weights = [
         WeightGather(links, shard, full)
-        for shard, full in ((first, first_full), (output, output_full), (gate, gate_full))
+        for shard, full in ((first, first_full), (output, output_full))
     ]
+    weights.append(UnitGather(links, gate, gate_unit))
     links.enter()
     weights[0].turn()
     crossing.start()
@@ -1095,7 +1198,6 @@
     gather_tokens.finish()
     weights[1].finish()
     weights[2].settle_unit()
-    links.drop(weights[2].direct + weights[2].forward)
     links.leave()
 
 
@@ -1109,7 +1211,7 @@
             full(tokens, tensor_count),
             full(first, dp_count),
             full(output, dp_count),
-            full(gate, dp_count),
+            full(gate, 2),
         ],
         in_specs=in_vmem(4),
         out_specs=anywhere(4),
@@ -1130,13 +1232,14 @@
     up_turned,
     up_crossed,
     down,
-    gate_part,
+    gate_unit,
     *rest,
 ):
     gate_units, rest = rest[:moved_units], rest[moved_units:]
     gain_ref, residual_ref, normed_all, cot_all, up_full, down_full, gate_full = rest[:7]
-    own, normed, mine, others, sums, arrivals = rest[7:13]
-    links = Links(dp_count, tensor_count, *rest[13:])
+    gate_values, up_values, hidden = rest[7:10]
+    own, normed, mine, others, sums, arrivals = rest[10:16]
+    links = Links(dp_count, tensor_count, *rest[16:])
     rows = cot.shape[0]
     scatter = RowScatter(links, partial, mine, others, sums, arrivals, rows)
     gather_normed = RowGather(links, normed_all, rows)
@@ -1156,7 +1259,7 @@
     ]
     gate_placements = [
         links.keep(unit, gate_full.at[pl.ds(links.chip(step) * 2 * shard, 2 * shard)])
-        for step, unit in zip(links.chip_steps(), gate_units)
+        for step, unit in zip((0,) + links.chip_steps(), (gate_unit,) + tuple(gate_units))
     ]
     cot_crossing = links.copy(cot, cot_all.at[pl.ds(links.tensor_index * rows, rows)], links.cross_peer(), links.away)
     cot_staying = links.keep(cot, cot_all.at[quarter], links.home)
@@ -1200,16 +1303,24 @@
     cot_crossing.arrived()
     gather_cot.start()
     up_gather.finish()
+    gather_normed.finish()
+    product(normed_all, gate_full, gate_values, 1, 0, 512, 1024)
     down_gather.pass_on()
-    gather_normed.finish()
     gather_cot.pass_on()
+
+    def finish(up, gate_ref, up_ref, hidden_ref):
+        gate = gate_ref[...]
+        up_ref[...] = up
+        hidden_ref[...] = (gate * jax.nn.sigmoid(gate) * up).astype(jnp.bfloat16)
+
+    product(normed_all, up_full, up_values, 1, 0, 256, 1024, finish, (gate_values,), (hidden,))
     down_gather.finish()
     gather_cot.finish()
     links.leave()
 
 
 def middle(
-    dp_count, tensor_count, partial, tokens_all, cot, up, up_turned, up_crossed, down, gate_part, gate_units, gain
+    dp_count, tensor_count, partial, tokens_all, cot, up, up_turned, up_crossed, down, gate_unit, gate_units, gain
 ):
     rows, width = cot.shape
     low = tensor_count // 2
@@ -1225,17 +1336,19 @@
             full(cot, tensor_count),
             full(up, dp_count),
             full(down, dp_count),
-            jax.ShapeDtypeStruct(gate_part.shape, gate_part.dtype),
+            full(gate_unit, dp_count // 2),
+            jax.ShapeDtypeStruct((rows * tensor_count, up.shape[1]), jnp.float32),
+            jax.ShapeDtypeStruct((rows * tensor_count, up.shape[1]), jnp.float32),
+            jax.ShapeDtypeStruct((rows * tensor_count, up.shape[1]), jnp.bfloat16),
         ],
-        in_specs=anywhere(2) + in_vmem(5) + anywhere(1) + in_vmem(len(gate_units) + 1),
-        out_specs=in_vmem(1) + anywhere(5),
+        in_specs=anywhere(2) + in_vmem(len(gate_units) + 7),
+        out_specs=in_vmem(1) + anywhere(8),
         scratch_shapes=[pltpu.VMEM((rows, width), jnp.bfloat16)] * 2
         + scatter_scratch(low, rows, width)
         + semaphores(64, 24),
-        input_output_aliases={7: 5},
         compiler_params=link_params(1),
         name="middle",
-    )(partial, tokens_all, cot, up, up_turned, up_crossed, down, gate_part, *gate_units, gain)
+    )(partial, tokens_all, cot, up, up_turned, up_crossed, down, gate_unit, *gate_units, gain)
 
 
 def turn_back_kernel(
@@ -1244,18 +1357,30 @@
     partial,
     cot_all,
     grad_down,
+    normed_ffn,
+    gate_signal,
+    up_signal,
+    hidden,
+    down_full,
     residual_ref,
     gain_ref,
     grad_residual_ref,
     gain_part_ref,
     down_ref,
+    gate_ref,
+    gate_turning,
     grad_rows,
     down_in,
+    gate_in,
+    grad_gate,
+    grad_up,
+    down_part,
     own,
     low_grad,
     turned,
     added,
     turning,
+    gate_added,
     stage,
     total_ref,
     mine,
@@ -1267,7 +1392,9 @@
     links = Links(dp_count, tensor_count, *sems)
     rows = residual_ref.shape[0]
     down = WeightScatter(links, grad_down, down_ref, down_in, turned, added, turning, stage)
-    down.total = total_ref
+    gate = WeightScatter(links, grad_gate, gate_ref, gate_in, turned, gate_added, gate_turning, stage)
+    down.total = gate.total = total_ref
+    links.drop([gate.first, gate.second])
     scatter = RowScatter(links, partial, mine, others, sums, arrivals, rows)
     gather = RowGather(links, grad_rows, rows)
     quarter = pl.ds(links.quarter * rows, rows)
@@ -1277,9 +1404,9 @@
     scatter.start()
     load.start()
     down.start("before")
-    down.start("direct")
     scatter.send_sums()
     load.done()
+    product(normed_ffn, gate_signal, grad_gate, 0, 0, 512, 1024)
     down.add_before()
     gain_part_ref[...] = jnp.zeros_like(gain_part_ref)
 
@@ -1299,16 +1426,37 @@
     store.start()
     store.done()
     gather.start()
+    gate.start("before")
     down.arrived("direct")
     down.arrived("summed")
-    down.turn()
+    down.reduce()
+    down.send_turned()
+    gate.add_before()
+    product(normed_ffn, up_signal, grad_up, 0, 0, 512, 1024)
     gather.pass_on()
+    product(hidden, down_full, down_part, 1, 1, 512, 1024)
+    gate.arrived("direct")
+    gate.arrived("summed")
     down.finish()
     gather.finish()
+    gate.reduce()
     links.leave()
 
 
-def turn_back(dp_count, tensor_count, partial, cot_all, grad_down, residual, gain):
+def turn_back(
+    dp_count,
+    tensor_count,
+    partial,
+    cot_all,
+    grad_down,
+    normed_ffn,
+    gate_signal,
+    up_signal,
+    hidden,
+    down_full,
+    residual,
+    gain,
+):
     rows, width = residual.shape
     low, chips = tensor_count // 2, dp_count // 2
     block, columns = scatter_shapes(chips, grad_down)
@@ -1318,22 +1466,29 @@
             jax.ShapeDtypeStruct((rows, width), jnp.float32),
             jax.ShapeDtypeStruct((1, width), jnp.float32),
             jax.ShapeDtypeStruct((block, columns), jnp.float32),
+            jax.ShapeDtypeStruct((block, columns), jnp.float32),
+            jax.ShapeDtypeStruct((2, block, columns), jnp.bfloat16),
             jax.ShapeDtypeStruct((rows * tensor_count, width), jnp.bfloat16),
             inbox_shape(chips, block, columns),
+            inbox_shape(chips, block, columns),
+            jax.ShapeDtypeStruct(grad_down.shape, jnp.bfloat16),
+            jax.ShapeDtypeStruct(grad_down.shape, jnp.bfloat16),
+            jax.ShapeDtypeStruct((rows * tensor_count, width), jnp.bfloat16),
         ],
-        in_specs=anywhere(3) + in_vmem(2),
-        out_specs=in_vmem(3) + anywhere(2),
+        in_specs=anywhere(8) + in_vmem(2),
+        out_specs=in_vmem(5) + anywhere(6),
         scratch_shapes=[pltpu.VMEM((rows, width), jnp.bfloat16)] * 2
         + weight_scatter_scratch(chips, block, columns)
         + [
+            pltpu.VMEM((2, block, columns), jnp.bfloat16),
             pltpu.VMEM((3, block, columns), jnp.bfloat16),
             pltpu.VMEM((block, columns) if chips != 4 else (8, 128), jnp.float32),
         ]
         + scatter_scratch(low, rows, width)
-        + semaphores(48, 16),
+        + semaphores(64, 24),
         compiler_params=link_params(2),
         name="turn_back",
-    )(partial, cot_all, grad_down, residual, gain)[:4]
+    )(partial, cot_all, grad_down, normed_ffn, gate_signal, up_signal, hidden, down_full, residual, gain)
 
 
 def starts_of(positions, length_row):
@@ -1346,7 +1501,7 @@
     frequency = jnp.exp(
         jnp.arange(HALF, dtype=jnp.float32) * (-2.0 * math.log(rope_base) / HEAD_DIM)
     )
-    angles = positions.astype(jnp.float32)[:, None] * frequency[None, :]
+    angles = positions.astype(jnp.float32)[None, :] * frequency[:, None]
     return (jnp.cos(angles), jnp.sin(angles))
 
 
@@ -1388,7 +1543,7 @@
     gate_shard = wide(gate_weight, hidden_padded)
     up_shard = wide(up_weight, hidden_padded)
     down_shard = wide(down_weight.T, hidden_padded)
-    tokens_all, first_weight, output_turned, gate_part = gather_first(
+    tokens_all, first_weight, output_turned, gate_unit = gather_first(
         dp_count,
         tensor_count,
         tokens,
@@ -1406,8 +1561,6 @@
     late_up = after(up_shard, tokens_all)
     up_turned = place.home_turn(late_up)
     up_crossed = place.cross(late_up)
-    unit = gate_part.shape[0] // place.chips
-    gate_unit = lax.dynamic_slice_in_dim(gate_part, place.p * unit, unit, 0)
     steps = (1, 2) if place.chips == 4 else tuple(range(1, place.chips))
     gate_units = [place.to_chip(gate_unit, step) for step in steps]
 
@@ -1428,7 +1581,7 @@
 
     attention_scale = first_weight[:, head_columns].astype(jnp.float32)[None, :]
     feedforward_scale = first_weight[:, head_columns + 1].astype(jnp.float32)[None, :]
-    normed, heads_stored = project(
+    normed, heads_stored, token_roots = project(
         tokens_all,
         attention_scale,
         first_weight,
@@ -1441,7 +1594,7 @@
     attended, log_totals = attend(first_blocks, heads_all, start_row, pad_column, kv_heads, group)
     attended_stored = contract(to_storage, attended, 1, 0, jnp.bfloat16)
 
-    residual, normed_ffn, cot_all, up_full, down_turned, gate_full = middle(
+    residual, normed_ffn, cot_all, up_full, down_turned, gate_full, gate_values, up_values, hidden = middle(
         dp_count,
         tensor_count,
         contract(attended_stored, output_turned, 1, 1, jnp.bfloat16),
@@ -1451,14 +1604,11 @@
         up_turned,
         up_crossed,
         down_shard,
-        gate_part,
+        gate_unit,
         gate_units,
         feedforward_scale,
     )
-    gate_values = contract(normed_ffn, gate_full, 1, 0)
-    up_values = contract(normed_ffn, up_full, 1, 0)
     sigmoid = jax.nn.sigmoid(gate_values)
-    hidden = (gate_values * sigmoid * up_values).astype(jnp.bfloat16)
 
     def leave(own):
         arrived = place.cross(own.astype(jnp.bfloat16)).astype(jnp.float32)
@@ -1472,23 +1622,29 @@
     grad_part = (contract(grad_gate, gate_full, 1, 1) + contract(grad_up, up_full, 1, 1)).astype(
         jnp.bfloat16
     )
-    down_part_grad = contract(cot_all, hidden, 0, 0, jnp.bfloat16)
-    grad_residual, feedforward_part, down_grad, grad_rows = turn_back(
-        dp_count, tensor_count, grad_part, cot_all, down_part_grad, residual, feedforward_scale
-    )
-    late_hidden = after(hidden, grad_rows)
-    down_part = contract(late_hidden, down_turned, 1, 1, jnp.bfloat16)
-
-    layer_own = residual + place.scatter_rows(down_part)
-    layer_output = leave(layer_own)
+    turned_back = turn_back(
+        dp_count,
+        tensor_count,
+        grad_part,
+        cot_all,
+        contract(cot_all, hidden, 0, 0, jnp.bfloat16),
+        normed_ffn,
+        grad_gate,
+        grad_up,
+        hidden,
+        down_turned,
+        residual,
+        feedforward_scale,
+    )
+    grad_residual, feedforward_part, down_grad, gate_grad, gate_turning, grad_rows = turned_back[:6]
+    up_part, down_part = turned_back[9:]
+    gate_turned = place.away_turn(gate_turning[0])
+    gate_crossed = place.cross(gate_turning[1])
+
+    pairs = place.pair_rows(down_part)
     grad_attended = contract(grad_rows, output_turned, 1, 0, jnp.bfloat16)
     grad_attended = contract(to_sequence, grad_attended, 1, 0, jnp.bfloat16)
-    late_rows, late_gate, late_up_grad = lax.optimization_barrier((normed_ffn, grad_gate, grad_up, grad_rows))[:3]
-    grads = [
-        contract(late_rows, late_gate, 0, 0, jnp.bfloat16),
-        contract(late_rows, late_up_grad, 0, 0, jnp.bfloat16),
-        wide(contract(grad_rows, attended_stored, 0, 0, jnp.bfloat16), output_padded),
-    ]
+    grad_attended = after(grad_attended, *pairs)
     grad_query, grad_rest = attend_back(
         first_blocks,
         heads_all,
@@ -1502,32 +1658,34 @@
         kv_heads,
         group,
     )
+    spare = jnp.zeros((count, first_padded - head_columns), jnp.bfloat16)
     grad_heads = contract(
-        to_storage, jnp.concatenate([grad_query, grad_rest], axis=1), 1, 0, jnp.bfloat16
-    )
-    grad_normed_part = contract(grad_heads, first_weight[:, :head_columns], 1, 1)
+        to_storage, jnp.concatenate([grad_query, grad_rest, spare], axis=1), 1, 0, jnp.bfloat16
+    )
+    grad_normed_part = contract(grad_heads, first_weight, 1, 1)
     tokens_wide = tokens_all.astype(jnp.float32)
-    attention_part = jnp.sum(grad_normed_part * (tokens_wide * inverse_root(tokens_wide)), axis=0)
-    grads.append(
-        wide(
-            jnp.concatenate(
-                [
-                    contract(normed, grad_heads, 0, 0, jnp.bfloat16),
-                    attention_part.astype(jnp.bfloat16)[:, None],
-                    feedforward_part[0].astype(jnp.bfloat16)[:, None],
-                ],
-                axis=1,
-            ),
-            first_padded,
-        )
-    )
-    input_grad, gate_grad, up_grad, output_grad, first_grad = tail(
+    attention_part = jnp.sum(grad_normed_part * (tokens_wide * token_roots), axis=0)
+    layer_own = after(residual, grad_query) + place.sum_rows(pairs)
+    layer_output = leave(layer_own)
+    gate_turned, gate_crossed = lax.optimization_barrier((gate_turned, gate_crossed, grad_query))[:2]
+    gate_grad = jnp.where(place.home, gate_grad, gate_crossed.astype(jnp.float32)) + gate_turned.astype(
+        jnp.float32
+    )
+    gain_parts = jnp.stack([attention_part, feedforward_part[0]], axis=1)
+    before = head_columns - (first_padded - 128)
+    gain_parts = jnp.pad(gain_parts, ((0, 0), (before, 126 - before)))
+    input_grad, up_grad, output_grad, first_grad = tail(
         dp_count,
         tensor_count,
         head_columns,
-        grad_normed_part.astype(jnp.bfloat16),
-        grads,
-        place.quarter_rows(tokens_all, 0, 0),
+        after(grad_normed_part.astype(jnp.bfloat16), layer_own),
+        tokens_all,
+        up_part,
+        grad_rows,
+        wide(attended_stored, output_padded),
+        normed,
+        grad_heads,
+        gain_parts,
         grad_residual,
         attention_scale,
     )

time: 1280 us -> 1130 us (0.88); the launches traced: 1260 us -> 1130 us
  matrix products: 263 us -> 137 us
  Pallas kernels: 857 us -> 884 us
  starting transfers between devices: 41.6 us -> 26.4 us
  waiting for transfers between devices: 19.3 us -> 5.88 us
    dot_general x17 -> x10, matrix products: 263 us -> 137 us  [contract(): lax.dot_general(left, right, (((left_dim,), (right_dim,)), ((), ())), pre...]
    pallas_call x1, Pallas kernels: 283 us -> 224 us  [tail(): pl.pallas_call(functools.partial(tail_kernel, dp_count, tensor_count, gai...]
    pallas_call x1, Pallas kernels: 131 us -> 187 us  [turn_back(): pl.pallas_call(functools.partial(turn_back_kernel, dp_count, tensor_count...]
    ppermute x9 -> x11, starting transfers between devices: 41.6 us -> 26.4 us  [move(): return lax.ppermute(array, AXES, pairs)]
    ppermute x9 -> x11, waiting for transfers between devices: 19.3 us -> 5.88 us  [move(): return lax.ppermute(array, AXES, pairs)]
  transfers between devices with their start and end apart: 9 -> 11, of which waited for: 1 -> 2; matrix products, arithmetic and copies ran while one was open for 12% -> 8% of each run, Pallas kernels for 31% -> 31%
where the time goes in v3:
time: 1130 us
  Pallas kernels  884 us (78%)
  matrix products  137 us (12%)
  other arithmetic  42.9 us (4%)
  local copies, waits for them, and re-layouts  32.2 us (3%)
  starting transfers between devices  26.4 us (2%)
    pallas_call x1, Pallas kernels, tail(): pl.pallas_call(functools.partial(tail_kernel, dp_count, tensor_count, gai...  224 us
    pallas_call x1, Pallas kernels, middle(): pl.pallas_call(functools.partial(middle_kernel, dp_count, tensor_count, l...  209 us
    pallas_call x1, Pallas kernels, turn_back(): pl.pallas_call(functools.partial(turn_back_kernel, dp_count, tensor_count...  187 us
    pallas_call x1, Pallas kernels, gather_first(): pl.pallas_call(functools.partial(gather_first_kernel, dp_count, tensor_co...  141 us
    dot_general x10, matrix products, contract(): lax.dot_general(left, right, (((left_dim,), (right_dim,)), ((), ())), pre...  137 us
    pallas_call x1, Pallas kernels, attend_back(): pl.pallas_call(functools.partial(attend_back_kernel, kv_heads, group), gr...  57.7 us
    pallas_call x1, Pallas kernels, attend(): pl.pallas_call(functools.partial(attend_kernel, kv_heads, group), grid_sp...  43.6 us
    ppermute x11, starting transfers between devices, move(): return lax.ppermute(array, AXES, pairs)  26.4 us
  transfers between devices with their start and end apart: 11, of which 2 were waited for; matrix products, arithmetic and copies ran while one was open for 8% of the time, Pallas kernels for 31%

profile of v3, /device:TPU:0, one launch (start us, length us, event | category | flops | bytes accessed | tf_op | source)
XLA Modules:
  0.0 1130.0 jit_solution(677388093341656582)
XLA Ops:
  9.0 140.5 %gather_first.1 = (bf16[1536,2560]{1,0:T(8,128)(2,1)}, bf16[2560,1024]{1,0:T(8,128)(2,1)}, bf16[2560,640]{1,0:T(8,128)(2,1)}, bf16[640,1792]{1,0:T(8,128)(2,1)}) custom-call(bf16[384,2560]{1,0:T(8,128)(2,1)} %tokens.1, bf16[320,1024]{1,0:T(8,128)(2,1)} %pad.18.first, bf16[320,640]{1,0:T(8,128)(2,1)} %bitcast.45, bf16[320,1792]{1,0:T(8,128)(2,1)} %pad.19.gate), custom_call_target="tpu_custom_call" | custom-call | tf_op jit(solution)/shard_map/gather_first/pallas_call | solution.py:1208
  151.2 14.7 %collective-permute-start.1 = (bf16[320,1792]{1,0:T(8,128)(2,1)S(1)}, bf16[320,1792]{1,0:T(8,128)(2,1)}, u32[]{:S(2)}, u32[]{:S(2)}) collective-permute-start(bf16[320,1792]{1,0:T(8,128)(2,1)S(1)} %pad.20.up), channel_id=1, source_target_pairs={{0,2},{1,3},{2,6},{3,7},{4,0},{5,1},{6,4},{7,5},{8,10},{9,11},{10,... | collective-permute-start | bytes 3440648 | tf_op jit(solution)/shard_map/ppermute | solution.py:65
  175.7 21.6 %project.1 = (bf16[1536,2560]{1,0:T(8,128)(2,1)}, bf16[1536,960]{1,0:T(8,128)(2,1)S(1)}, f32[1536,1]{1,0:T(8,128)S(1)}) custom-call(bf16[1536,2560]{1,0:T(8,128)(2,1)} %get-tuple-element.49.tokens_ref.tokens_all, f32[1,2560]{1,0:T(1,128)S(1)} %reshape.88.gain_ref, bf16[2560,1024]{1,0:T(8,128)(2,1)} %get-tuple-element.50.weight_ref, ...), custom_call_target="tpu_custom_call" | custom-call | flops 8053063680 | bytes 20971520 | tf_op jit(solution)/shard_map/project/pallas_call | solution.py:137
  197.3 5.3 fusion.9.query_ref.all_ref
  202.6 43.6 %attend.1 = (bf16[1536,640]{1,0:T(8,128)(2,1)S(1)}, f32[8,1536]{1,0:T(8,128)S(1)}) custom-call(s32[12]{0:T(128)S(1)} %and_select_fusion.first_ref, bf16[1536,960]{1,0:T(8,128)(2,1)S(1)} %fusion.9.query_ref.all_ref, bf16[1536,960]{1,0:T(8,128)(2,1)S(1)} %fusion.9.query_ref.all_ref, s32[1,1536]{1,0:T(1,128)S(1)} %broadcast_in_dim.51.start_ref, ...), custom_call_target="tpu_custom_call" | custom-call | flops 49999998976 | bytes 1474560 | tf_op jit(solution)/shard_map/attend/pallas_call | solution.py:248
  246.3 4.3 fusion.10.attended
  250.6 9.0 convolution_convert_fusion.partial
  259.7 209.0 %middle.1 = (f32[384,2560]{1,0:T(8,128)}, bf16[1536,2560]{1,0:T(8,128)(2,1)}, bf16[1536,2560]{1,0:T(8,128)(2,1)}, bf16[2560,1792]{1,0:T(8,128)(2,1)}, bf16[2560,...) custom-call(bf16[1536,2560]{1,0:T(8,128)(2,1)} %convolution_convert_, ...), custom_call_target="tpu_custom_call" | custom-call | tf_op jit(solution)/shard_map/middle/pallas_call | solution.py:1331
  468.7 20.9 %convolution_convert_fusion.1.grad_down = bf16[2560,1792]{1,0:T(8,128)(2,1)} fusion(bf16[1536,2560]{1,0:T(8,128)(2,1)} %get-tuple-element.58.cot_all, bf16[1536,1792]{1,0:T(8,128)(2,1)} %get-tuple-element.64.hidden), kind=kOutput, calls=%fused_computation.3 | convolution fusion | flops 14097448960 | bytes 22544384 | tf_op jit(solution)/shard_map/dot_general | solution.py:25
  489.7 16.9 %fusion.22 = f32[1536,1792]{1,0:T(8,128)} fusion(bf16[1536,2560]{1,0:T(8,128)(2,1)S(1)} %copy-done.13, bf16[2560,1792]{1,0:T(8,128)(2,1)S(1)} %copy-done.12), kind=kOutput, calls=%fused_computation.64 | convolution fusion | flops 14092861440 | bytes 28049408 | tf_op jit(solution)/shard_map/dot_general | solution.py:25
  506.6 15.0 %multiply_convert_fusion.1 = (bf16[1536,1792]{1,0:T(8,128)(2,1)}, bf16[1536,1792]{1,0:T(8,128)(2,1)S(1)}) fusion(f32[1536,1792]{1,0:T(8,128)} %get-tuple-element.61, f32[1536,1792]{1,0:T(8,128)} %fusion.22, f32[1536,1792]{1,0:T(8,128)} %get-tuple-element.60), kind=kLoop, calls=%fused_computation.5 | loop fusion | flops 35782656 | bytes 44040192 | tf_op jit(solution)/shard_map/convert_element_type | solution.py:1618
  521.6 22.6 %fusion.23 = f32[1536,2560]{1,0:T(8,128)} fusion(bf16[1536,1792]{1,0:T(8,128)(2,1)S(1)} %get-tuple-element.140.up_signal, bf16[2560,1792]{1,0:T(8,128)(2,1)} %get-tuple-element.63), kind=kOutput, calls=%fused_computation.65 | convolution fusion | flops 14092861440 | bytes 30408704 | tf_op jit(solution)/shard_map/dot_general | solution.py:25
  544.1 23.3 %add_convert_fusion.partial = bf16[1536,2560]{1,0:T(8,128)(2,1)} fusion(f32[1536,2560]{1,0:T(8,128)} %fusion.23, bf16[1536,1792]{1,0:T(8,128)(2,1)} %get-tuple-element.139.gate_signal, bf16[2560,1792]{1,0:T(8,128)(2,1)} %get-tuple-element.62), kind=kOutput, calls=%fused_computation.1 | convolution fusion | flops 14100725760 | bytes 38273024 | tf_op jit(solution)/shard_map/dot_general | solution.py:25
  567.4 187.1 %turn_back.1 = (f32[384,2560]{1,0:T(8,128)}, f32[1,2560]{1,0:T(1,128)}, f32[320,1792]{1,0:T(8,128)}, f32[320,1792]{1,0:T(8,128)}, bf16[2,320,1792]{2,1,0:T(8,128...) custom-call(bf16[1536,2560]{1,0:T(8,128)(2,1)} %add_convert_fusion.p, ...), custom_call_target="tpu_custom_call" | custom-call | tf_op jit(solution)/shard_map/turn_back/pallas_call | solution.py:1463
  761.6 4.6 convert_add_fusion
  770.7 15.5 %fusion.11.grad_ref = bf16[1536,640]{1,0:T(8,128)(2,1)} fusion(s32[1536]{0:T(1024)S(1)} %copy-done.26, bf16[1536,2560]{1,0:T(8,128)(2,1)} %get-tuple-element.66.grad_rows, bf16[2560,640]{1,0:T(8,128)(2,1)} %get-tuple-element.53), kind=kOutput, calls=%fused_computation.25 | convolution fusion | flops 8057389056 | bytes 13113344 | tf_op jit(solution)/shard_map/dot_general | solution.py:25
  788.3 4.6 convert_add_fusion.1
  793.0 57.7 %attend_back.1 = (bf16[1536,640]{1,0:T(8,128)(2,1)S(1)}, bf16[1536,320]{1,0:T(8,128)(2,1)S(1)}) custom-call(s32[12]{0:T(128)S(1)} %copy-done.6, bf16[1536,960]{1,0:T(8,128)(2,1)} %copy-done.8, bf16[1536,960]{1,0:T(8,128)(2,1)} %copy-done.8, s32[1,1536]{1,0:T(1,128)S(1)} %copy-done.4, s32[1536,1]{1,0:T(8,128)S(1)} %copy-done.1, ...), custom_call_target="tpu_custom_call" | custom-call | flops 49999998976 | bytes 1474560 | tf_op jit(solution)/shard_map/attend_back/pallas_call | solution.py:384
  850.7 5.2 collective-permute-done.7
  855.9 6.5 fusion.19
  864.3 5.3 fusion.8.grad_heads
  869.7 14.0 %multiply_reduce_fusion = (f32[2560]{0:T(1024)S(1)}, bf16[1536,2560]{1,0:T(8,128)(2,1)}) fusion(bf16[1536,2560]{1,0:T(8,128)(2,1)S(1)} %bitcast.41, f32[1536]{0:T(1024)S(1)} %reduce.2, bf16[1536,1024]{1,0:T(8,128)(2,1)S(1)} %fusion.8.grad_heads, bf16[2560,1024]{1,0:T(8,128)(2,1)} %get-tuple-element.50.weight_ref), kind=kOutput, calls=%fused_computation | convolution fusion | flops 8072721920 | bytes 24133632 | tf_op jit(solution)/shard_map/dot_general | solution.py:25
  885.6 224.5 %tail.1 = (f32[384,2560]{1,0:T(8,128)}, f32[320,1792]{1,0:T(8,128)}, f32[320,640]{1,0:T(8,128)}, f32[320,1024]{1,0:T(8,128)}, bf16[6,320,1792]{2,1,0:T(8,128)(2,...) custom-call(bf16[1536,2560]{1,0:T(8,128)(2,1)} %get-tuple-element.72, ...), custom_call_target="tpu_custom_call" | custom-call | tf_op jit(solution)/shard_map/tail/pallas_call | solution.py:1135
  1120.6 4.2 convert_select_fusion
  (133 shorter events, 52.5 us)
Async XLA Ops:
  6.4 162.5 %copy-start.27 = (s32[1536]{0:T(1024)S(1)}, s32[1536]{0:T(1024)}, u32[]{:S(2)}) copy-start(s32[1536]{0:T(1024)} %param.28) | copy-start | bytes 18436
  6.4 162.5 %copy-start.28 = (s32[1536]{0:T(1024)S(1)}, s32[1536]{0:T(1024)}, u32[]{:S(2)}) copy-start(s32[1536]{0:T(1024)} %param.27) | copy-start | bytes 18436
  6.4 162.5 %copy-start.30 = (s32[1,3]{1,0:T(1,128)S(1)}, s32[1,3]{1,0:T(1,128)}, u32[]{:S(2)}) copy-start(s32[1,3]{1,0:T(1,128)} %param.26) | copy-start | bytes 40
  7.8 163.5 %copy-start.14 = (bf16[320,1792]{1,0:T(8,128)(2,1)}, bf16[320,1792]{1,0:T(8,128)(2,1)S(1)}, u32[]{:S(2)}) copy-start(bf16[320,1792]{1,0:T(8,128)(2,1)S(1)} %pad.20.up) | copy-start | bytes 3440644
  7.8 163.5 %copy-start.23 = (bf16[1728,320]{0,1:T(8,128)(2,1)S(1)}, bf16[1728,320]{0,1:T(8,128)(2,1)}, u32[]{:S(2)}) copy-start(bf16[1728,320]{0,1:T(8,128)(2,1)} %param.24) | copy-start | bytes 3317764
  149.5 110.2 %collective-permute-start.2 = (bf16[320,1792]{1,0:T(8,128)(2,1)S(1)}, bf16[320,1792]{1,0:T(8,128)(2,1)}, u32[]{:S(2)}, u32[]{:S(2)}) collective-permute-start(bf16[320,1792]{1,0:T(8,128)(2,1)S(1)} %pad.20.up), channel_id=1, source_target_pairs={{2,4},{3,5},{4,2},{5,3},{10,12},{11,13},{12,10},{13,11},{18,20},{1... | collective-permute-start | bytes 3440648 | tf_op jit(solution)/shard_map/ppermute | solution.py:65
  151.2 108.5 %collective-permute-start.1 = (bf16[320,1792]{1,0:T(8,128)(2,1)S(1)}, bf16[320,1792]{1,0:T(8,128)(2,1)}, u32[]{:S(2)}, u32[]{:S(2)}) collective-permute-start(bf16[320,1792]{1,0:T(8,128)(2,1)S(1)} %pad.20.up), channel_id=1, source_target_pairs={{0,2},{1,3},{2,6},{3,7},{4,0},{5,1},{6,4},{7,5},{8,10},{9,11},{10,... | collective-permute-start | bytes 3440648 | tf_op jit(solution)/shard_map/ppermute | solution.py:65
  165.9 93.8 %collective-permute-start.4 = (bf16[640,1792]{1,0:T(8,128)(2,1)}, bf16[640,1792]{1,0:T(8,128)(2,1)}, u32[]{:S(2)}, u32[]{:S(2)}) collective-permute-start(bf16[640,1792]{1,0:T(8,128)(2,1)} %get-tuple-element.55.gate_unit), channel_id=1, source_target_pairs={{0,16},{1,17},{2,18},{3,19},{4,20},{5,21},{6,22},{7,23},{8,24},{9,... | collective-permute-start | bytes 6881288 | tf_op jit(solution)/shard_map/ppermute | solution.py:65
  167.4 92.3 %collective-permute-start.3 = (bf16[640,1792]{1,0:T(8,128)(2,1)}, bf16[640,1792]{1,0:T(8,128)(2,1)}, u32[]{:S(2)}, u32[]{:S(2)}) collective-permute-start(bf16[640,1792]{1,0:T(8,128)(2,1)} %get-tuple-element.55.gate_unit), channel_id=1, source_target_pairs={{0,8},{1,9},{2,10},{3,11},{4,12},{5,13},{6,14},{7,15},{8,0},{9,1},... | collective-permute-start | bytes 6881288 | tf_op jit(solution)/shard_map/ppermute | solution.py:65
  168.9 4.2 collective-permute-start
  173.1 24.2 %copy-start.2 = (f32[1,2560]{1,0:T(1,128)}, f32[1,2560]{1,0:T(1,128)S(1)}, u32[]{:S(2)}) copy-start(f32[1,2560]{1,0:T(1,128)S(1)} %reshape.88.gain_ref) | copy-start | bytes 30724
  173.2 73.1 %copy-start.25 = (s32[1536]{0:T(1024)}, s32[1536]{0:T(1024)S(1)}, u32[]{:S(2)}) copy-start(s32[1536]{0:T(1024)S(1)} %slice.64) | copy-start | bytes 18436
  173.6 29.0 %copy-start.3 = (s32[1,1536]{1,0:T(1,128)}, s32[1,1536]{1,0:T(1,128)S(1)}, u32[]{:S(2)}) copy-start(s32[1,1536]{1,0:T(1,128)S(1)} %broadcast_in_dim.51.start_ref) | copy-start | bytes 18436
  173.6 29.0 %copy-start.5 = (s32[12]{0:T(128)}, s32[12]{0:T(128)S(1)}, u32[]{:S(2)}) copy-start(s32[12]{0:T(128)S(1)} %and_select_fusion.first_ref) | copy-start | bytes 148
  173.9 28.7 %copy-start = (s32[1536,1]{1,0:T(8,128)}, s32[1536,1]{1,0:T(8,128)S(1)}, u32[]{:S(2)}) copy-start(s32[1536,1]{1,0:T(8,128)S(1)} %broadcast_in_dim.56.pad_ref) | copy-start | bytes 18436
  202.6 43.6 %copy-start.8 = (bf16[1536,960]{1,0:T(8,128)(2,1)}, bf16[1536,960]{1,0:T(8,128)(2,1)S(1)}, u32[]{:S(2)}) copy-start(bf16[1536,960]{1,0:T(8,128)(2,1)S(1)} %fusion.9.query_ref.all_ref) | copy-start | bytes 8847364
  521.6 22.6 %copy-start.9 = (bf16[1536,1792]{1,0:T(8,128)(2,1)}, bf16[1536,1792]{1,0:T(8,128)(2,1)S(1)}, u32[]{:S(2)}) copy-start(bf16[1536,1792]{1,0:T(8,128)(2,1)S(1)} %get-tuple-element.140.up_signal) | copy-start | bytes 16515076
  757.5 4.2 collective-permute-start.6
  766.3 22.0 %collective-permute-start.5 = (bf16[384,2560]{1,0:T(8,128)(2,1)}, bf16[384,2560]{1,0:T(8,128)(2,1)}, u32[]{:S(2)}, u32[]{:S(2)}) collective-permute-start(bf16[384,2560]{1,0:T(8,128)(2,1)} %get-tuple-element.144), channel_id=1, source_target_pairs={{0,4},{1,5},{2,6},{3,7},{4,0},{5,1},{6,2},{7,3},{8,12},{9,13},{10,... | collective-permute-start | bytes 5898248 | tf_op jit(solution)/shard_map/ppermute | solution.py:65
  768.0 115.6 %collective-permute-start.10 = (bf16[320,1792]{1,0:T(8,128)(2,1)}, bf16[320,1792]{1,0:T(8,128)(2,1)}, u32[]{:S(2)}, u32[]{:S(2)}) collective-permute-start(bf16[320,1792]{1,0:T(8,128)(2,1)} %get-tuple-element.145), channel_id=1, source_target_pairs={{2,4},{3,5},{4,2},{5,3},{10,12},{11,13},{12,10},{13,11},{18,20},{1... | collective-permute-start | bytes 3440648 | tf_op jit(solution)/shard_map/ppermute | solution.py:65
  769.7 114.0 %collective-permute-start.9 = (bf16[320,1792]{1,0:T(8,128)(2,1)}, bf16[320,1792]{1,0:T(8,128)(2,1)}, u32[]{:S(2)}, u32[]{:S(2)}) collective-permute-start(bf16[320,1792]{1,0:T(8,128)(2,1)} %get-tuple-element.146), channel_id=1, source_target_pairs={{0,4},{1,5},{2,0},{3,1},{4,6},{5,7},{6,2},{7,3},{8,12},{9,13},{10,... | collective-permute-start | bytes 3440648 | tf_op jit(solution)/shard_map/ppermute | solution.py:65
  786.2 69.7 %collective-permute-start.7 = (bf16[384,2560]{1,0:T(8,128)(2,1)S(1)}, bf16[384,2560]{1,0:T(8,128)(2,1)}, u32[]{:S(2)}, u32[]{:S(2)}) collective-permute-start(bf16[384,2560]{1,0:T(8,128)(2,1)S(1)} %copy-done.20), channel_id=1, source_target_pairs={{0,1},{1,0},{2,3},{3,2},{4,5},{5,4},{6,7},{7,6},{8,9},{9,8},{10,11... | collective-permute-start | bytes 5898248 | tf_op jit(solution)/shard_map/ppermute | solution.py:65
  793.0 63.0 %copy-start.10 = (f32[384,2560]{1,0:T(8,128)S(1)}, f32[384,2560]{1,0:T(8,128)}, u32[]{:S(2)}) copy-start(f32[384,2560]{1,0:T(8,128)} %get-tuple-element.70.residual_ref) | copy-start | bytes 11796484
  862.4 258.2 %collective-permute-start.8 = (bf16[384,2560]{1,0:T(8,128)(2,1)}, bf16[384,2560]{1,0:T(8,128)(2,1)}, u32[]{:S(2)}, u32[]{:S(2)}) collective-permute-start(bf16[384,2560]{1,0:T(8,128)(2,1)} %get-tuple-element.137), channel_id=1, source_target_pairs={{2,4},{3,5},{4,2},{5,3},{10,12},{11,13},{12,10},{13,11},{18,20},{1... | collective-permute-start | bytes 5898248 | tf_op jit(solution)/shard_map/ppermute | solution.py:65
  (21 other events, 176.9 us)

commit v4 on v3

--- a/solution.py
+++ b/solution.py
@@ -86,10 +86,11 @@
             array, lambda p, c, th, tl: (p, c, 1 - th, tl) if c == th else (p, 1 - c, th, tl)
         )
 
-    def away_turn(self, array):
-        return self.move(
-            array, lambda p, c, th, tl: (p, 1 - c, th, tl) if c == th else (p, c, 1 - th, tl)
-        )
+    def away_to_home(self, array):
+        return self.move(array, lambda p, c, th, tl: (p, c, 1 - th, tl) if c != th else None)
+
+    def home_to_core(self, array):
+        return self.move(array, lambda p, c, th, tl: (p, 1 - c, th, tl) if c == th else None)
 
     def swap(self, array):
         return jnp.where(self.home, array, self.cross(array))
@@ -98,6 +99,27 @@
         rows = array.shape[0] // self.tensor_count
         index = (self.c ^ other) * self.low + (self.tl + step) % self.low
         return lax.dynamic_slice_in_dim(array, index * rows, rows, 0)
+
+    def plane_moves(self, partial):
+        rows, columns = 2 * partial.shape[0] // self.dp_count, partial.shape[1]
+
+        def unit(step):
+            return lax.dynamic_slice(partial, ((self.p ^ step) * rows, 0), (rows, columns))
+
+        return unit(0), [self.to_chip(unit(step), step) for step in range(self.chips - 1, 0, -1)]
+
+    def plane_sum(self, own, moves):
+        total = own.astype(jnp.float32)
+        for arrived in moves:
+            total = total + arrived.astype(jnp.float32)
+        rows = own.shape[0] // 2
+        sums = [total[:rows], total[rows:]]
+        mine = jnp.where(self.c == 0, sums[0], sums[1])
+        other = jnp.where(self.c == 0, sums[1], sums[0])
+        leaving = jnp.stack(
+            [jnp.where(self.home, other, mine).astype(jnp.bfloat16), other.astype(jnp.bfloat16)]
+        )
+        return mine, leaving
 
     def pair_rows(self, partial):
         return [
@@ -488,6 +510,15 @@
             self.tl,
         )
 
+    def back_peer(self):
+        home = self.home.astype(jnp.int32)
+        return self.at(
+            self.p,
+            home * (1 - self.c) + (1 - home) * self.c,
+            home * self.th + (1 - home) * (1 - self.th),
+            self.tl,
+        )
+
     def partner(self):
         return self.at(self.p, self.c, 1 - self.th, self.tl)
 
@@ -800,6 +831,7 @@
         width = partial.shape[1]
         self.stage = [stage.at[i, pl.ds(0, rows), pl.ds(0, width)] for i in range(3)]
         self.both = links.chips == 4
+        self.direct_started = False
         self.loads = [
             links.local_slot() for _ in range(3)
         ]
@@ -829,17 +861,7 @@
             self.arrivals = tuple(
                 tuple(2 * (step - 1) + half for step in links.chip_steps()) for half in range(2)
             )
-        home_int = links.home.astype(jnp.int32)
-        self.first = links.copy(
-            leaving.at[0],
-            turned.at[0],
-            links.at(
-                links.p,
-                home_int * (1 - links.c) + (1 - home_int) * links.c,
-                home_int * links.th + (1 - home_int) * (1 - links.th),
-                links.tl,
-            ),
-        )
+        self.first = links.copy(leaving.at[0], turned.at[0], links.back_peer())
         self.second = links.copy(leaving.at[1], turned.at[1], links.cross_peer(), links.away)
 
     def part(self, step, half):
@@ -860,16 +882,21 @@
         for item in getattr(self, which):
             item.start()
 
+    def start_direct(self):
+        if not self.direct_started:
+            self.start("direct")
+        self.direct_started = True
+
     def arrived(self, which):
         for item in getattr(self, which):
             item.arrived()
 
     def add_before(self):
         if not self.both:
-            self.start("direct")
+            self.start_direct()
             return
         self.arrived("before")
-        self.start("direct")
+        self.start_direct()
         for index, part in ((0, self.part(2, 0)), (1, self.part(1, 1))):
             self.load([part, self.inbox.at[index]])
 
@@ -961,6 +988,38 @@
             row_loop(self.rows, body)
 
 
+class TurnScatter:
+    def __init__(self, links, mine, leaving, result, turned):
+        self.links, self.mine, self.result, self.turned = links, mine, result, turned
+        self.rows = mine.shape[0]
+        self.first = links.copy(leaving.at[0], turned.at[0], links.back_peer())
+        self.second = links.copy(leaving.at[1], turned.at[1], links.cross_peer(), links.away)
+
+    def send_turned(self):
+        self.first.start()
+        self.second.start()
+
+    def finish(self):
+        self.first.arrived()
+        self.second.arrived()
+
+        @pl.when(self.links.home)
+        def _():
+            def body(span):
+                self.result[span] = self.mine[span] + self.turned[0, span].astype(jnp.float32)
+
+            row_loop(self.rows, body)
+
+        @pl.when(self.links.away)
+        def _():
+            def body(span):
+                self.result[span] = self.turned[1, span].astype(jnp.float32) + self.turned[0, span].astype(
+                    jnp.float32
+                )
+
+            row_loop(self.rows, body)
+
+
 def weight_scatter_scratch(chips, rows, width):
     return [pltpu.VMEM((2, rows, width), jnp.bfloat16)] * 3
 
@@ -982,36 +1041,37 @@
     gain_column,
     partial,
     tokens_all,
-    grad_up,
     grad_rows,
     attended,
     normed,
     grad_heads,
     gain_parts,
+    up_mine,
+    up_leaving,
     grad_residual_ref,
     gain_ref,
     input_ref,
     up_ref,
     output_ref,
     first_ref,
-    up_in,
     output_in,
     first_in,
     grad_output,
     grad_first,
     *scratch,
 ):
-    up_work, output_work, first_work = (scratch[3 * i : 3 * i + 3] for i in range(3))
-    stage, own_ref, leaving, crossed, mine, others, sums, arrivals, gains_out, gains_in, total = scratch[9:20]
-    links = Links(dp_count, tensor_count, *scratch[20:])
+    output_work, first_work = scratch[:3], scratch[3:6]
+    up_turned, stage, own_ref, leaving, crossed, mine, others, sums, arrivals = scratch[6:15]
+    gains_out, gains_in, total = scratch[15:18]
+    links = Links(dp_count, tensor_count, *scratch[18:])
     links.all_low = True
     rows = own_ref.shape[0]
     load_own = links.keep(tokens_all.at[pl.ds(links.quarter * rows, rows)], own_ref)
     scatter = RowScatter(links, partial, mine, others, sums, arrivals, rows)
     crossing = links.copy(leaving, crossed, links.cross_peer(), links.away)
+    up = TurnScatter(links, up_mine, up_leaving, up_ref, up_turned)
     weights = []
     for grad, result, inbox, work in (
-        (grad_up, up_ref, up_in, up_work),
         (grad_output, output_ref, output_in, output_work),
         (grad_first, first_ref, first_in, first_work),
     ):
@@ -1019,7 +1079,7 @@
         made = WeightScatter(links, grad, result, inbox, turned, added, turning, stage)
         made.total = None if made.both else total.at[pl.ds(0, made.rows), pl.ds(0, grad.shape[1])]
         weights.append(made)
-    up, output, first = weights
+    output, first = weights
     gain_sends = []
     for step in range(1, tensor_count):
         other = (links.tensor_index + step) % tensor_count
@@ -1030,7 +1090,7 @@
     links.enter()
     scatter.start()
     load_own.start()
-    up.start("before")
+    up.send_turned()
     scatter.send_sums()
     load_own.done()
 
@@ -1040,8 +1100,10 @@
         out_ref[:, columns - 128 :] = (value[:, columns - 128 :] + parts_ref[...]).astype(jnp.bfloat16)
 
     product(normed, grad_heads, grad_first, 0, 0, 512, 1024, finish, (gain_parts,))
-    up.add_before()
+    first.start("before")
     product(grad_rows, attended, grad_output, 0, 0, 512, 1024)
+    first.add_before()
+    output.start("before")
 
     def use(span, grad_normed):
         own = own_ref[span].astype(jnp.float32)
@@ -1056,16 +1118,10 @@
 
     scatter.collect(use)
     crossing.start()
-    up.arrived("direct")
-    up.arrived("summed")
-    first.start("before")
-    up.turn()
-    first.add_before()
-    output.start("before")
+    output.add_before()
     first.arrived("direct")
     first.arrived("summed")
     first.turn()
-    output.add_before()
     crossing.arrived()
 
     @pl.when(links.away)
@@ -1101,20 +1157,20 @@
     gain_column,
     partial,
     tokens_all,
-    grad_up,
     grad_rows,
     attended,
     normed,
     grad_heads,
     gain_parts,
+    up_mine,
+    up_leaving,
     grad_residual,
     gain,
 ):
     rows, width = grad_residual.shape
     low, chips = tensor_count // 2, dp_count // 2
-    features = grad_up.shape[0]
+    features = width
     partials = [
-        grad_up,
         jax.ShapeDtypeStruct((features, attended.shape[1]), jnp.bfloat16),
         jax.ShapeDtypeStruct((features, grad_heads.shape[1]), jnp.bfloat16),
     ]
@@ -1124,6 +1180,7 @@
     scratch = []
     for block, columns in shapes:
         scratch += weight_scatter_scratch(chips, block, columns)
+    scratch += [pltpu.VMEM(up_leaving.shape, jnp.bfloat16)]
     scratch += [pltpu.VMEM((3, most, widest), jnp.bfloat16)]
     scratch += [pltpu.VMEM((rows, width), jnp.bfloat16)] * 3
     scratch += scatter_scratch(low, rows, width)
@@ -1135,23 +1192,24 @@
     return pl.pallas_call(
         functools.partial(tail_kernel, dp_count, tensor_count, gain_column),
         out_shape=[jax.ShapeDtypeStruct((rows, width), jnp.float32)]
-        + [jax.ShapeDtypeStruct(shape, jnp.float32) for shape in shapes]
+        + [jax.ShapeDtypeStruct(shape, jnp.float32) for shape in [up_mine.shape] + shapes]
         + [inbox_shape(chips, *shape) for shape in shapes]
-        + partials[1:],
-        in_specs=anywhere(8) + in_vmem(2),
-        out_specs=in_vmem(4) + anywhere(5),
+        + partials,
+        in_specs=anywhere(7) + in_vmem(4),
+        out_specs=in_vmem(4) + anywhere(4),
         scratch_shapes=scratch + semaphores(96, 24),
         compiler_params=link_params(3),
         name="tail",
     )(
         partial,
         tokens_all,
-        grad_up,
         grad_rows,
         attended,
         normed,
         grad_heads,
         gain_parts,
+        up_mine,
+        up_leaving,
         grad_residual,
         gain,
     )[:4]
@@ -1356,7 +1414,6 @@
     tensor_count,
     partial,
     cot_all,
-    grad_down,
     normed_ffn,
     gate_signal,
     up_signal,
@@ -1372,6 +1429,7 @@
     grad_rows,
     down_in,
     gate_in,
+    grad_down,
     grad_gate,
     grad_up,
     down_part,
@@ -1403,11 +1461,28 @@
     links.enter()
     scatter.start()
     load.start()
-    down.start("before")
-    scatter.send_sums()
+    unit = 2 * down.rows
+
+    def down_unit(step):
+        at = pl.multiple_of(links.chip(step) * unit, 128)
+        product(cot_all.at[:, pl.ds(at, unit)], hidden, grad_down.at[pl.ds(at, unit)], 0, 0, unit, 1024)
+
+    if down.both and unit % 128 == 0:
+        down_unit(3)
+        down.start("before")
+        scatter.send_sums()
+        down_unit(1)
+        down_unit(2)
+        down.start_direct()
+        down_unit(0)
+    else:
+        product(cot_all, hidden, grad_down, 0, 0, 512, 1024)
+        down.start("before")
+        scatter.send_sums()
     load.done()
+    down.add_before()
     product(normed_ffn, gate_signal, grad_gate, 0, 0, 512, 1024)
-    down.add_before()
+    gate.start("before")
     gain_part_ref[...] = jnp.zeros_like(gain_part_ref)
 
     def use(span, grad_normed):
@@ -1426,20 +1501,19 @@
     store.start()
     store.done()
     gather.start()
-    gate.start("before")
     down.arrived("direct")
+    gate.start_direct()
     down.arrived("summed")
-    down.reduce()
-    down.send_turned()
+    down.turn()
     gate.add_before()
     product(normed_ffn, up_signal, grad_up, 0, 0, 512, 1024)
     gather.pass_on()
     product(hidden, down_full, down_part, 1, 1, 512, 1024)
     gate.arrived("direct")
     gate.arrived("summed")
+    gate.reduce()
     down.finish()
     gather.finish()
-    gate.reduce()
     links.leave()
 
 
@@ -1448,7 +1522,6 @@
     tensor_count,
     partial,
     cot_all,
-    grad_down,
     normed_ffn,
     gate_signal,
     up_signal,
@@ -1459,7 +1532,8 @@
 ):
     rows, width = residual.shape
     low, chips = tensor_count // 2, dp_count // 2
-    block, columns = scatter_shapes(chips, grad_down)
+    grad = jax.ShapeDtypeStruct((width, hidden.shape[1]), jnp.bfloat16)
+    block, columns = scatter_shapes(chips, grad)
     return pl.pallas_call(
         functools.partial(turn_back_kernel, dp_count, tensor_count),
         out_shape=[
@@ -1471,12 +1545,13 @@
             jax.ShapeDtypeStruct((rows * tensor_count, width), jnp.bfloat16),
             inbox_shape(chips, block, columns),
             inbox_shape(chips, block, columns),
-            jax.ShapeDtypeStruct(grad_down.shape, jnp.bfloat16),
-            jax.ShapeDtypeStruct(grad_down.shape, jnp.bfloat16),
+            grad,
+            grad,
+            grad,
             jax.ShapeDtypeStruct((rows * tensor_count, width), jnp.bfloat16),
         ],
-        in_specs=anywhere(8) + in_vmem(2),
-        out_specs=in_vmem(5) + anywhere(6),
+        in_specs=anywhere(7) + in_vmem(2),
+        out_specs=in_vmem(5) + anywhere(7),
         scratch_shapes=[pltpu.VMEM((rows, width), jnp.bfloat16)] * 2
         + weight_scatter_scratch(chips, block, columns)
         + [
@@ -1488,7 +1563,51 @@
         + semaphores(64, 24),
         compiler_params=link_params(2),
         name="turn_back",
-    )(partial, cot_all, grad_down, normed_ffn, gate_signal, up_signal, hidden, down_full, residual, gain)
+    )(partial, cot_all, normed_ffn, gate_signal, up_signal, hidden, down_full, residual, gain)
+
+
+def hidden_back_kernel(
+    cot_all, down_full, gate_values, up_values, gate_full, up_full, gate_signal, up_signal, partial
+):
+    def signals(grad_hidden, gate_ref, up_ref, gate_out, up_out):
+        gate = gate_ref[...]
+        sigmoid = jax.nn.sigmoid(gate)
+        grad_hidden = grad_hidden * sigmoid
+        gate_out[...] = (grad_hidden * up_ref[...] * (1.0 + gate * (1.0 - sigmoid))).astype(jnp.bfloat16)
+        up_out[...] = (grad_hidden * gate).astype(jnp.bfloat16)
+
+    product(
+        cot_all, down_full, gate_signal, 1, 0, 256, 1024, signals, (gate_values, up_values), (up_signal,)
+    )
+    count, width = partial.shape
+    depth = gate_full.shape[1]
+    rows, columns = math.gcd(count, 512), cut(width, 1536)
+
+    def body(gate_ref, up_ref, gate_weight, up_weight, out_ref):
+        total = times(gate_ref[...], gate_weight[...], 1, 1) + times(up_ref[...], up_weight[...], 1, 1)
+        out_ref[...] = total.astype(jnp.bfloat16)
+
+    pltpu.emit_pipeline(
+        body,
+        grid=(width // columns, count // rows),
+        in_specs=[pl.BlockSpec((rows, depth), lambda j, i: (i, 0))] * 2
+        + [pl.BlockSpec((columns, depth), lambda j, i: (j, 0))] * 2,
+        out_specs=[pl.BlockSpec((rows, columns), lambda j, i: (i, j))],
+    )(gate_signal, up_signal, gate_full, up_full, partial)
+
+
+def hidden_back(cot_all, down_full, gate_values, up_values, gate_full, up_full):
+    signal = jax.ShapeDtypeStruct(gate_values.shape, jnp.bfloat16)
+    flops = 6 * cot_all.size * gate_values.shape[1]
+    return pl.pallas_call(
+        hidden_back_kernel,
+        out_shape=[signal, signal, jax.ShapeDtypeStruct(cot_all.shape, jnp.bfloat16)],
+        in_specs=anywhere(6),
+        out_specs=anywhere(3),
+        compiler_params=pltpu.CompilerParams(vmem_limit_bytes=LINK_VMEM_LIMIT),
+        cost_estimate=pl.CostEstimate(flops=flops, bytes_accessed=flops // 1000, transcendentals=0),
+        name="hidden_back",
+    )(cot_all, down_full, gate_values, up_values, gate_full, up_full)
 
 
 def starts_of(positions, length_row):
@@ -1608,26 +1727,19 @@
         gate_units,
         feedforward_scale,
     )
-    sigmoid = jax.nn.sigmoid(gate_values)
 
     def leave(own):
         arrived = place.cross(own.astype(jnp.bfloat16)).astype(jnp.float32)
         return jnp.where(place.home, own, arrived)
 
-    grad_hidden = contract(cot_all, down_turned, 1, 0)
-    grad_gate = (grad_hidden * up_values * sigmoid * (1.0 + gate_values * (1.0 - sigmoid))).astype(
-        jnp.bfloat16
-    )
-    grad_up = (grad_hidden * gate_values * sigmoid).astype(jnp.bfloat16)
-    grad_part = (contract(grad_gate, gate_full, 1, 1) + contract(grad_up, up_full, 1, 1)).astype(
-        jnp.bfloat16
+    grad_gate, grad_up, grad_part = hidden_back(
+        cot_all, down_turned, gate_values, up_values, gate_full, up_full
     )
     turned_back = turn_back(
         dp_count,
         tensor_count,
         grad_part,
         cot_all,
-        contract(cot_all, hidden, 0, 0, jnp.bfloat16),
         normed_ffn,
         grad_gate,
         grad_up,
@@ -1637,9 +1749,9 @@
         feedforward_scale,
     )
     grad_residual, feedforward_part, down_grad, gate_grad, gate_turning, grad_rows = turned_back[:6]
-    up_part, down_part = turned_back[9:]
-    gate_turned = place.away_turn(gate_turning[0])
-    gate_crossed = place.cross(gate_turning[1])
+    up_part, down_part = turned_back[10:]
+    up_own, up_moves = place.plane_moves(up_part)
+    gate_arrived = place.away_to_home(gate_turning)
 
     pairs = place.pair_rows(down_part)
     grad_attended = contract(grad_rows, output_turned, 1, 0, jnp.bfloat16)
@@ -1658,19 +1770,18 @@
         kv_heads,
         group,
     )
+    layer_own = after(residual, grad_query) + place.sum_rows(pairs)
     spare = jnp.zeros((count, first_padded - head_columns), jnp.bfloat16)
-    grad_heads = contract(
-        to_storage, jnp.concatenate([grad_query, grad_rest, spare], axis=1), 1, 0, jnp.bfloat16
-    )
+    up_mine, up_leaving = place.plane_sum(after(up_own, grad_query), up_moves)
+    sequence_grads = after(jnp.concatenate([grad_query, grad_rest, spare], axis=1), layer_own)
+    grad_heads = contract(to_storage, sequence_grads, 1, 0, jnp.bfloat16)
     grad_normed_part = contract(grad_heads, first_weight, 1, 1)
     tokens_wide = tokens_all.astype(jnp.float32)
     attention_part = jnp.sum(grad_normed_part * (tokens_wide * token_roots), axis=0)
-    layer_own = after(residual, grad_query) + place.sum_rows(pairs)
     layer_output = leave(layer_own)
-    gate_turned, gate_crossed = lax.optimization_barrier((gate_turned, gate_crossed, grad_query))[:2]
-    gate_grad = jnp.where(place.home, gate_grad, gate_crossed.astype(jnp.float32)) + gate_turned.astype(
-        jnp.float32
-    )
+    gate_arrived = after(gate_arrived, grad_query).astype(jnp.float32)
+    gate_other = place.home_to_core((gate_turning[0].astype(jnp.float32) + gate_arrived[1]).astype(jnp.bfloat16))
+    gate_grad = jnp.where(place.home, gate_grad + gate_arrived[0], gate_other.astype(jnp.float32))
     gain_parts = jnp.stack([attention_part, feedforward_part[0]], axis=1)
     before = head_columns - (first_padded - 128)
     gain_parts = jnp.pad(gain_parts, ((0, 0), (before, 126 - before)))
@@ -1680,12 +1791,13 @@
         head_columns,
         after(grad_normed_part.astype(jnp.bfloat16), layer_own),
         tokens_all,
-        up_part,
         grad_rows,
         wide(attended_stored, output_padded),
         normed,
         grad_heads,
         gain_parts,
+        up_mine,
+        up_leaving,
         grad_residual,
         attention_scale,
     )

time: 1130 us -> 1090 us (0.965)
  matrix products: 137 us -> 54.4 us
  Pallas kernels: 884 us -> 914 us
    dot_general x10 -> x6, matrix products: 137 us -> 54.4 us  [contract(): lax.dot_general(left, right, (((left_dim,), (right_dim,)), ((), ())), pre...]
    pallas_call x0 -> x1, Pallas kernels: none -> 64.3 us  [hidden_back(): pl.pallas_call(hidden_back_kernel, out_shape=[signal, signal, jax.ShapeDt...]
    pallas_call x1, Pallas kernels: 224 us -> 187 us  [tail(): pl.pallas_call(functools.partial(tail_kernel, dp_count, tensor_count, gai...]
    convert_element_type x1 -> x2, other arithmetic: 15 us -> 3.52 us  [the longest x1 2.15 us: per_device(): gate_arrived = after(gate_arrived, grad_query).astype(jnp.float32)]
    ppermute x11 -> x14, starting transfers between devices: 26.4 us -> 36.1 us  [move(): return lax.ppermute(array, AXES, pairs)]
  transfers between devices with their start and end apart: 11 -> 14, of which waited for: 2 -> 0; matrix products, arithmetic and copies ran while one was open for 8% -> 10% of each run, Pallas kernels for 31% -> 29%
where the time goes in v4:
time: 1090 us; the launch traced here: 1080 us
  Pallas kernels  914 us (84%)
  matrix products  54.4 us (5%)
  other arithmetic  41.5 us (4%)
  local copies, waits for them, and re-layouts  37.2 us (3%)
  starting transfers between devices  36.1 us (3%)
    pallas_call x1, Pallas kernels, middle(): pl.pallas_call(functools.partial(middle_kernel, dp_count, tensor_count, l...  210 us
    pallas_call x1, Pallas kernels, turn_back(): pl.pallas_call(functools.partial(turn_back_kernel, dp_count, tensor_count...  190 us
    pallas_call x1, Pallas kernels, tail(): pl.pallas_call(functools.partial(tail_kernel, dp_count, tensor_count, gai...  187 us
    pallas_call x1, Pallas kernels, gather_first(): pl.pallas_call(functools.partial(gather_first_kernel, dp_count, tensor_co...  141 us
    pallas_call x1, Pallas kernels, hidden_back(): pl.pallas_call(hidden_back_kernel, out_shape=[signal, signal, jax.ShapeDt...  64.3 us
    pallas_call x1, Pallas kernels, attend_back(): pl.pallas_call(functools.partial(attend_back_kernel, kv_heads, group), gr...  57.4 us
    dot_general x6, matrix products, contract(): lax.dot_general(left, right, (((left_dim,), (right_dim,)), ((), ())), pre...  54.4 us
    pallas_call x1, Pallas kernels, attend(): pl.pallas_call(functools.partial(attend_kernel, kv_heads, group), grid_sp...  43.6 us
  transfers between devices with their start and end apart: 14, of which 0 were waited for; matrix products, arithmetic and copies ran while one was open for 10% of the time, Pallas kernels for 29%

profile of v4, /device:TPU:0, one launch (start us, length us, event | category | flops | bytes accessed | tf_op | source)
XLA Modules:
  0.0 1084.4 jit_solution(5794313508402092981)
XLA Ops:
  8.2 140.5 %gather_first.1 = (bf16[1536,2560]{1,0:T(8,128)(2,1)}, bf16[2560,1024]{1,0:T(8,128)(2,1)}, bf16[2560,640]{1,0:T(8,128)(2,1)}, bf16[640,1792]{1,0:T(8,128)(2,1)}) custom-call(bf16[384,2560]{1,0:T(8,128)(2,1)} %tokens.1, bf16[320,1024]{1,0:T(8,128)(2,1)} %pad.18.first, bf16[320,640]{1,0:T(8,128)(2,1)} %bitcast.42, bf16[320,1792]{1,0:T(8,128)(2,1)} %pad.19.gate), custom_call_target="tpu_custom_call" | custom-call | tf_op jit(solution)/shard_map/gather_first/pallas_call | solution.py:1266
  150.5 14.7 %collective-permute-start.1 = (bf16[320,1792]{1,0:T(8,128)(2,1)S(1)}, bf16[320,1792]{1,0:T(8,128)(2,1)}, u32[]{:S(2)}, u32[]{:S(2)}) collective-permute-start(bf16[320,1792]{1,0:T(8,128)(2,1)S(1)} %pad.20.up), channel_id=1, source_target_pairs={{0,2},{1,3},{2,6},{3,7},{4,0},{5,1},{6,4},{7,5},{8,10},{9,11},{10,... | collective-permute-start | bytes 3440648 | tf_op jit(solution)/shard_map/ppermute | solution.py:65
  174.9 21.6 %project.1 = (bf16[1536,2560]{1,0:T(8,128)(2,1)}, bf16[1536,960]{1,0:T(8,128)(2,1)S(1)}, f32[1536,1]{1,0:T(8,128)S(1)}) custom-call(bf16[1536,2560]{1,0:T(8,128)(2,1)} %get-tuple-element.53.tokens_ref.tokens_all, f32[1,2560]{1,0:T(1,128)S(1)} %reshape.91.gain_ref, bf16[2560,1024]{1,0:T(8,128)(2,1)} %get-tuple-element.54.weight_ref, ...), custom_call_target="tpu_custom_call" | custom-call | flops 8053063680 | bytes 20971520 | tf_op jit(solution)/shard_map/project/pallas_call | solution.py:159
  196.6 5.2 fusion.9.query_ref.all_ref
  201.8 43.6 %attend.1 = (bf16[1536,640]{1,0:T(8,128)(2,1)S(1)}, f32[8,1536]{1,0:T(8,128)S(1)}) custom-call(s32[12]{0:T(128)S(1)} %and_select_fusion.first_ref, bf16[1536,960]{1,0:T(8,128)(2,1)S(1)} %fusion.9.query_ref.all_ref, bf16[1536,960]{1,0:T(8,128)(2,1)S(1)} %fusion.9.query_ref.all_ref, s32[1,1536]{1,0:T(1,128)S(1)} %broadcast_in_dim.51.start_ref, ...), custom_call_target="tpu_custom_call" | custom-call | flops 49999998976 | bytes 1474560 | tf_op jit(solution)/shard_map/attend/pallas_call | solution.py:270
  245.5 4.3 fusion.10.attended
  249.8 8.8 convolution_convert_fusion.partial
  258.6 209.6 %middle.1 = (f32[384,2560]{1,0:T(8,128)}, bf16[1536,2560]{1,0:T(8,128)(2,1)}, bf16[1536,2560]{1,0:T(8,128)(2,1)}, bf16[2560,1792]{1,0:T(8,128)(2,1)}, bf16[2560,...) custom-call(bf16[1536,2560]{1,0:T(8,128)(2,1)} %convolution_convert_, ...), custom_call_target="tpu_custom_call" | custom-call | tf_op jit(solution)/shard_map/middle/pallas_call | solution.py:1389
  468.2 64.3 %hidden_back.1 = (bf16[1536,1792]{1,0:T(8,128)(2,1)}, bf16[1536,1792]{1,0:T(8,128)(2,1)}, bf16[1536,2560]{1,0:T(8,128)(2,1)}) custom-call(bf16[1536,2560]{1,0:T(8,128)(2,1)} %get-tuple-element.62.cot_all, bf16[2560,1792]{1,0:T(8,128)(2,1)} %get-tuple-element.63.down_full, f32[1536,1792]{1,0:T(8,128)} %get-tuple-element.64.gate_values, ...), custom_call_target="tpu_custom_call" | custom-call | flops 42278584320 | bytes 42278584 | tf_op jit(solution)/shard_map/hidden_back/pallas_call | solution.py:1602
  532.5 189.9 %turn_back.1 = (f32[384,2560]{1,0:T(8,128)}, f32[1,2560]{1,0:T(1,128)}, f32[320,1792]{1,0:T(8,128)}, f32[320,1792]{1,0:T(8,128)}, bf16[2,320,1792]{2,1,0:T(8,128...) custom-call(bf16[1536,2560]{1,0:T(8,128)(2,1)} %get-tuple-element.68, ...), custom_call_target="tpu_custom_call" | custom-call | tf_op jit(solution)/shard_map/turn_back/pallas_call | solution.py:1537
  727.2 3.2 slice_bitcast_fusion.1
  730.4 4.7 convert_add_fusion.1
  737.7 3.7 constant_dynamic-slice_fusion.3
  744.9 15.6 %fusion.11.grad_ref = bf16[1536,640]{1,0:T(8,128)(2,1)} fusion(s32[1536]{0:T(1024)S(1)} %slice.76, bf16[1536,2560]{1,0:T(8,128)(2,1)} %get-tuple-element.73.grad_rows, bf16[2560,640]{1,0:T(8,128)(2,1)} %get-tuple-element.57), kind=kOutput, calls=%fused_computation.21 | convolution fusion | flops 8057389056 | bytes 13113344 | tf_op jit(solution)/shard_map/dot_general | solution.py:25
  765.2 57.4 %attend_back.1 = (bf16[1536,640]{1,0:T(8,128)(2,1)S(1)}, bf16[1536,320]{1,0:T(8,128)(2,1)S(1)}) custom-call(s32[12]{0:T(128)S(1)} %and_select_fusion.first_ref, bf16[1536,960]{1,0:T(8,128)(2,1)} %copy-done.2, bf16[1536,960]{1,0:T(8,128)(2,1)} %copy-done.2, s32[1,1536]{1,0:T(1,128)S(1)} %broadcast_in_dim.51.start_ref, ...), custom_call_target="tpu_custom_call" | custom-call | flops 49999998976 | bytes 1474560 | tf_op jit(solution)/shard_map/attend_back/pallas_call | solution.py:406
  824.7 3.6 fusion.16
  830.3 6.6 fusion.8.grad_heads
  840.7 5.2 collective-permute-start.13
  845.9 13.8 %multiply_reduce_fusion = (f32[2560]{0:T(1024)S(1)}, bf16[1536,2560]{1,0:T(8,128)(2,1)}) fusion(bf16[1536,2560]{1,0:T(8,128)(2,1)S(1)} %bitcast.38, f32[1536]{0:T(1024)S(1)} %reduce.2, bf16[1536,1024]{1,0:T(8,128)(2,1)} %fusion.8.grad_heads, bf16[2560,1024]{1,0:T(8,128)(2,1)} %get-tuple-element.54.weight_ref), kind=kOutput, calls=%fused_computation | convolution fusion | flops 8072721920 | bytes 24133632 | tf_op jit(solution)/shard_map/dot_general | solution.py:25
  859.8 6.2 convert_add_fusion
  870.4 5.7 fusion.14
  877.6 186.5 %tail.1 = (f32[384,2560]{1,0:T(8,128)}, f32[320,1792]{1,0:T(8,128)}, f32[320,640]{1,0:T(8,128)}, f32[320,1024]{1,0:T(8,128)}, bf16[6,320,640]{2,1,0:T(8,128)(2,1...) custom-call(bf16[1536,2560]{1,0:T(8,128)(2,1)} %get-tuple-element.80.partial, ...), custom_call_target="tpu_custom_call" | custom-call | tf_op jit(solution)/shard_map/tail/pallas_call | solution.py:1192
  1071.0 3.8 fusion.12
  1074.8 4.2 convert_select_fusion
  (119 shorter events, 59.8 us)
Async XLA Ops:
  7.1 143.3 %copy-start.7 = (bf16[320,1792]{1,0:T(8,128)(2,1)}, bf16[320,1792]{1,0:T(8,128)(2,1)S(1)}, u32[]{:S(2)}) copy-start(bf16[320,1792]{1,0:T(8,128)(2,1)S(1)} %pad.20.up) | copy-start | bytes 3440644
  7.1 161.1 %copy-start.16 = (s32[1536]{0:T(1024)S(1)}, s32[1536]{0:T(1024)}, u32[]{:S(2)}) copy-start(s32[1536]{0:T(1024)} %param.28) | copy-start | bytes 18436
  7.1 161.1 %copy-start.17 = (s32[1536]{0:T(1024)S(1)}, s32[1536]{0:T(1024)}, u32[]{:S(2)}) copy-start(s32[1536]{0:T(1024)} %param.27) | copy-start | bytes 18436
  7.1 161.1 %copy-start.19 = (s32[1,3]{1,0:T(1,128)S(1)}, s32[1,3]{1,0:T(1,128)}, u32[]{:S(2)}) copy-start(s32[1,3]{1,0:T(1,128)} %param.26) | copy-start | bytes 40
  8.2 162.4 %copy-start.13 = (bf16[1728,320]{0,1:T(8,128)(2,1)S(1)}, bf16[1728,320]{0,1:T(8,128)(2,1)}, u32[]{:S(2)}) copy-start(bf16[1728,320]{0,1:T(8,128)(2,1)} %param.24) | copy-start | bytes 3317764
  148.8 109.8 %collective-permute-start.2 = (bf16[320,1792]{1,0:T(8,128)(2,1)S(1)}, bf16[320,1792]{1,0:T(8,128)(2,1)}, u32[]{:S(2)}, u32[]{:S(2)}) collective-permute-start(bf16[320,1792]{1,0:T(8,128)(2,1)S(1)} %pad.20.up), channel_id=1, source_target_pairs={{2,4},{3,5},{4,2},{5,3},{10,12},{11,13},{12,10},{13,11},{18,20},{1... | collective-permute-start | bytes 3440648 | tf_op jit(solution)/shard_map/ppermute | solution.py:65
  150.5 108.2 %collective-permute-start.1 = (bf16[320,1792]{1,0:T(8,128)(2,1)S(1)}, bf16[320,1792]{1,0:T(8,128)(2,1)}, u32[]{:S(2)}, u32[]{:S(2)}) collective-permute-start(bf16[320,1792]{1,0:T(8,128)(2,1)S(1)} %pad.20.up), channel_id=1, source_target_pairs={{0,2},{1,3},{2,6},{3,7},{4,0},{5,1},{6,4},{7,5},{8,10},{9,11},{10,... | collective-permute-start | bytes 3440648 | tf_op jit(solution)/shard_map/ppermute | solution.py:65
  165.2 93.4 %collective-permute-start.4 = (bf16[640,1792]{1,0:T(8,128)(2,1)}, bf16[640,1792]{1,0:T(8,128)(2,1)}, u32[]{:S(2)}, u32[]{:S(2)}) collective-permute-start(bf16[640,1792]{1,0:T(8,128)(2,1)} %get-tuple-element.59.gate_unit), channel_id=1, source_target_pairs={{0,16},{1,17},{2,18},{3,19},{4,20},{5,21},{6,22},{7,23},{8,24},{9,... | collective-permute-start | bytes 6881288 | tf_op jit(solution)/shard_map/ppermute | solution.py:65
  166.7 91.9 %collective-permute-start.3 = (bf16[640,1792]{1,0:T(8,128)(2,1)}, bf16[640,1792]{1,0:T(8,128)(2,1)}, u32[]{:S(2)}, u32[]{:S(2)}) collective-permute-start(bf16[640,1792]{1,0:T(8,128)(2,1)} %get-tuple-element.59.gate_unit), channel_id=1, source_target_pairs={{0,8},{1,9},{2,10},{3,11},{4,12},{5,13},{6,14},{7,15},{8,0},{9,1},... | collective-permute-start | bytes 6881288 | tf_op jit(solution)/shard_map/ppermute | solution.py:65
  168.2 4.2 collective-permute-start
  172.4 24.2 %copy-start = (f32[1,2560]{1,0:T(1,128)}, f32[1,2560]{1,0:T(1,128)S(1)}, u32[]{:S(2)}) copy-start(f32[1,2560]{1,0:T(1,128)S(1)} %reshape.91.gain_ref) | copy-start | bytes 30724
  201.8 43.6 %copy-start.2 = (bf16[1536,960]{1,0:T(8,128)(2,1)}, bf16[1536,960]{1,0:T(8,128)(2,1)S(1)}, u32[]{:S(2)}) copy-start(bf16[1536,960]{1,0:T(8,128)(2,1)S(1)} %fusion.9.query_ref.all_ref) | copy-start | bytes 8847364
  249.8 8.9 copy-start.10
  725.4 5.0 collective-permute-start.6
  725.8 111.2 %collective-permute-start.12 = (bf16[2,320,1792]{2,1,0:T(8,128)(2,1)}, bf16[2,320,1792]{2,1,0:T(8,128)(2,1)}, u32[]{:S(2)}, u32[]{:S(2)}) collective-permute-start(bf16[2,320,1792]{2,1,0:T(8,128)(2,1)} %get-tuple-element.91), channel_id=1, source_target_pairs={{2,0},{3,1},{4,6},{5,7},{10,8},{11,9},{12,14},{13,15},{18,16},{19,... | collective-permute-start | bytes 6881288 | tf_op jit(solution)/shard_map/ppermute | solution.py:65
  735.1 25.4 %collective-permute-start.5 = (bf16[384,2560]{1,0:T(8,128)(2,1)}, bf16[384,2560]{1,0:T(8,128)(2,1)}, u32[]{:S(2)}, u32[]{:S(2)}) collective-permute-start(bf16[384,2560]{1,0:T(8,128)(2,1)} %get-tuple-element.156), channel_id=1, source_target_pairs={{0,4},{1,5},{2,6},{3,7},{4,0},{5,1},{6,2},{7,3},{8,12},{9,13},{10,... | collective-permute-start | bytes 5898248 | tf_op jit(solution)/shard_map/ppermute | solution.py:65
  741.4 118.4 %collective-permute-start.11 = (bf16[640,1792]{1,0:T(8,128)(2,1)}, bf16[640,1792]{1,0:T(8,128)(2,1)}, u32[]{:S(2)}, u32[]{:S(2)}) collective-permute-start(bf16[640,1792]{1,0:T(8,128)(2,1)} %get-tuple-element.152), channel_id=1, source_target_pairs={{0,8},{1,9},{2,10},{3,11},{4,12},{5,13},{6,14},{7,15},{8,0},{9,1},... | collective-permute-start | bytes 6881288 | tf_op jit(solution)/shard_map/ppermute | solution.py:65
  742.7 117.1 %collective-permute-start.10 = (bf16[640,1792]{1,0:T(8,128)(2,1)}, bf16[640,1792]{1,0:T(8,128)(2,1)}, u32[]{:S(2)}, u32[]{:S(2)}) collective-permute-start(bf16[640,1792]{1,0:T(8,128)(2,1)} %get-tuple-element.153), channel_id=1, source_target_pairs={{0,16},{1,17},{2,18},{3,19},{4,20},{5,21},{6,22},{7,23},{8,24},{9,... | collective-permute-start | bytes 6881288 | tf_op jit(solution)/shard_map/ppermute | solution.py:65
  743.4 116.4 %collective-permute-start.9 = (bf16[640,1792]{1,0:T(8,128)(2,1)}, bf16[640,1792]{1,0:T(8,128)(2,1)}, u32[]{:S(2)}, u32[]{:S(2)}) collective-permute-start(bf16[640,1792]{1,0:T(8,128)(2,1)} %get-tuple-element.154), channel_id=1, source_target_pairs={{0,24},{1,25},{2,26},{3,27},{4,28},{5,29},{6,30},{7,31},{8,16},{9,... | collective-permute-start | bytes 6881288 | tf_op jit(solution)/shard_map/ppermute | solution.py:65
  760.5 62.9 %collective-permute-start.7 = (bf16[384,2560]{1,0:T(8,128)(2,1)S(1)}, bf16[384,2560]{1,0:T(8,128)(2,1)S(1)}, u32[]{:S(2)}, u32[]{:S(2)}) collective-permute-start(bf16[384,2560]{1,0:T(8,128)(2,1)S(1)} %get-tuple-element.155), channel_id=1, source_target_pairs={{0,1},{1,0},{2,3},{3,2},{4,5},{5,4},{6,7},{7,6},{8,9},{9,8},{10,11... | collective-permute-start | bytes 5898248 | tf_op jit(solution)/shard_map/ppermute | solution.py:65
  828.4 246.4 %collective-permute-start.8 = (bf16[384,2560]{1,0:T(8,128)(2,1)}, bf16[384,2560]{1,0:T(8,128)(2,1)}, u32[]{:S(2)}, u32[]{:S(2)}) collective-permute-start(bf16[384,2560]{1,0:T(8,128)(2,1)} %get-tuple-element.147), channel_id=1, source_target_pairs={{2,4},{3,5},{4,2},{5,3},{10,12},{11,13},{12,10},{13,11},{18,20},{1... | collective-permute-start | bytes 5898248 | tf_op jit(solution)/shard_map/ppermute | solution.py:65
  837.0 8.9 slice-start
  840.7 19.1 %copy-start.5 = (bf16[640,1792]{1,0:T(8,128)(2,1)S(1)}, bf16[640,1792]{1,0:T(8,128)(2,1)}, u32[]{:S(2)}) copy-start(bf16[640,1792]{1,0:T(8,128)(2,1)} %get-tuple-element.85) | copy-start | bytes 6881284
  840.7 230.3 %collective-permute-start.13 = (bf16[320,1792]{1,0:T(8,128)(2,1)}, bf16[320,1792]{1,0:T(8,128)(2,1)}, u32[]{:S(2)}, u32[]{:S(2)}) collective-permute-start(bf16[320,1792]{1,0:T(8,128)(2,1)} %get-tuple-element.157), channel_id=1, source_target_pairs={{0,4},{1,5},{6,2},{7,3},{8,12},{9,13},{14,10},{15,11},{16,20},{17,... | collective-permute-start | bytes 3440648 | tf_op jit(solution)/shard_map/ppermute | solution.py:65
  (13 other events, 54.2 us)

commit v5 on v4

--- a/solution.py
+++ b/solution.py
@@ -10,7 +10,7 @@
 
 HEAD_DIM = 80
 HALF = HEAD_DIM // 2
-QUERY_BLOCK = 128
+QUERY_BLOCK = 256
 KEY_BLOCK = 256
 MASKED = -1e30
 VMEM_LIMIT = 48 * 1024 * 1024
@@ -76,6 +76,11 @@
     def to_low(self, array, step):
         return self.move(array, lambda p, c, th, tl: (p, c, th, (tl + step) % self.low))
 
+    def home_to_low(self, array, step):
+        return self.move(
+            array, lambda p, c, th, tl: (p, c, th, (tl + step) % self.low) if c == th else None
+        )
+
     def cross(self, array):
         return self.move(
             array, lambda p, c, th, tl: (p, 1 - c, 1 - th, tl) if c != th else None
@@ -101,38 +106,39 @@
         return lax.dynamic_slice_in_dim(array, index * rows, rows, 0)
 
     def plane_moves(self, partial):
-        rows, columns = 2 * partial.shape[0] // self.dp_count, partial.shape[1]
-
-        def unit(step):
-            return lax.dynamic_slice(partial, ((self.p ^ step) * rows, 0), (rows, columns))
-
-        return unit(0), [self.to_chip(unit(step), step) for step in range(self.chips - 1, 0, -1)]
-
-    def plane_sum(self, own, moves):
-        total = own.astype(jnp.float32)
-        for arrived in moves:
-            total = total + arrived.astype(jnp.float32)
-        rows = own.shape[0] // 2
-        sums = [total[:rows], total[rows:]]
-        mine = jnp.where(self.c == 0, sums[0], sums[1])
-        other = jnp.where(self.c == 0, sums[1], sums[0])
-        leaving = jnp.stack(
-            [jnp.where(self.home, other, mine).astype(jnp.bfloat16), other.astype(jnp.bfloat16)]
-        )
-        return mine, leaving
-
-    def pair_rows(self, partial):
-        return [
-            self.quarter_rows(partial, step, 0).astype(jnp.float32)
-            + self.to_core(self.quarter_rows(partial, step, 1)).astype(jnp.float32)
-            for step in range(self.low)
+        rows, columns = partial.shape[0] // self.dp_count, partial.shape[1]
+
+        def half(step, which):
+            start = ((self.p ^ step) * 2 + which) * rows
+            return lax.dynamic_slice(partial, (start, 0), (rows, columns))
+
+        if self.chips == 4:
+            return half, [
+                self.to_chip(jnp.stack([half(3, 0), half(1, 0)]), 1),
+                self.to_chip(jnp.stack([half(3, 1), half(2, 1)]), 2),
+            ]
+        return half, [
+            self.to_chip(jnp.stack([half(step, 0), half(step, 1)]), step) for step in range(1, self.chips)
         ]
 
-    def sum_rows(self, pairs):
-        total = pairs[0]
-        for step in range(1, self.low):
-            total = total + self.to_low(pairs[step].astype(jnp.bfloat16), step).astype(jnp.float32)
-        return total
+    def plane_sum(self, half, moves):
+        def wide(value):
+            return value.astype(jnp.float32)
+
+        if self.chips == 4:
+            by_x, by_y = moves
+            first = self.to_chip((wide(half(2, 0)) + wide(by_x[0])).astype(jnp.bfloat16), 2)
+            second = self.to_chip((wide(half(1, 1)) + wide(by_y[0])).astype(jnp.bfloat16), 1)
+            parts = [[half(0, 0), by_x[1], first], [half(0, 1), by_y[1], second]]
+        else:
+            parts = [[half(0, which)] + [arrived[which] for arrived in moves] for which in range(2)]
+
+        def total(which):
+            return sum(wide(jnp.where(which == 0, one, two)) for one, two in zip(*parts))
+
+        mine, other = total(self.c), total(1 - self.c)
+        low = other.astype(jnp.bfloat16)
+        return mine, jnp.where(self.home, low, mine.astype(jnp.bfloat16)), low
 
 
 def project_kernel(heads, tokens_ref, gain_ref, weight_ref, cosine_ref, sine_ref, normed_ref, out_ref, root_ref):
@@ -667,14 +673,14 @@
 
 
 class RowGather:
-    def __init__(self, links, full, rows):
+    def __init__(self, links, full, rows, low_when=None):
         self.links = links
         mine = full.at[pl.ds(links.quarter * rows, rows)]
         self.to_core = links.copy(mine, mine, links.core_peer())
         self.to_low = []
         self.onward = []
         for step in range(1, links.low):
-            self.to_low.append(links.copy(mine, mine, links.low_peer(step)))
+            self.to_low.append(links.copy(mine, mine, links.low_peer(step), low_when))
             came = (links.tl + links.low - step) % links.low
             block = full.at[pl.ds((links.c * links.low + came) * rows, rows)]
             self.onward.append(links.copy(block, block, links.core_peer()))
@@ -691,6 +697,9 @@
 
     def finish(self):
         self.to_core.arrived()
+        self.finish_onward()
+
+    def finish_onward(self):
         for item in self.onward:
             item.arrived()
 
@@ -989,11 +998,11 @@
 
 
 class TurnScatter:
-    def __init__(self, links, mine, leaving, result, turned):
+    def __init__(self, links, mine, first, second, result, turned):
         self.links, self.mine, self.result, self.turned = links, mine, result, turned
         self.rows = mine.shape[0]
-        self.first = links.copy(leaving.at[0], turned.at[0], links.back_peer())
-        self.second = links.copy(leaving.at[1], turned.at[1], links.cross_peer(), links.away)
+        self.first = links.copy(first, turned.at[0], links.back_peer())
+        self.second = links.copy(second, turned.at[1], links.cross_peer(), links.away)
 
     def send_turned(self):
         self.first.start()
@@ -1047,7 +1056,8 @@
     grad_heads,
     gain_parts,
     up_mine,
-    up_leaving,
+    up_first,
+    up_second,
     grad_residual_ref,
     gain_ref,
     input_ref,
@@ -1069,7 +1079,7 @@
     load_own = links.keep(tokens_all.at[pl.ds(links.quarter * rows, rows)], own_ref)
     scatter = RowScatter(links, partial, mine, others, sums, arrivals, rows)
     crossing = links.copy(leaving, crossed, links.cross_peer(), links.away)
-    up = TurnScatter(links, up_mine, up_leaving, up_ref, up_turned)
+    up = TurnScatter(links, up_mine, up_first, up_second, up_ref, up_turned)
     weights = []
     for grad, result, inbox, work in (
         (grad_output, output_ref, output_in, output_work),
@@ -1163,7 +1173,8 @@
     grad_heads,
     gain_parts,
     up_mine,
-    up_leaving,
+    up_first,
+    up_second,
     grad_residual,
     gain,
 ):
@@ -1180,7 +1191,7 @@
     scratch = []
     for block, columns in shapes:
         scratch += weight_scatter_scratch(chips, block, columns)
-    scratch += [pltpu.VMEM(up_leaving.shape, jnp.bfloat16)]
+    scratch += [pltpu.VMEM((2,) + up_mine.shape, jnp.bfloat16)]
     scratch += [pltpu.VMEM((3, most, widest), jnp.bfloat16)]
     scratch += [pltpu.VMEM((rows, width), jnp.bfloat16)] * 3
     scratch += scatter_scratch(low, rows, width)
@@ -1195,7 +1206,7 @@
         + [jax.ShapeDtypeStruct(shape, jnp.float32) for shape in [up_mine.shape] + shapes]
         + [inbox_shape(chips, *shape) for shape in shapes]
         + partials,
-        in_specs=anywhere(7) + in_vmem(4),
+        in_specs=anywhere(7) + in_vmem(5),
         out_specs=in_vmem(4) + anywhere(4),
         scratch_shapes=scratch + semaphores(96, 24),
         compiler_params=link_params(3),
@@ -1209,7 +1220,8 @@
         grad_heads,
         gain_parts,
         up_mine,
-        up_leaving,
+        up_first,
+        up_second,
         grad_residual,
         gain,
     )[:4]
@@ -1286,6 +1298,7 @@
     partial,
     tokens_all,
     cot,
+    cot_low,
     up,
     up_turned,
     up_crossed,
@@ -1301,7 +1314,7 @@
     rows = cot.shape[0]
     scatter = RowScatter(links, partial, mine, others, sums, arrivals, rows)
     gather_normed = RowGather(links, normed_all, rows)
-    gather_cot = RowGather(links, cot_all, rows)
+    gather_cot = RowGather(links, cot_all, rows, links.away)
     gate_gather = WeightGather(links, up, gate_full)
     up_gather = WeightGather(links, up, up_full)
     down_gather = WeightGather(links, down, down_full)
@@ -1315,11 +1328,20 @@
         links.keep(up_turned, here, links.away),
         links.keep(up_crossed, beside, links.away),
     ]
+    gate_places = [links.chip(step) * 2 * shard for step in (0,) + links.chip_steps()]
     gate_placements = [
-        links.keep(unit, gate_full.at[pl.ds(links.chip(step) * 2 * shard, 2 * shard)])
-        for step, unit in zip((0,) + links.chip_steps(), (gate_unit,) + tuple(gate_units))
+        links.keep(unit, gate_full.at[pl.ds(at, unit.shape[0])])
+        for at, unit in zip(gate_places, (gate_unit,) + tuple(gate_units))
     ]
     cot_crossing = links.copy(cot, cot_all.at[pl.ds(links.tensor_index * rows, rows)], links.cross_peer(), links.away)
+    cot_placements = [
+        links.keep(
+            cot_low.at[step - 1],
+            cot_all.at[pl.ds((links.c * links.low + (links.tl + links.low - step) % links.low) * rows, rows)],
+            links.home,
+        )
+        for step in range(1, links.low)
+    ]
     cot_staying = links.keep(cot, cot_all.at[quarter], links.home)
     load = links.keep(tokens_all.at[quarter], own)
     store = links.keep(normed, normed_all.at[quarter])
@@ -1339,6 +1361,8 @@
     up_gather.spread_unit()
     down_gather.turn()
     cot_staying.start()
+    for item in cot_placements:
+        item.start()
     load.done()
 
     def use(span, total):
@@ -1358,6 +1382,8 @@
     gate_gather.finish()
     gather_normed.pass_on()
     cot_staying.done()
+    for item in cot_placements:
+        item.done()
     cot_crossing.arrived()
     gather_cot.start()
     up_gather.finish()
@@ -1378,7 +1404,7 @@
 
 
 def middle(
-    dp_count, tensor_count, partial, tokens_all, cot, up, up_turned, up_crossed, down, gate_unit, gate_units, gain
+    dp_count, tensor_count, partial, tokens_all, cot, cot_low, up, up_turned, up_crossed, down, gate_unit, gate_units, gain
 ):
     rows, width = cot.shape
     low = tensor_count // 2
@@ -1399,14 +1425,14 @@
             jax.ShapeDtypeStruct((rows * tensor_count, up.shape[1]), jnp.float32),
             jax.ShapeDtypeStruct((rows * tensor_count, up.shape[1]), jnp.bfloat16),
         ],
-        in_specs=anywhere(2) + in_vmem(len(gate_units) + 7),
+        in_specs=anywhere(2) + in_vmem(len(gate_units) + 8),
         out_specs=in_vmem(1) + anywhere(8),
         scratch_shapes=[pltpu.VMEM((rows, width), jnp.bfloat16)] * 2
         + scatter_scratch(low, rows, width)
         + semaphores(64, 24),
         compiler_params=link_params(1),
         name="middle",
-    )(partial, tokens_all, cot, up, up_turned, up_crossed, down, gate_unit, *gate_units, gain)
+    )(partial, tokens_all, cot, cot_low, up, up_turned, up_crossed, down, gate_unit, *gate_units, gain)
 
 
 def turn_back_kernel(
@@ -1433,6 +1459,8 @@
     grad_gate,
     grad_up,
     down_part,
+    pair_own,
+    pair_low,
     own,
     low_grad,
     turned,
@@ -1453,6 +1481,12 @@
     gate = WeightScatter(links, grad_gate, gate_ref, gate_in, turned, gate_added, gate_turning, stage)
     down.total = gate.total = total_ref
     links.drop([gate.first, gate.second])
+    low = links.low
+    half = low * residual_ref.shape[0]
+    swap_layer = links.copy(down_part.at[pl.ds((1 - links.c) * half, half)], others, links.core_peer())
+    load_layer = links.keep(down_part.at[pl.ds(links.c * half, half)], mine)
+    keep_own = links.keep(low_grad, pair_own)
+    keep_low = [links.keep(sums.at[step - 1], pair_low.at[step - 1]) for step in range(1, low)]
     scatter = RowScatter(links, partial, mine, others, sums, arrivals, rows)
     gather = RowGather(links, grad_rows, rows)
     quarter = pl.ds(links.quarter * rows, rows)
@@ -1509,11 +1543,38 @@
     product(normed_ffn, up_signal, grad_up, 0, 0, 512, 1024)
     gather.pass_on()
     product(hidden, down_full, down_part, 1, 1, 512, 1024)
+    gather.to_core.arrived()
+    swap_layer.start()
+    load_layer.start()
     gate.arrived("direct")
     gate.arrived("summed")
     gate.reduce()
+    for item in scatter.sends:
+        item.sent()
+    links.drop(scatter.sends)
+    load_layer.done()
+    swap_layer.arrived()
+    for step in range(low):
+        base = ((links.tl + step) % low) * rows
+
+        @pl.loop(0, rows // CHUNK)
+        def _(i, base=base, step=step):
+            at = pl.multiple_of(i * CHUNK, CHUNK)
+            span = pl.ds(pl.multiple_of(base + at, CHUNK), CHUNK)
+            total = (mine[span].astype(jnp.float32) + others[span].astype(jnp.float32)).astype(jnp.bfloat16)
+            if step:
+                sums[step - 1, pl.ds(at, CHUNK)] = total
+            else:
+                low_grad[pl.ds(at, CHUNK)] = total
+
+    keep_own.start()
+    for item in keep_low:
+        item.start()
     down.finish()
-    gather.finish()
+    gather.finish_onward()
+    keep_own.done()
+    for item in keep_low:
+        item.done()
     links.leave()
 
 
@@ -1549,9 +1610,11 @@
             grad,
             grad,
             jax.ShapeDtypeStruct((rows * tensor_count, width), jnp.bfloat16),
+            jax.ShapeDtypeStruct((rows, width), jnp.bfloat16),
+            jax.ShapeDtypeStruct((low - 1, rows, width), jnp.bfloat16),
         ],
         in_specs=anywhere(7) + in_vmem(2),
-        out_specs=in_vmem(5) + anywhere(7),
+        out_specs=in_vmem(5) + anywhere(9),
         scratch_shapes=[pltpu.VMEM((rows, width), jnp.bfloat16)] * 2
         + weight_scatter_scratch(chips, block, columns)
         + [
@@ -1682,6 +1745,8 @@
     up_crossed = place.cross(late_up)
     steps = (1, 2) if place.chips == 4 else tuple(range(1, place.chips))
     gate_units = [place.to_chip(gate_unit, step) for step in steps]
+    late_cot = after(cotangent, tokens_all)
+    cot_low = jnp.stack([place.home_to_low(late_cot, step) for step in range(1, place.low)])
 
     numbers = jnp.concatenate([storage_order, pad_mask, lengths[0]])
     numbers = jnp.where(place.home, numbers, place.to_core(numbers))
@@ -1719,6 +1784,7 @@
         contract(attended_stored, output_turned, 1, 1, jnp.bfloat16),
         tokens_all,
         cotangent,
+        cot_low,
         up_shard,
         up_turned,
         up_crossed,
@@ -1749,14 +1815,13 @@
         feedforward_scale,
     )
     grad_residual, feedforward_part, down_grad, gate_grad, gate_turning, grad_rows = turned_back[:6]
-    up_part, down_part = turned_back[10:]
-    up_own, up_moves = place.plane_moves(up_part)
+    up_part, pair_own, pair_low = turned_back[10], turned_back[12], turned_back[13]
+    up_half, up_moves = place.plane_moves(up_part)
     gate_arrived = place.away_to_home(gate_turning)
 
-    pairs = place.pair_rows(down_part)
+    layer_moves = [place.to_low(pair_low[step - 1], step) for step in range(1, place.low)]
     grad_attended = contract(grad_rows, output_turned, 1, 0, jnp.bfloat16)
     grad_attended = contract(to_sequence, grad_attended, 1, 0, jnp.bfloat16)
-    grad_attended = after(grad_attended, *pairs)
     grad_query, grad_rest = attend_back(
         first_blocks,
         heads_all,
@@ -1770,10 +1835,14 @@
         kv_heads,
         group,
     )
-    layer_own = after(residual, grad_query) + place.sum_rows(pairs)
+    layer_own = after(residual, grad_query) + pair_own.astype(jnp.float32)
+    for arrived in layer_moves:
+        layer_own = layer_own + arrived.astype(jnp.float32)
     spare = jnp.zeros((count, first_padded - head_columns), jnp.bfloat16)
-    up_mine, up_leaving = place.plane_sum(after(up_own, grad_query), up_moves)
-    sequence_grads = after(jnp.concatenate([grad_query, grad_rest, spare], axis=1), layer_own)
+    sequence_grads, _, *up_moves = lax.optimization_barrier(
+        (jnp.concatenate([grad_query, grad_rest, spare], axis=1), layer_own, *up_moves)
+    )
+    up_mine, up_first, up_second = place.plane_sum(up_half, up_moves)
     grad_heads = contract(to_storage, sequence_grads, 1, 0, jnp.bfloat16)
     grad_normed_part = contract(grad_heads, first_weight, 1, 1)
     tokens_wide = tokens_all.astype(jnp.float32)
@@ -1797,7 +1866,8 @@
         grad_heads,
         gain_parts,
         up_mine,
-        up_leaving,
+        up_first,
+        up_second,
         grad_residual,
         attention_scale,
     )

time: 1090 us -> 1060 us (0.972)
  Pallas kernels: 914 us -> 878 us
  waiting for transfers between devices: 0.04 us -> 11.6 us
    add x3 -> x0, other arithmetic: 13.6 us -> none  [the longest x2 7.39 us: pair_rows(): self.quarter_rows(partial, step, 0).astype(jnp.float32)]
    ppermute x14, waiting for transfers between devices: 0.04 us -> 11.6 us  [move(): return lax.ppermute(array, AXES, pairs)]
  transfers between devices with their start and end apart: 14 -> 14, of which waited for: 0 -> 3; matrix products, arithmetic and copies ran while one was open for 10% -> 8% of each run, Pallas kernels for 29% -> 28%
where the time goes in v5:
time: 1060 us; the launch traced here: 1050 us
  Pallas kernels  878 us (83%)
  matrix products  54.8 us (5%)
  starting transfers between devices  39.4 us (4%)
  other arithmetic  33.7 us (3%)
  local copies, waits for them, and re-layouts  32.2 us (3%)
  waiting for transfers between devices  11.6 us (1%)
    pallas_call x1, Pallas kernels, middle(): pl.pallas_call(functools.partial(middle_kernel, dp_count, tensor_count, l...  202 us
    pallas_call x1, Pallas kernels, tail(): pl.pallas_call(functools.partial(tail_kernel, dp_count, tensor_count, gai...  186 us
    pallas_call x1, Pallas kernels, turn_back(): pl.pallas_call(functools.partial(turn_back_kernel, dp_count, tensor_count...  179 us
    pallas_call x1, Pallas kernels, gather_first(): pl.pallas_call(functools.partial(gather_first_kernel, dp_count, tensor_co...  141 us
    pallas_call x1, Pallas kernels, hidden_back(): pl.pallas_call(hidden_back_kernel, out_shape=[signal, signal, jax.ShapeDt...  64.5 us
    dot_general x6, matrix products, contract(): lax.dot_general(left, right, (((left_dim,), (right_dim,)), ((), ())), pre...  54.8 us
    pallas_call x1, Pallas kernels, attend_back(): pl.pallas_call(functools.partial(attend_back_kernel, kv_heads, group), gr...  52.2 us
    ppermute x14, starting transfers between devices, move(): return lax.ppermute(array, AXES, pairs)  39.4 us
  transfers between devices with their start and end apart: 14, of which 3 were waited for; matrix products, arithmetic and copies ran while one was open for 8% of the time, Pallas kernels for 28%

profile of v5, /device:TPU:0, one launch (start us, length us, event | category | flops | bytes accessed | tf_op | source)
XLA Modules:
  0.0 1051.6 jit_solution(13917851215784038320)
XLA Ops:
  8.0 140.6 %gather_first.1 = (bf16[1536,2560]{1,0:T(8,128)(2,1)}, bf16[2560,1024]{1,0:T(8,128)(2,1)}, bf16[2560,640]{1,0:T(8,128)(2,1)}, bf16[640,1792]{1,0:T(8,128)(2,1)}) custom-call(bf16[384,2560]{1,0:T(8,128)(2,1)} %tokens.1, bf16[320,1024]{1,0:T(8,128)(2,1)} %pad.18.first, bf16[320,640]{1,0:T(8,128)(2,1)} %bitcast.62, bf16[320,1792]{1,0:T(8,128)(2,1)} %pad.19.gate), custom_call_target="tpu_custom_call" | custom-call | tf_op jit(solution)/shard_map/gather_first/pallas_call | solution.py:1278
  150.3 14.7 %collective-permute-start.2 = (bf16[320,1792]{1,0:T(8,128)(2,1)S(1)}, bf16[320,1792]{1,0:T(8,128)(2,1)}, u32[]{:S(2)}, u32[]{:S(2)}) collective-permute-start(bf16[320,1792]{1,0:T(8,128)(2,1)S(1)} %pad.20.up), channel_id=1, source_target_pairs={{0,2},{1,3},{2,6},{3,7},{4,0},{5,1},{6,4},{7,5},{8,10},{9,11},{10,... | collective-permute-start | bytes 3440648 | tf_op jit(solution)/shard_map/ppermute | solution.py:65
  172.9 5.7 collective-permute-start.1
  181.1 21.5 %project.1 = (bf16[1536,2560]{1,0:T(8,128)(2,1)}, bf16[1536,960]{1,0:T(8,128)(2,1)S(1)}, f32[1536,1]{1,0:T(8,128)S(1)}) custom-call(bf16[1536,2560]{1,0:T(8,128)(2,1)} %get-tuple-element.55.tokens_ref.tokens_all, f32[1,2560]{1,0:T(1,128)S(1)} %reshape.103.gain_ref, bf16[2560,1024]{1,0:T(8,128)(2,1)} %get-tuple-element.56.weight_ref, ...), custom_call_target="tpu_custom_call" | custom-call | flops 8053063680 | bytes 20971520 | tf_op jit(solution)/shard_map/project/pallas_call | solution.py:165
  202.6 6.4 fusion.9.query_ref.all_ref
  211.7 32.7 %attend.1 = (bf16[1536,640]{1,0:T(8,128)(2,1)S(1)}, f32[8,1536]{1,0:T(8,128)S(1)}) custom-call(s32[6]{0:T(128)S(1)} %and_select_fusion.first_ref, bf16[1536,960]{1,0:T(8,128)(2,1)S(1)} %copy-done.2, bf16[1536,960]{1,0:T(8,128)(2,1)S(1)} %copy-done.2, s32[1,1536]{1,0:T(1,128)S(1)} %broadcast_in_dim.51.start_ref, s32[1536,1]{1,0:T(8,128)S(1)} %broadcast_in_dim.56.pad_ref), custom_call_target="tpu_custom_call" | custom-call | flops 49999998976 | bytes 1474560 | tf_op jit(solution)/shard_map/attend/pallas_call | solution.py:276
  244.5 4.3 fusion.10.attended
  248.8 8.5 convolution_convert_fusion.partial
  257.4 201.9 %middle.1 = (f32[384,2560]{1,0:T(8,128)}, bf16[1536,2560]{1,0:T(8,128)(2,1)}, bf16[1536,2560]{1,0:T(8,128)(2,1)}, bf16[2560,1792]{1,0:T(8,128)(2,1)}, bf16[2560,...) custom-call(bf16[1536,2560]{1,0:T(8,128)(2,1)} %convolution_convert_, ...), custom_call_target="tpu_custom_call" | custom-call | tf_op jit(solution)/shard_map/middle/pallas_call | solution.py:1415
  459.3 64.5 %hidden_back.1 = (bf16[1536,1792]{1,0:T(8,128)(2,1)}, bf16[1536,1792]{1,0:T(8,128)(2,1)}, bf16[1536,2560]{1,0:T(8,128)(2,1)}) custom-call(bf16[1536,2560]{1,0:T(8,128)(2,1)} %get-tuple-element.65.cot_all, bf16[2560,1792]{1,0:T(8,128)(2,1)} %get-tuple-element.66.down_full, f32[1536,1792]{1,0:T(8,128)} %get-tuple-element.67.gate_values, ...), custom_call_target="tpu_custom_call" | custom-call | flops 42278584320 | bytes 42278584 | tf_op jit(solution)/shard_map/hidden_back/pallas_call | solution.py:1665
  523.8 179.2 %turn_back.1 = (f32[384,2560]{1,0:T(8,128)}, f32[1,2560]{1,0:T(1,128)}, f32[320,1792]{1,0:T(8,128)}, f32[320,1792]{1,0:T(8,128)}, bf16[2,320,1792]{2,1,0:T(8,128...) custom-call(bf16[1536,2560]{1,0:T(8,128)(2,1)} %get-tuple-element.71, ...), custom_call_target="tpu_custom_call" | custom-call | tf_op jit(solution)/shard_map/turn_back/pallas_call | solution.py:1598
  703.0 15.4 %fusion.11.grad_ref = bf16[1536,640]{1,0:T(8,128)(2,1)} fusion(s32[1536]{0:T(1024)S(1)} %slice.84, bf16[1536,2560]{1,0:T(8,128)(2,1)} %get-tuple-element.76.grad_rows, bf16[2560,640]{1,0:T(8,128)(2,1)} %get-tuple-element.59), kind=kOutput, calls=%fused_computation.18 | convolution fusion | flops 8057389056 | bytes 13113344 | tf_op jit(solution)/shard_map/dot_general | solution.py:25
  729.9 52.2 %attend_back.1 = (bf16[1536,640]{1,0:T(8,128)(2,1)S(1)}, bf16[1536,320]{1,0:T(8,128)(2,1)S(1)}) custom-call(s32[6]{0:T(128)S(1)} %and_select_fusion.first_ref, bf16[1536,960]{1,0:T(8,128)(2,1)} %fusion.9.query_ref.all_ref, bf16[1536,960]{1,0:T(8,128)(2,1)} %fusion.9.query_ref.all_ref, s32[1,1536]{1,0:T(1,128)S(1)} %broadcast_in_dim.51.start_ref, ...), custom_call_target="tpu_custom_call" | custom-call | flops 49999998976 | bytes 1474560 | tf_op jit(solution)/shard_map/attend_back/pallas_call | solution.py:412
  784.4 3.9 collective-permute-done.6
  788.3 3.6 fusion.22
  795.8 3.6 collective-permute-start.13
  799.5 6.7 fusion.8.grad_heads
  806.2 4.3 fusion.16
  813.3 13.5 %multiply_reduce_fusion = (f32[2560]{0:T(1024)S(1)}, bf16[1536,2560]{1,0:T(8,128)(2,1)}) fusion(bf16[1536,2560]{1,0:T(8,128)(2,1)S(1)} %bitcast.58, f32[1536]{0:T(1024)S(1)} %copy-done.19, bf16[1536,1024]{1,0:T(8,128)(2,1)} %fusion.8.grad_heads, bf16[2560,1024]{1,0:T(8,128)(2,1)} %get-tuple-element.56.weight_ref), kind=kOutput, calls=%fused_computation | convolution fusion | flops 8072721920 | bytes 24133632 | tf_op jit(solution)/shard_map/dot_general | solution.py:25
  831.1 6.1 collective-permute-done.11
  838.8 6.7 convert_select_fusion.1
  845.6 186.0 %tail.1 = (f32[384,2560]{1,0:T(8,128)}, f32[320,1792]{1,0:T(8,128)}, f32[320,640]{1,0:T(8,128)}, f32[320,1024]{1,0:T(8,128)}, bf16[6,320,640]{2,1,0:T(8,128)(2,1...) custom-call(bf16[1536,2560]{1,0:T(8,128)(2,1)} %get-tuple-element.84.partial, ...), custom_call_target="tpu_custom_call" | custom-call | tf_op jit(solution)/shard_map/tail/pallas_call | solution.py:1203
  1038.4 3.8 fusion.12
  1042.2 4.2 convert_select_fusion
  (121 shorter events, 60.3 us)
Async XLA Ops:
  6.7 143.6 %copy-start.5 = (bf16[320,1792]{1,0:T(8,128)(2,1)}, bf16[320,1792]{1,0:T(8,128)(2,1)S(1)}, u32[]{:S(2)}) copy-start(bf16[320,1792]{1,0:T(8,128)(2,1)S(1)} %pad.20.up) | copy-start | bytes 3440644
  8.0 160.0 %copy-start.16 = (s32[1536]{0:T(1024)S(1)}, s32[1536]{0:T(1024)}, u32[]{:S(2)}) copy-start(s32[1536]{0:T(1024)} %param.28) | copy-start | bytes 18436
  8.0 160.0 %copy-start.17 = (s32[1536]{0:T(1024)S(1)}, s32[1536]{0:T(1024)}, u32[]{:S(2)}) copy-start(s32[1536]{0:T(1024)} %param.27) | copy-start | bytes 18436
  8.0 160.0 %copy-start.21 = (s32[1,3]{1,0:T(1,128)S(1)}, s32[1,3]{1,0:T(1,128)}, u32[]{:S(2)}) copy-start(s32[1,3]{1,0:T(1,128)} %param.26) | copy-start | bytes 40
  8.0 162.5 %copy-start.13 = (bf16[1728,320]{0,1:T(8,128)(2,1)S(1)}, bf16[1728,320]{0,1:T(8,128)(2,1)}, u32[]{:S(2)}) copy-start(bf16[1728,320]{0,1:T(8,128)(2,1)} %param.24) | copy-start | bytes 3317764
  148.5 108.8 %collective-permute-start.3 = (bf16[320,1792]{1,0:T(8,128)(2,1)S(1)}, bf16[320,1792]{1,0:T(8,128)(2,1)}, u32[]{:S(2)}, u32[]{:S(2)}) collective-permute-start(bf16[320,1792]{1,0:T(8,128)(2,1)S(1)} %pad.20.up), channel_id=1, source_target_pairs={{2,4},{3,5},{4,2},{5,3},{10,12},{11,13},{12,10},{13,11},{18,20},{1... | collective-permute-start | bytes 3440648 | tf_op jit(solution)/shard_map/ppermute | solution.py:65
  150.3 107.1 %collective-permute-start.2 = (bf16[320,1792]{1,0:T(8,128)(2,1)S(1)}, bf16[320,1792]{1,0:T(8,128)(2,1)}, u32[]{:S(2)}, u32[]{:S(2)}) collective-permute-start(bf16[320,1792]{1,0:T(8,128)(2,1)S(1)} %pad.20.up), channel_id=1, source_target_pairs={{0,2},{1,3},{2,6},{3,7},{4,0},{5,1},{6,4},{7,5},{8,10},{9,11},{10,... | collective-permute-start | bytes 3440648 | tf_op jit(solution)/shard_map/ppermute | solution.py:65
  165.0 92.4 %collective-permute-start.5 = (bf16[640,1792]{1,0:T(8,128)(2,1)}, bf16[640,1792]{1,0:T(8,128)(2,1)}, u32[]{:S(2)}, u32[]{:S(2)}) collective-permute-start(bf16[640,1792]{1,0:T(8,128)(2,1)} %get-tuple-element.62.gate_unit), channel_id=1, source_target_pairs={{0,16},{1,17},{2,18},{3,19},{4,20},{5,21},{6,22},{7,23},{8,24},{9,... | collective-permute-start | bytes 6881288 | tf_op jit(solution)/shard_map/ppermute | solution.py:65
  166.5 90.9 %collective-permute-start.4 = (bf16[640,1792]{1,0:T(8,128)(2,1)}, bf16[640,1792]{1,0:T(8,128)(2,1)}, u32[]{:S(2)}, u32[]{:S(2)}) collective-permute-start(bf16[640,1792]{1,0:T(8,128)(2,1)} %get-tuple-element.62.gate_unit), channel_id=1, source_target_pairs={{0,8},{1,9},{2,10},{3,11},{4,12},{5,13},{6,14},{7,15},{8,0},{9,1},... | collective-permute-start | bytes 6881288 | tf_op jit(solution)/shard_map/ppermute | solution.py:65
  168.0 4.9 collective-permute-start
  172.2 30.4 %copy-start = (f32[1,2560]{1,0:T(1,128)}, f32[1,2560]{1,0:T(1,128)S(1)}, u32[]{:S(2)}) copy-start(f32[1,2560]{1,0:T(1,128)S(1)} %reshape.103.gain_ref) | copy-start | bytes 30724
  172.9 84.5 %collective-permute-start.1 = (bf16[384,2560]{1,0:T(8,128)(2,1)}, bf16[384,2560]{1,0:T(8,128)(2,1)}, u32[]{:S(2)}, u32[]{:S(2)}) collective-permute-start(bf16[384,2560]{1,0:T(8,128)(2,1)} %cot.1), channel_id=1, source_target_pairs={{0,1},{1,0},{6,7},{7,6},{8,9},{9,8},{14,15},{15,14},{16,17},{17,16... | collective-permute-start | bytes 5898248 | tf_op jit(solution)/shard_map/ppermute | solution.py:65
  718.4 69.9 %collective-permute-start.6 = (bf16[384,2560]{1,0:T(8,128)(2,1)}, bf16[384,2560]{1,0:T(8,128)(2,1)S(1)}, u32[]{:S(2)}, u32[]{:S(2)}) collective-permute-start(bf16[384,2560]{1,0:T(8,128)(2,1)} %bitcast.67), channel_id=1, source_target_pairs={{0,1},{1,0},{2,3},{3,2},{4,5},{5,4},{6,7},{7,6},{8,9},{9,8},{10,11... | collective-permute-start | bytes 5898248 | tf_op jit(solution)/shard_map/ppermute | solution.py:65
  720.6 73.4 %collective-permute-start.12 = (bf16[2,320,1792]{2,1,0:T(8,128)(2,1)}, bf16[2,320,1792]{2,1,0:T(8,128)(2,1)S(1)}, u32[]{:S(2)}, u32[]{:S(2)}) collective-permute-start(bf16[2,320,1792]{2,1,0:T(8,128)(2,1)} %get-tuple-element.95), channel_id=1, source_target_pairs={{2,0},{3,1},{4,6},{5,7},{10,8},{11,9},{12,14},{13,15},{18,16},{19,... | collective-permute-start | bytes 6881288 | tf_op jit(solution)/shard_map/ppermute | solution.py:65
  726.3 73.2 %collective-permute-start.8 = (bf16[2,320,1792]{2,1,0:T(8,128)(2,1)}, bf16[2,320,1792]{2,1,0:T(8,128)(2,1)}, u32[]{:S(2)}, u32[]{:S(2)}) collective-permute-start(bf16[2,320,1792]{2,1,0:T(8,128)(2,1)} %pad_maximum_fusion), channel_id=1, source_target_pairs={{0,8},{1,9},{2,10},{3,11},{4,12},{5,13},{6,14},{7,15},{8,0},{9,1},... | collective-permute-start | bytes 6881288 | tf_op jit(solution)/shard_map/ppermute | solution.py:65
  729.0 70.5 %collective-permute-start.9 = (bf16[2,320,1792]{2,1,0:T(8,128)(2,1)}, bf16[2,320,1792]{2,1,0:T(8,128)(2,1)}, u32[]{:S(2)}, u32[]{:S(2)}) collective-permute-start(bf16[2,320,1792]{2,1,0:T(8,128)(2,1)} %pad_maximum_fusion.1), channel_id=1, source_target_pairs={{0,16},{1,17},{2,18},{3,19},{4,20},{5,21},{6,22},{7,23},{8,24},{9,... | collective-permute-start | bytes 6881288 | tf_op jit(solution)/shard_map/ppermute | solution.py:65
  729.9 52.2 %copy-start.7 = (f32[320,1792]{1,0:T(8,128)S(1)}, f32[320,1792]{1,0:T(8,128)}, u32[]{:S(2)}) copy-start(f32[320,1792]{1,0:T(8,128)} %get-tuple-element.98) | copy-start | bytes 6881284
  791.9 250.4 %collective-permute-start.7 = (bf16[384,2560]{1,0:T(8,128)(2,1)}, bf16[384,2560]{1,0:T(8,128)(2,1)}, u32[]{:S(2)}, u32[]{:S(2)}) collective-permute-start(bf16[384,2560]{1,0:T(8,128)(2,1)} %get-tuple-element.152), channel_id=1, source_target_pairs={{2,4},{3,5},{4,2},{5,3},{10,12},{11,13},{12,10},{13,11},{18,20},{1... | collective-permute-start | bytes 5898248 | tf_op jit(solution)/shard_map/ppermute | solution.py:65
  794.4 18.9 %slice-start = ((s8[7864320]{0:T(1024)(128)(4,1)}), s8[4194304]{0:T(1024)(128)(4,1)S(1)}, s32[]{:S(2)}) async-start(s8[7864320]{0:T(1024)(128)(4,1)} %bitcast.57), calls=%async_computation | async-start | bytes 8388608
  795.8 242.6 %collective-permute-start.13 = (bf16[320,1792]{1,0:T(8,128)(2,1)}, bf16[320,1792]{1,0:T(8,128)(2,1)}, u32[]{:S(2)}, u32[]{:S(2)}) collective-permute-start(bf16[320,1792]{1,0:T(8,128)(2,1)} %get-tuple-element.162), channel_id=1, source_target_pairs={{0,4},{1,5},{6,2},{7,3},{8,12},{9,13},{14,10},{15,11},{16,20},{17,... | collective-permute-start | bytes 3440648 | tf_op jit(solution)/shard_map/ppermute | solution.py:65
  799.5 13.7 %slice-start.1 = ((s8[7864320]{0:T(1024)(128)(4,1)}), s8[3670016]{0:T(1024)(128)(4,1)S(1)}, s32[]{:S(2)}) async-start(s8[7864320]{0:T(1024)(128)(4,1)} %bitcast.57), calls=%async_computation.1 | async-start | bytes 7340032
  810.5 26.7 %collective-permute-start.11 = (bf16[320,1792]{1,0:T(8,128)(2,1)}, bf16[320,1792]{1,0:T(8,128)(2,1)S(1)}, u32[]{:S(2)}, u32[]{:S(2)}) collective-permute-start(bf16[320,1792]{1,0:T(8,128)(2,1)} %get-tuple-element.156), channel_id=1, source_target_pairs={{0,8},{1,9},{2,10},{3,11},{4,12},{5,13},{6,14},{7,15},{8,0},{9,1},... | collective-permute-start | bytes 3440648 | tf_op jit(solution)/shard_map/ppermute | solution.py:65
  813.2 13.6 %copy-start.18 = (f32[1,2560]{1,0:T(1,128)S(1)}, f32[1,2560]{1,0:T(1,128)}, u32[]{:S(2)}) copy-start(f32[1,2560]{1,0:T(1,128)} %get-tuple-element.87) | copy-start | bytes 30724
  813.2 25.6 %collective-permute-start.10 = (bf16[320,1792]{1,0:T(8,128)(2,1)}, bf16[320,1792]{1,0:T(8,128)(2,1)}, u32[]{:S(2)}, u32[]{:S(2)}) collective-permute-start(bf16[320,1792]{1,0:T(8,128)(2,1)} %get-tuple-element.157), channel_id=1, source_target_pairs={{0,16},{1,17},{2,18},{3,19},{4,20},{5,21},{6,22},{7,23},{8,24},{9,... | collective-permute-start | bytes 3440648 | tf_op jit(solution)/shard_map/ppermute | solution.py:65
  (15 other events, 61.4 us)

commit v6 on v5

--- a/solution.py
+++ b/solution.py
@@ -218,7 +218,7 @@
     step = pl.program_id(0)
     heads = kv_heads * group
     query_rows = query_ref.shape[0]
-    scale = 1.0 / math.sqrt(HEAD_DIM)
+    scale = math.log2(math.e) / math.sqrt(HEAD_DIM)
 
     @pl.when(step == 0)
     def _():
@@ -241,8 +241,8 @@
             bias = jnp.concatenate([bias] * group, axis=1)
             scores = times(key_heads[k, pl.ds(at, KEY_BLOCK), :], queries, 1, 1) * scale + bias
             new_top = jnp.maximum(top, jnp.max(scores, axis=0, keepdims=True))
-            weight = jnp.exp(scores - new_top)
-            shrink = jnp.exp(top - new_top)
+            weight = jnp.exp2(scores - new_top)
+            shrink = jnp.exp2(top - new_top)
             total = total * shrink + jnp.sum(weight, axis=0, keepdims=True)
             mixed = mixed * shrink + times(
                 value_turned[k, :, pl.ds(at, KEY_BLOCK)], weight.astype(jnp.bfloat16), 1, 0
@@ -261,7 +261,7 @@
             ),
         )
         mixed = mixed / total
-        log_total = top + jnp.log(total)
+        log_total = top + jnp.log2(total)
         for g in range(group):
             span = slice(g * query_rows, (g + 1) * query_rows)
             pieces.append(mixed[:, span].T)
@@ -366,8 +366,8 @@
             span = pl.ds(at, KEY_BLOCK)
             bias = block_bias(at, query_start, start_ref[...], pad_ref[span, :])
             bias = jnp.concatenate([bias] * group, axis=1)
-            scores = times(key_heads[k, span, :], queries, 1, 1) * scale + bias
-            weight = jnp.exp(scores - log_total)
+            scores = times(key_heads[k, span, :], queries, 1, 1) * (scale * math.log2(math.e)) + bias
+            weight = jnp.exp2(scores - log_total)
             grad_weight = times(value_heads[k, span, :], grads, 1, 1)
             grad_scores = (weight * (grad_weight - inner)).astype(jnp.bfloat16)
             grad_values[k, span, :] += times(weight.astype(jnp.bfloat16), grads, 1, 0)
@@ -1109,11 +1109,11 @@
         out_ref[:, : columns - 128] = value[:, : columns - 128].astype(jnp.bfloat16)
         out_ref[:, columns - 128 :] = (value[:, columns - 128 :] + parts_ref[...]).astype(jnp.bfloat16)
 
+    product(grad_rows, attended, grad_output, 0, 0, 512, 1024)
+    output.start("before")
     product(normed, grad_heads, grad_first, 0, 0, 512, 1024, finish, (gain_parts,))
+    output.add_before()
     first.start("before")
-    product(grad_rows, attended, grad_output, 0, 0, 512, 1024)
-    first.add_before()
-    output.start("before")
 
     def use(span, grad_normed):
         own = own_ref[span].astype(jnp.float32)
@@ -1126,9 +1126,12 @@
         input_ref[span] = grad
         leaving[span] = grad.astype(jnp.bfloat16)
 
+    output.arrived("direct")
+    output.arrived("summed")
+    output.turn()
+    first.add_before()
     scatter.collect(use)
     crossing.start()
-    output.add_before()
     first.arrived("direct")
     first.arrived("summed")
     first.turn()
@@ -1141,16 +1144,13 @@
 
         row_loop(rows, body)
 
-    output.arrived("direct")
-    output.arrived("summed")
-    output.turn()
     up.finish()
+    output.finish()
     first.finish()
     width = first_ref.shape[1]
     gains_out[...] = first_ref[:, width - 128 :]
     for item in gain_sends:
         item.start()
-    output.finish()
     for item in gain_sends:
         item.arrived()
     summed = gains_out[...]

time: 1060 us -> 1050 us (level)
  Pallas kernels: 878 us -> 864 us
  transfers between devices with their start and end apart: 14 -> 14, of which waited for: 3 -> 3; matrix products, arithmetic and copies ran while one was open for 8% -> 8% of each run, Pallas kernels for 28% -> 26%
where the time goes in v6:
time: 1050 us
  Pallas kernels  864 us (82%)
  matrix products  54.8 us (5%)
  starting transfers between devices  38.4 us (4%)
  other arithmetic  33.7 us (3%)
  local copies, waits for them, and re-layouts  32.2 us (3%)
  waiting for transfers between devices  20.7 us (2%)
    pallas_call x1, Pallas kernels, middle(): pl.pallas_call(functools.partial(middle_kernel, dp_count, tensor_count, l...  203 us
    pallas_call x1, Pallas kernels, tail(): pl.pallas_call(functools.partial(tail_kernel, dp_count, tensor_count, gai...  184 us
    pallas_call x1, Pallas kernels, turn_back(): pl.pallas_call(functools.partial(turn_back_kernel, dp_count, tensor_count...  182 us
    pallas_call x1, Pallas kernels, gather_first(): pl.pallas_call(functools.partial(gather_first_kernel, dp_count, tensor_co...  141 us
    pallas_call x1, Pallas kernels, hidden_back(): pl.pallas_call(hidden_back_kernel, out_shape=[signal, signal, jax.ShapeDt...  64.5 us
    dot_general x6, matrix products, contract(): lax.dot_general(left, right, (((left_dim,), (right_dim,)), ((), ())), pre...  54.8 us
    pallas_call x1, Pallas kernels, attend_back(): pl.pallas_call(functools.partial(attend_back_kernel, kv_heads, group), gr...  42.3 us
    ppermute x14, starting transfers between devices, move(): return lax.ppermute(array, AXES, pairs)  38.4 us
  transfers between devices with their start and end apart: 14, of which 3 were waited for; matrix products, arithmetic and copies ran while one was open for 8% of the time, Pallas kernels for 26%

profile of v6, /device:TPU:0, one launch (start us, length us, event | category | flops | bytes accessed | tf_op | source)
XLA Modules:
  0.0 1045.5 jit_solution(1591116072575549283)
XLA Ops:
  8.0 140.6 %gather_first.1 = (bf16[1536,2560]{1,0:T(8,128)(2,1)}, bf16[2560,1024]{1,0:T(8,128)(2,1)}, bf16[2560,640]{1,0:T(8,128)(2,1)}, bf16[640,1792]{1,0:T(8,128)(2,1)}) custom-call(bf16[384,2560]{1,0:T(8,128)(2,1)} %tokens.1, bf16[320,1024]{1,0:T(8,128)(2,1)} %pad.18.first, bf16[320,640]{1,0:T(8,128)(2,1)} %bitcast.62, bf16[320,1792]{1,0:T(8,128)(2,1)} %pad.19.gate), custom_call_target="tpu_custom_call" | custom-call | tf_op jit(solution)/shard_map/gather_first/pallas_call | solution.py:1278
  150.3 14.7 %collective-permute-start.2 = (bf16[320,1792]{1,0:T(8,128)(2,1)S(1)}, bf16[320,1792]{1,0:T(8,128)(2,1)}, u32[]{:S(2)}, u32[]{:S(2)}) collective-permute-start(bf16[320,1792]{1,0:T(8,128)(2,1)S(1)} %pad.20.up), channel_id=1, source_target_pairs={{0,2},{1,3},{2,6},{3,7},{4,0},{5,1},{6,4},{7,5},{8,10},{9,11},{10,... | collective-permute-start | bytes 3440648 | tf_op jit(solution)/shard_map/ppermute | solution.py:65
  172.9 5.7 collective-permute-start.1
  181.1 21.5 %project.1 = (bf16[1536,2560]{1,0:T(8,128)(2,1)}, bf16[1536,960]{1,0:T(8,128)(2,1)S(1)}, f32[1536,1]{1,0:T(8,128)S(1)}) custom-call(bf16[1536,2560]{1,0:T(8,128)(2,1)} %get-tuple-element.55.tokens_ref.tokens_all, f32[1,2560]{1,0:T(1,128)S(1)} %reshape.103.gain_ref, bf16[2560,1024]{1,0:T(8,128)(2,1)} %get-tuple-element.56.weight_ref, ...), custom_call_target="tpu_custom_call" | custom-call | flops 8053063680 | bytes 20971520 | tf_op jit(solution)/shard_map/project/pallas_call | solution.py:165
  202.6 6.4 fusion.9.query_ref.all_ref
  211.7 25.7 %attend.1 = (bf16[1536,640]{1,0:T(8,128)(2,1)S(1)}, f32[8,1536]{1,0:T(8,128)S(1)}) custom-call(s32[6]{0:T(128)S(1)} %and_select_fusion.first_ref, bf16[1536,960]{1,0:T(8,128)(2,1)S(1)} %copy-done.2, bf16[1536,960]{1,0:T(8,128)(2,1)S(1)} %copy-done.2, s32[1,1536]{1,0:T(1,128)S(1)} %broadcast_in_dim.51.start_ref, s32[1536,1]{1,0:T(8,128)S(1)} %broadcast_in_dim.56.pad_ref), custom_call_target="tpu_custom_call" | custom-call | flops 49999998976 | bytes 1474560 | tf_op jit(solution)/shard_map/attend/pallas_call | solution.py:276
  237.5 4.3 fusion.10.attended
  241.8 8.5 convolution_convert_fusion.partial
  250.4 203.3 %middle.1 = (f32[384,2560]{1,0:T(8,128)}, bf16[1536,2560]{1,0:T(8,128)(2,1)}, bf16[1536,2560]{1,0:T(8,128)(2,1)}, bf16[2560,1792]{1,0:T(8,128)(2,1)}, bf16[2560,...) custom-call(bf16[1536,2560]{1,0:T(8,128)(2,1)} %convolution_convert_, ...), custom_call_target="tpu_custom_call" | custom-call | tf_op jit(solution)/shard_map/middle/pallas_call | solution.py:1415
  453.7 64.5 %hidden_back.1 = (bf16[1536,1792]{1,0:T(8,128)(2,1)}, bf16[1536,1792]{1,0:T(8,128)(2,1)}, bf16[1536,2560]{1,0:T(8,128)(2,1)}) custom-call(bf16[1536,2560]{1,0:T(8,128)(2,1)} %get-tuple-element.65.cot_all, bf16[2560,1792]{1,0:T(8,128)(2,1)} %get-tuple-element.66.down_full, f32[1536,1792]{1,0:T(8,128)} %get-tuple-element.67.gate_values, ...), custom_call_target="tpu_custom_call" | custom-call | flops 42278584320 | bytes 42278584 | tf_op jit(solution)/shard_map/hidden_back/pallas_call | solution.py:1665
  518.2 182.4 %turn_back.1 = (f32[384,2560]{1,0:T(8,128)}, f32[1,2560]{1,0:T(1,128)}, f32[320,1792]{1,0:T(8,128)}, f32[320,1792]{1,0:T(8,128)}, bf16[2,320,1792]{2,1,0:T(8,128...) custom-call(bf16[1536,2560]{1,0:T(8,128)(2,1)} %get-tuple-element.71, ...), custom_call_target="tpu_custom_call" | custom-call | tf_op jit(solution)/shard_map/turn_back/pallas_call | solution.py:1598
  700.7 15.4 %fusion.11.grad_ref = bf16[1536,640]{1,0:T(8,128)(2,1)} fusion(s32[1536]{0:T(1024)S(1)} %slice.84, bf16[1536,2560]{1,0:T(8,128)(2,1)} %get-tuple-element.76.grad_rows, bf16[2560,640]{1,0:T(8,128)(2,1)} %get-tuple-element.59), kind=kOutput, calls=%fused_computation.18 | convolution fusion | flops 8057389056 | bytes 13113344 | tf_op jit(solution)/shard_map/dot_general | solution.py:25
  726.8 42.3 %attend_back.1 = (bf16[1536,640]{1,0:T(8,128)(2,1)S(1)}, bf16[1536,320]{1,0:T(8,128)(2,1)S(1)}) custom-call(s32[6]{0:T(128)S(1)} %and_select_fusion.first_ref, bf16[1536,960]{1,0:T(8,128)(2,1)} %fusion.9.query_ref.all_ref, bf16[1536,960]{1,0:T(8,128)(2,1)} %fusion.9.query_ref.all_ref, s32[1,1536]{1,0:T(1,128)S(1)} %broadcast_in_dim.51.start_ref, ...), custom_call_target="tpu_custom_call" | custom-call | flops 49999998976 | bytes 1474560 | tf_op jit(solution)/shard_map/attend_back/pallas_call | solution.py:412
  771.5 14.3 %collective-permute-done.6 = bf16[384,2560]{1,0:T(8,128)(2,1)S(1)} collective-permute-done((bf16[384,2560]{1,0:T(8,128)(2,1)}, bf16[384,2560]{1,0:T(8,128)(2,1)S(1)}, u32[]{:S(2)}, u32[]{:S(2)}) %collective-permute-start.6) | collective-permute-done | bytes 1966112 | tf_op jit(solution)/shard_map/ppermute | solution.py:65
  785.8 3.6 fusion.22
  793.4 4.1 collective-permute-start.13
  797.5 6.7 fusion.8.grad_heads
  804.2 4.3 fusion.16
  810.5 13.5 %multiply_reduce_fusion = (f32[2560]{0:T(1024)S(1)}, bf16[1536,2560]{1,0:T(8,128)(2,1)}) fusion(bf16[1536,2560]{1,0:T(8,128)(2,1)S(1)} %bitcast.58, f32[1536]{0:T(1024)S(1)} %copy-done.19, bf16[1536,1024]{1,0:T(8,128)(2,1)} %fusion.8.grad_heads, bf16[2560,1024]{1,0:T(8,128)(2,1)} %get-tuple-element.56.weight_ref), kind=kOutput, calls=%fused_computation | convolution fusion | flops 8072721920 | bytes 24133632 | tf_op jit(solution)/shard_map/dot_general | solution.py:25
  828.4 5.9 collective-permute-done.11
  834.8 6.7 convert_select_fusion.1
  841.5 183.9 %tail.1 = (f32[384,2560]{1,0:T(8,128)}, f32[320,1792]{1,0:T(8,128)}, f32[320,640]{1,0:T(8,128)}, f32[320,1024]{1,0:T(8,128)}, bf16[6,320,640]{2,1,0:T(8,128)(2,1...) custom-call(bf16[1536,2560]{1,0:T(8,128)(2,1)} %get-tuple-element.84.partial, ...), custom_call_target="tpu_custom_call" | custom-call | tf_op jit(solution)/shard_map/tail/pallas_call | solution.py:1203
  1032.3 3.8 fusion.12
  1036.1 4.2 convert_select_fusion
  (121 shorter events, 57.7 us)
Async XLA Ops:
  6.7 143.6 %copy-start.5 = (bf16[320,1792]{1,0:T(8,128)(2,1)}, bf16[320,1792]{1,0:T(8,128)(2,1)S(1)}, u32[]{:S(2)}) copy-start(bf16[320,1792]{1,0:T(8,128)(2,1)S(1)} %pad.20.up) | copy-start | bytes 3440644
  8.0 160.0 %copy-start.16 = (s32[1536]{0:T(1024)S(1)}, s32[1536]{0:T(1024)}, u32[]{:S(2)}) copy-start(s32[1536]{0:T(1024)} %param.28) | copy-start | bytes 18436
  8.0 160.0 %copy-start.17 = (s32[1536]{0:T(1024)S(1)}, s32[1536]{0:T(1024)}, u32[]{:S(2)}) copy-start(s32[1536]{0:T(1024)} %param.27) | copy-start | bytes 18436
  8.0 160.0 %copy-start.21 = (s32[1,3]{1,0:T(1,128)S(1)}, s32[1,3]{1,0:T(1,128)}, u32[]{:S(2)}) copy-start(s32[1,3]{1,0:T(1,128)} %param.26) | copy-start | bytes 40
  8.0 162.5 %copy-start.13 = (bf16[1728,320]{0,1:T(8,128)(2,1)S(1)}, bf16[1728,320]{0,1:T(8,128)(2,1)}, u32[]{:S(2)}) copy-start(bf16[1728,320]{0,1:T(8,128)(2,1)} %param.24) | copy-start | bytes 3317764
  148.5 101.8 %collective-permute-start.3 = (bf16[320,1792]{1,0:T(8,128)(2,1)S(1)}, bf16[320,1792]{1,0:T(8,128)(2,1)}, u32[]{:S(2)}, u32[]{:S(2)}) collective-permute-start(bf16[320,1792]{1,0:T(8,128)(2,1)S(1)} %pad.20.up), channel_id=1, source_target_pairs={{2,4},{3,5},{4,2},{5,3},{10,12},{11,13},{12,10},{13,11},{18,20},{1... | collective-permute-start | bytes 3440648 | tf_op jit(solution)/shard_map/ppermute | solution.py:65
  150.3 100.0 %collective-permute-start.2 = (bf16[320,1792]{1,0:T(8,128)(2,1)S(1)}, bf16[320,1792]{1,0:T(8,128)(2,1)}, u32[]{:S(2)}, u32[]{:S(2)}) collective-permute-start(bf16[320,1792]{1,0:T(8,128)(2,1)S(1)} %pad.20.up), channel_id=1, source_target_pairs={{0,2},{1,3},{2,6},{3,7},{4,0},{5,1},{6,4},{7,5},{8,10},{9,11},{10,... | collective-permute-start | bytes 3440648 | tf_op jit(solution)/shard_map/ppermute | solution.py:65
  165.0 85.4 %collective-permute-start.5 = (bf16[640,1792]{1,0:T(8,128)(2,1)}, bf16[640,1792]{1,0:T(8,128)(2,1)}, u32[]{:S(2)}, u32[]{:S(2)}) collective-permute-start(bf16[640,1792]{1,0:T(8,128)(2,1)} %get-tuple-element.62.gate_unit), channel_id=1, source_target_pairs={{0,16},{1,17},{2,18},{3,19},{4,20},{5,21},{6,22},{7,23},{8,24},{9,... | collective-permute-start | bytes 6881288 | tf_op jit(solution)/shard_map/ppermute | solution.py:65
  166.5 83.9 %collective-permute-start.4 = (bf16[640,1792]{1,0:T(8,128)(2,1)}, bf16[640,1792]{1,0:T(8,128)(2,1)}, u32[]{:S(2)}, u32[]{:S(2)}) collective-permute-start(bf16[640,1792]{1,0:T(8,128)(2,1)} %get-tuple-element.62.gate_unit), channel_id=1, source_target_pairs={{0,8},{1,9},{2,10},{3,11},{4,12},{5,13},{6,14},{7,15},{8,0},{9,1},... | collective-permute-start | bytes 6881288 | tf_op jit(solution)/shard_map/ppermute | solution.py:65
  168.0 4.9 collective-permute-start
  172.2 30.4 %copy-start = (f32[1,2560]{1,0:T(1,128)}, f32[1,2560]{1,0:T(1,128)S(1)}, u32[]{:S(2)}) copy-start(f32[1,2560]{1,0:T(1,128)S(1)} %reshape.103.gain_ref) | copy-start | bytes 30724
  172.9 77.4 %collective-permute-start.1 = (bf16[384,2560]{1,0:T(8,128)(2,1)}, bf16[384,2560]{1,0:T(8,128)(2,1)}, u32[]{:S(2)}, u32[]{:S(2)}) collective-permute-start(bf16[384,2560]{1,0:T(8,128)(2,1)} %cot.1), channel_id=1, source_target_pairs={{0,1},{1,0},{6,7},{7,6},{8,9},{9,8},{14,15},{15,14},{16,17},{17,16... | collective-permute-start | bytes 5898248 | tf_op jit(solution)/shard_map/ppermute | solution.py:65
  716.1 69.7 %collective-permute-start.6 = (bf16[384,2560]{1,0:T(8,128)(2,1)}, bf16[384,2560]{1,0:T(8,128)(2,1)S(1)}, u32[]{:S(2)}, u32[]{:S(2)}) collective-permute-start(bf16[384,2560]{1,0:T(8,128)(2,1)} %bitcast.67), channel_id=1, source_target_pairs={{0,1},{1,0},{2,3},{3,2},{4,5},{5,4},{6,7},{7,6},{8,9},{9,8},{10,11... | collective-permute-start | bytes 5898248 | tf_op jit(solution)/shard_map/ppermute | solution.py:65
  716.4 75.2 %collective-permute-start.12 = (bf16[2,320,1792]{2,1,0:T(8,128)(2,1)}, bf16[2,320,1792]{2,1,0:T(8,128)(2,1)S(1)}, u32[]{:S(2)}, u32[]{:S(2)}) collective-permute-start(bf16[2,320,1792]{2,1,0:T(8,128)(2,1)} %get-tuple-element.95), channel_id=1, source_target_pairs={{2,0},{3,1},{4,6},{5,7},{10,8},{11,9},{12,14},{13,15},{18,16},{19,... | collective-permute-start | bytes 6881288 | tf_op jit(solution)/shard_map/ppermute | solution.py:65
  722.1 75.4 %collective-permute-start.8 = (bf16[2,320,1792]{2,1,0:T(8,128)(2,1)}, bf16[2,320,1792]{2,1,0:T(8,128)(2,1)}, u32[]{:S(2)}, u32[]{:S(2)}) collective-permute-start(bf16[2,320,1792]{2,1,0:T(8,128)(2,1)} %pad_maximum_fusion), channel_id=1, source_target_pairs={{0,8},{1,9},{2,10},{3,11},{4,12},{5,13},{6,14},{7,15},{8,0},{9,1},... | collective-permute-start | bytes 6881288 | tf_op jit(solution)/shard_map/ppermute | solution.py:65
  726.8 70.6 %collective-permute-start.9 = (bf16[2,320,1792]{2,1,0:T(8,128)(2,1)}, bf16[2,320,1792]{2,1,0:T(8,128)(2,1)}, u32[]{:S(2)}, u32[]{:S(2)}) collective-permute-start(bf16[2,320,1792]{2,1,0:T(8,128)(2,1)} %pad_maximum_fusion.1), channel_id=1, source_target_pairs={{0,16},{1,17},{2,18},{3,19},{4,20},{5,21},{6,22},{7,23},{8,24},{9,... | collective-permute-start | bytes 6881288 | tf_op jit(solution)/shard_map/ppermute | solution.py:65
  726.8 42.4 %copy-start.7 = (f32[320,1792]{1,0:T(8,128)S(1)}, f32[320,1792]{1,0:T(8,128)}, u32[]{:S(2)}) copy-start(f32[320,1792]{1,0:T(8,128)} %get-tuple-element.98) | copy-start | bytes 6881284
  770.7 15.1 %copy-start.4 = (f32[384,2560]{1,0:T(8,128)S(1)}, f32[384,2560]{1,0:T(8,128)}, u32[]{:S(2)}) copy-start(f32[384,2560]{1,0:T(8,128)} %get-tuple-element.78.residual_ref) | copy-start | bytes 11796484
  770.7 15.1 %copy-start.10 = (bf16[384,2560]{1,0:T(8,128)(2,1)S(1)}, bf16[384,2560]{1,0:T(8,128)(2,1)}, u32[]{:S(2)}) copy-start(bf16[384,2560]{1,0:T(8,128)(2,1)} %get-tuple-element.79) | copy-start | bytes 5898244
  789.4 246.7 %collective-permute-start.7 = (bf16[384,2560]{1,0:T(8,128)(2,1)}, bf16[384,2560]{1,0:T(8,128)(2,1)}, u32[]{:S(2)}, u32[]{:S(2)}) collective-permute-start(bf16[384,2560]{1,0:T(8,128)(2,1)} %get-tuple-element.152), channel_id=1, source_target_pairs={{2,4},{3,5},{4,2},{5,3},{10,12},{11,13},{12,10},{13,11},{18,20},{1... | collective-permute-start | bytes 5898248 | tf_op jit(solution)/shard_map/ppermute | solution.py:65
  791.9 18.6 %slice-start = ((s8[7864320]{0:T(1024)(128)(4,1)}), s8[4194304]{0:T(1024)(128)(4,1)S(1)}, s32[]{:S(2)}) async-start(s8[7864320]{0:T(1024)(128)(4,1)} %bitcast.57), calls=%async_computation | async-start | bytes 8388608
  793.4 238.9 %collective-permute-start.13 = (bf16[320,1792]{1,0:T(8,128)(2,1)}, bf16[320,1792]{1,0:T(8,128)(2,1)}, u32[]{:S(2)}, u32[]{:S(2)}) collective-permute-start(bf16[320,1792]{1,0:T(8,128)(2,1)} %get-tuple-element.162), channel_id=1, source_target_pairs={{0,4},{1,5},{6,2},{7,3},{8,12},{9,13},{14,10},{15,11},{16,20},{17,... | collective-permute-start | bytes 3440648 | tf_op jit(solution)/shard_map/ppermute | solution.py:65
  808.5 25.8 %collective-permute-start.11 = (bf16[320,1792]{1,0:T(8,128)(2,1)}, bf16[320,1792]{1,0:T(8,128)(2,1)S(1)}, u32[]{:S(2)}, u32[]{:S(2)}) collective-permute-start(bf16[320,1792]{1,0:T(8,128)(2,1)} %get-tuple-element.156), channel_id=1, source_target_pairs={{0,8},{1,9},{2,10},{3,11},{4,12},{5,13},{6,14},{7,15},{8,0},{9,1},... | collective-permute-start | bytes 3440648 | tf_op jit(solution)/shard_map/ppermute | solution.py:65
  809.2 25.6 %collective-permute-start.10 = (bf16[320,1792]{1,0:T(8,128)(2,1)}, bf16[320,1792]{1,0:T(8,128)(2,1)}, u32[]{:S(2)}, u32[]{:S(2)}) collective-permute-start(bf16[320,1792]{1,0:T(8,128)(2,1)} %get-tuple-element.157), channel_id=1, source_target_pairs={{0,16},{1,17},{2,18},{3,19},{4,20},{5,21},{6,22},{7,23},{8,24},{9,... | collective-permute-start | bytes 3440648 | tf_op jit(solution)/shard_map/ppermute | solution.py:65
  (15 other events, 79.4 us)

commit v7 on v6

--- a/solution.py
+++ b/solution.py
@@ -1640,7 +1640,7 @@
         up_out[...] = (grad_hidden * gate).astype(jnp.bfloat16)
 
     product(
-        cot_all, down_full, gate_signal, 1, 0, 256, 1024, signals, (gate_values, up_values), (up_signal,)
+        cot_all, down_full, gate_signal, 1, 0, 512, 1024, signals, (gate_values, up_values), (up_signal,)
     )
     count, width = partial.shape
     depth = gate_full.shape[1]

time: 1050 us -> 1050 us (level)
  transfers between devices with their start and end apart: 14 -> 14, of which waited for: 3 -> 3; matrix products, arithmetic and copies ran while one was open for 8% -> 8% of each run, Pallas kernels for 26% -> 27%
where the time goes in v7:
time: 1050 us
  Pallas kernels  872 us (83%)
  matrix products  54.8 us (5%)
  starting transfers between devices  38.5 us (4%)
  other arithmetic  33.7 us (3%)
  local copies, waits for them, and re-layouts  32.2 us (3%)
  waiting for transfers between devices  12.8 us (1%)
    pallas_call x1, Pallas kernels, middle(): pl.pallas_call(functools.partial(middle_kernel, dp_count, tensor_count, l...  202 us
    pallas_call x1, Pallas kernels, tail(): pl.pallas_call(functools.partial(tail_kernel, dp_count, tensor_count, gai...  184 us
    pallas_call x1, Pallas kernels, turn_back(): pl.pallas_call(functools.partial(turn_back_kernel, dp_count, tensor_count...  179 us
    pallas_call x1, Pallas kernels, gather_first(): pl.pallas_call(functools.partial(gather_first_kernel, dp_count, tensor_co...  141 us
    pallas_call x1, Pallas kernels, hidden_back(): pl.pallas_call(hidden_back_kernel, out_shape=[signal, signal, jax.ShapeDt...  63.1 us
    dot_general x6, matrix products, contract(): lax.dot_general(left, right, (((left_dim,), (right_dim,)), ((), ())), pre...  54.8 us
    pallas_call x1, Pallas kernels, attend_back(): pl.pallas_call(functools.partial(attend_back_kernel, kv_heads, group), gr...  50.3 us
    ppermute x14, starting transfers between devices, move(): return lax.ppermute(array, AXES, pairs)  38.5 us
  transfers between devices with their start and end apart: 14, of which 3 were waited for; matrix products, arithmetic and copies ran while one was open for 8% of the time, Pallas kernels for 27%

profile of v7, /device:TPU:0, one launch (start us, length us, event | category | flops | bytes accessed | tf_op | source)
XLA Modules:
  0.0 1045.2 jit_solution(10918878066688140053)
XLA Ops:
  8.0 140.6 %gather_first.1 = (bf16[1536,2560]{1,0:T(8,128)(2,1)}, bf16[2560,1024]{1,0:T(8,128)(2,1)}, bf16[2560,640]{1,0:T(8,128)(2,1)}, bf16[640,1792]{1,0:T(8,128)(2,1)}) custom-call(bf16[384,2560]{1,0:T(8,128)(2,1)} %tokens.1, bf16[320,1024]{1,0:T(8,128)(2,1)} %pad.18.first, bf16[320,640]{1,0:T(8,128)(2,1)} %bitcast.62, bf16[320,1792]{1,0:T(8,128)(2,1)} %pad.19.gate), custom_call_target="tpu_custom_call" | custom-call | tf_op jit(solution)/shard_map/gather_first/pallas_call | solution.py:1278
  150.3 14.7 %collective-permute-start.2 = (bf16[320,1792]{1,0:T(8,128)(2,1)S(1)}, bf16[320,1792]{1,0:T(8,128)(2,1)}, u32[]{:S(2)}, u32[]{:S(2)}) collective-permute-start(bf16[320,1792]{1,0:T(8,128)(2,1)S(1)} %pad.20.up), channel_id=1, source_target_pairs={{0,2},{1,3},{2,6},{3,7},{4,0},{5,1},{6,4},{7,5},{8,10},{9,11},{10,... | collective-permute-start | bytes 3440648 | tf_op jit(solution)/shard_map/ppermute | solution.py:65
  172.9 5.7 collective-permute-start.1
  181.1 21.5 %project.1 = (bf16[1536,2560]{1,0:T(8,128)(2,1)}, bf16[1536,960]{1,0:T(8,128)(2,1)S(1)}, f32[1536,1]{1,0:T(8,128)S(1)}) custom-call(bf16[1536,2560]{1,0:T(8,128)(2,1)} %get-tuple-element.55.tokens_ref.tokens_all, f32[1,2560]{1,0:T(1,128)S(1)} %reshape.103.gain_ref, bf16[2560,1024]{1,0:T(8,128)(2,1)} %get-tuple-element.56.weight_ref, ...), custom_call_target="tpu_custom_call" | custom-call | flops 8053063680 | bytes 20971520 | tf_op jit(solution)/shard_map/project/pallas_call | solution.py:165
  202.6 6.4 fusion.9.query_ref.all_ref
  211.7 31.6 %attend.1 = (bf16[1536,640]{1,0:T(8,128)(2,1)S(1)}, f32[8,1536]{1,0:T(8,128)S(1)}) custom-call(s32[6]{0:T(128)S(1)} %and_select_fusion.first_ref, bf16[1536,960]{1,0:T(8,128)(2,1)S(1)} %copy-done.2, bf16[1536,960]{1,0:T(8,128)(2,1)S(1)} %copy-done.2, s32[1,1536]{1,0:T(1,128)S(1)} %broadcast_in_dim.51.start_ref, s32[1536,1]{1,0:T(8,128)S(1)} %broadcast_in_dim.56.pad_ref), custom_call_target="tpu_custom_call" | custom-call | flops 49999998976 | bytes 1474560 | tf_op jit(solution)/shard_map/attend/pallas_call | solution.py:276
  243.4 4.3 fusion.10.attended
  247.7 8.5 convolution_convert_fusion.partial
  256.3 201.9 %middle.1 = (f32[384,2560]{1,0:T(8,128)}, bf16[1536,2560]{1,0:T(8,128)(2,1)}, bf16[1536,2560]{1,0:T(8,128)(2,1)}, bf16[2560,1792]{1,0:T(8,128)(2,1)}, bf16[2560,...) custom-call(bf16[1536,2560]{1,0:T(8,128)(2,1)} %convolution_convert_, ...), custom_call_target="tpu_custom_call" | custom-call | tf_op jit(solution)/shard_map/middle/pallas_call | solution.py:1415
  458.2 63.1 %hidden_back.1 = (bf16[1536,1792]{1,0:T(8,128)(2,1)}, bf16[1536,1792]{1,0:T(8,128)(2,1)}, bf16[1536,2560]{1,0:T(8,128)(2,1)}) custom-call(bf16[1536,2560]{1,0:T(8,128)(2,1)} %get-tuple-element.65.cot_all, bf16[2560,1792]{1,0:T(8,128)(2,1)} %get-tuple-element.66.down_full, f32[1536,1792]{1,0:T(8,128)} %get-tuple-element.67.gate_values, ...), custom_call_target="tpu_custom_call" | custom-call | flops 42278584320 | bytes 42278584 | tf_op jit(solution)/shard_map/hidden_back/pallas_call | solution.py:1665
  521.3 178.9 %turn_back.1 = (f32[384,2560]{1,0:T(8,128)}, f32[1,2560]{1,0:T(1,128)}, f32[320,1792]{1,0:T(8,128)}, f32[320,1792]{1,0:T(8,128)}, bf16[2,320,1792]{2,1,0:T(8,128...) custom-call(bf16[1536,2560]{1,0:T(8,128)(2,1)} %get-tuple-element.71, ...), custom_call_target="tpu_custom_call" | custom-call | tf_op jit(solution)/shard_map/turn_back/pallas_call | solution.py:1598
  700.2 15.4 %fusion.11.grad_ref = bf16[1536,640]{1,0:T(8,128)(2,1)} fusion(s32[1536]{0:T(1024)S(1)} %slice.84, bf16[1536,2560]{1,0:T(8,128)(2,1)} %get-tuple-element.76.grad_rows, bf16[2560,640]{1,0:T(8,128)(2,1)} %get-tuple-element.59), kind=kOutput, calls=%fused_computation.18 | convolution fusion | flops 8057389056 | bytes 13113344 | tf_op jit(solution)/shard_map/dot_general | solution.py:25
  726.5 50.3 %attend_back.1 = (bf16[1536,640]{1,0:T(8,128)(2,1)S(1)}, bf16[1536,320]{1,0:T(8,128)(2,1)S(1)}) custom-call(s32[6]{0:T(128)S(1)} %and_select_fusion.first_ref, bf16[1536,960]{1,0:T(8,128)(2,1)} %fusion.9.query_ref.all_ref, bf16[1536,960]{1,0:T(8,128)(2,1)} %fusion.9.query_ref.all_ref, s32[1,1536]{1,0:T(1,128)S(1)} %broadcast_in_dim.51.start_ref, ...), custom_call_target="tpu_custom_call" | custom-call | flops 49999998976 | bytes 1474560 | tf_op jit(solution)/shard_map/attend_back/pallas_call | solution.py:412
  779.1 6.3 collective-permute-done.6
  785.4 3.6 fusion.22
  792.9 4.1 collective-permute-start.13
  797.1 6.7 fusion.8.grad_heads
  803.8 4.3 fusion.16
  810.1 13.5 %multiply_reduce_fusion = (f32[2560]{0:T(1024)S(1)}, bf16[1536,2560]{1,0:T(8,128)(2,1)}) fusion(bf16[1536,2560]{1,0:T(8,128)(2,1)S(1)} %bitcast.58, f32[1536]{0:T(1024)S(1)} %copy-done.19, bf16[1536,1024]{1,0:T(8,128)(2,1)} %fusion.8.grad_heads, bf16[2560,1024]{1,0:T(8,128)(2,1)} %get-tuple-element.56.weight_ref), kind=kOutput, calls=%fused_computation | convolution fusion | flops 8072721920 | bytes 24133632 | tf_op jit(solution)/shard_map/dot_general | solution.py:25
  827.9 5.9 collective-permute-done.11
  834.4 6.7 convert_select_fusion.1
  841.2 183.9 %tail.1 = (f32[384,2560]{1,0:T(8,128)}, f32[320,1792]{1,0:T(8,128)}, f32[320,640]{1,0:T(8,128)}, f32[320,1024]{1,0:T(8,128)}, bf16[6,320,640]{2,1,0:T(8,128)(2,1...) custom-call(bf16[1536,2560]{1,0:T(8,128)(2,1)} %get-tuple-element.84.partial, ...), custom_call_target="tpu_custom_call" | custom-call | tf_op jit(solution)/shard_map/tail/pallas_call | solution.py:1203
  1032.0 3.8 fusion.12
  1035.8 4.2 convert_select_fusion
  (121 shorter events, 57.9 us)
Async XLA Ops:
  6.7 143.6 %copy-start.5 = (bf16[320,1792]{1,0:T(8,128)(2,1)}, bf16[320,1792]{1,0:T(8,128)(2,1)S(1)}, u32[]{:S(2)}) copy-start(bf16[320,1792]{1,0:T(8,128)(2,1)S(1)} %pad.20.up) | copy-start | bytes 3440644
  8.0 160.0 %copy-start.16 = (s32[1536]{0:T(1024)S(1)}, s32[1536]{0:T(1024)}, u32[]{:S(2)}) copy-start(s32[1536]{0:T(1024)} %param.28) | copy-start | bytes 18436
  8.0 160.0 %copy-start.17 = (s32[1536]{0:T(1024)S(1)}, s32[1536]{0:T(1024)}, u32[]{:S(2)}) copy-start(s32[1536]{0:T(1024)} %param.27) | copy-start | bytes 18436
  8.0 160.0 %copy-start.21 = (s32[1,3]{1,0:T(1,128)S(1)}, s32[1,3]{1,0:T(1,128)}, u32[]{:S(2)}) copy-start(s32[1,3]{1,0:T(1,128)} %param.26) | copy-start | bytes 40
  8.0 162.5 %copy-start.13 = (bf16[1728,320]{0,1:T(8,128)(2,1)S(1)}, bf16[1728,320]{0,1:T(8,128)(2,1)}, u32[]{:S(2)}) copy-start(bf16[1728,320]{0,1:T(8,128)(2,1)} %param.24) | copy-start | bytes 3317764
  148.5 107.7 %collective-permute-start.3 = (bf16[320,1792]{1,0:T(8,128)(2,1)S(1)}, bf16[320,1792]{1,0:T(8,128)(2,1)}, u32[]{:S(2)}, u32[]{:S(2)}) collective-permute-start(bf16[320,1792]{1,0:T(8,128)(2,1)S(1)} %pad.20.up), channel_id=1, source_target_pairs={{2,4},{3,5},{4,2},{5,3},{10,12},{11,13},{12,10},{13,11},{18,20},{1... | collective-permute-start | bytes 3440648 | tf_op jit(solution)/shard_map/ppermute | solution.py:65
  150.3 105.9 %collective-permute-start.2 = (bf16[320,1792]{1,0:T(8,128)(2,1)S(1)}, bf16[320,1792]{1,0:T(8,128)(2,1)}, u32[]{:S(2)}, u32[]{:S(2)}) collective-permute-start(bf16[320,1792]{1,0:T(8,128)(2,1)S(1)} %pad.20.up), channel_id=1, source_target_pairs={{0,2},{1,3},{2,6},{3,7},{4,0},{5,1},{6,4},{7,5},{8,10},{9,11},{10,... | collective-permute-start | bytes 3440648 | tf_op jit(solution)/shard_map/ppermute | solution.py:65
  165.0 91.3 %collective-permute-start.5 = (bf16[640,1792]{1,0:T(8,128)(2,1)}, bf16[640,1792]{1,0:T(8,128)(2,1)}, u32[]{:S(2)}, u32[]{:S(2)}) collective-permute-start(bf16[640,1792]{1,0:T(8,128)(2,1)} %get-tuple-element.62.gate_unit), channel_id=1, source_target_pairs={{0,16},{1,17},{2,18},{3,19},{4,20},{5,21},{6,22},{7,23},{8,24},{9,... | collective-permute-start | bytes 6881288 | tf_op jit(solution)/shard_map/ppermute | solution.py:65
  166.5 89.8 %collective-permute-start.4 = (bf16[640,1792]{1,0:T(8,128)(2,1)}, bf16[640,1792]{1,0:T(8,128)(2,1)}, u32[]{:S(2)}, u32[]{:S(2)}) collective-permute-start(bf16[640,1792]{1,0:T(8,128)(2,1)} %get-tuple-element.62.gate_unit), channel_id=1, source_target_pairs={{0,8},{1,9},{2,10},{3,11},{4,12},{5,13},{6,14},{7,15},{8,0},{9,1},... | collective-permute-start | bytes 6881288 | tf_op jit(solution)/shard_map/ppermute | solution.py:65
  168.0 4.9 collective-permute-start
  172.2 30.4 %copy-start = (f32[1,2560]{1,0:T(1,128)}, f32[1,2560]{1,0:T(1,128)S(1)}, u32[]{:S(2)}) copy-start(f32[1,2560]{1,0:T(1,128)S(1)} %reshape.103.gain_ref) | copy-start | bytes 30724
  172.9 83.3 %collective-permute-start.1 = (bf16[384,2560]{1,0:T(8,128)(2,1)}, bf16[384,2560]{1,0:T(8,128)(2,1)}, u32[]{:S(2)}, u32[]{:S(2)}) collective-permute-start(bf16[384,2560]{1,0:T(8,128)(2,1)} %cot.1), channel_id=1, source_target_pairs={{0,1},{1,0},{6,7},{7,6},{8,9},{9,8},{14,15},{15,14},{16,17},{17,16... | collective-permute-start | bytes 5898248 | tf_op jit(solution)/shard_map/ppermute | solution.py:65
  715.6 69.7 %collective-permute-start.6 = (bf16[384,2560]{1,0:T(8,128)(2,1)}, bf16[384,2560]{1,0:T(8,128)(2,1)S(1)}, u32[]{:S(2)}, u32[]{:S(2)}) collective-permute-start(bf16[384,2560]{1,0:T(8,128)(2,1)} %bitcast.67), channel_id=1, source_target_pairs={{0,1},{1,0},{2,3},{3,2},{4,5},{5,4},{6,7},{7,6},{8,9},{9,8},{10,11... | collective-permute-start | bytes 5898248 | tf_op jit(solution)/shard_map/ppermute | solution.py:65
  715.9 75.2 %collective-permute-start.12 = (bf16[2,320,1792]{2,1,0:T(8,128)(2,1)}, bf16[2,320,1792]{2,1,0:T(8,128)(2,1)S(1)}, u32[]{:S(2)}, u32[]{:S(2)}) collective-permute-start(bf16[2,320,1792]{2,1,0:T(8,128)(2,1)} %get-tuple-element.95), channel_id=1, source_target_pairs={{2,0},{3,1},{4,6},{5,7},{10,8},{11,9},{12,14},{13,15},{18,16},{19,... | collective-permute-start | bytes 6881288 | tf_op jit(solution)/shard_map/ppermute | solution.py:65
  721.6 75.4 %collective-permute-start.8 = (bf16[2,320,1792]{2,1,0:T(8,128)(2,1)}, bf16[2,320,1792]{2,1,0:T(8,128)(2,1)}, u32[]{:S(2)}, u32[]{:S(2)}) collective-permute-start(bf16[2,320,1792]{2,1,0:T(8,128)(2,1)} %pad_maximum_fusion), channel_id=1, source_target_pairs={{0,8},{1,9},{2,10},{3,11},{4,12},{5,13},{6,14},{7,15},{8,0},{9,1},... | collective-permute-start | bytes 6881288 | tf_op jit(solution)/shard_map/ppermute | solution.py:65
  726.5 70.6 %collective-permute-start.9 = (bf16[2,320,1792]{2,1,0:T(8,128)(2,1)}, bf16[2,320,1792]{2,1,0:T(8,128)(2,1)}, u32[]{:S(2)}, u32[]{:S(2)}) collective-permute-start(bf16[2,320,1792]{2,1,0:T(8,128)(2,1)} %pad_maximum_fusion.1), channel_id=1, source_target_pairs={{0,16},{1,17},{2,18},{3,19},{4,20},{5,21},{6,22},{7,23},{8,24},{9,... | collective-permute-start | bytes 6881288 | tf_op jit(solution)/shard_map/ppermute | solution.py:65
  726.5 50.3 %copy-start.7 = (f32[320,1792]{1,0:T(8,128)S(1)}, f32[320,1792]{1,0:T(8,128)}, u32[]{:S(2)}) copy-start(f32[320,1792]{1,0:T(8,128)} %get-tuple-element.98) | copy-start | bytes 6881284
  789.0 246.8 %collective-permute-start.7 = (bf16[384,2560]{1,0:T(8,128)(2,1)}, bf16[384,2560]{1,0:T(8,128)(2,1)}, u32[]{:S(2)}, u32[]{:S(2)}) collective-permute-start(bf16[384,2560]{1,0:T(8,128)(2,1)} %get-tuple-element.152), channel_id=1, source_target_pairs={{2,4},{3,5},{4,2},{5,3},{10,12},{11,13},{12,10},{13,11},{18,20},{1... | collective-permute-start | bytes 5898248 | tf_op jit(solution)/shard_map/ppermute | solution.py:65
  791.5 18.6 %slice-start = ((s8[7864320]{0:T(1024)(128)(4,1)}), s8[4194304]{0:T(1024)(128)(4,1)S(1)}, s32[]{:S(2)}) async-start(s8[7864320]{0:T(1024)(128)(4,1)} %bitcast.57), calls=%async_computation | async-start | bytes 8388608
  792.9 239.0 %collective-permute-start.13 = (bf16[320,1792]{1,0:T(8,128)(2,1)}, bf16[320,1792]{1,0:T(8,128)(2,1)}, u32[]{:S(2)}, u32[]{:S(2)}) collective-permute-start(bf16[320,1792]{1,0:T(8,128)(2,1)} %get-tuple-element.162), channel_id=1, source_target_pairs={{0,4},{1,5},{6,2},{7,3},{8,12},{9,13},{14,10},{15,11},{16,20},{17,... | collective-permute-start | bytes 3440648 | tf_op jit(solution)/shard_map/ppermute | solution.py:65
  797.0 13.0 %slice-start.1 = ((s8[7864320]{0:T(1024)(128)(4,1)}), s8[3670016]{0:T(1024)(128)(4,1)S(1)}, s32[]{:S(2)}) async-start(s8[7864320]{0:T(1024)(128)(4,1)} %bitcast.57), calls=%async_computation.1 | async-start | bytes 7340032
  808.1 25.8 %collective-permute-start.11 = (bf16[320,1792]{1,0:T(8,128)(2,1)}, bf16[320,1792]{1,0:T(8,128)(2,1)S(1)}, u32[]{:S(2)}, u32[]{:S(2)}) collective-permute-start(bf16[320,1792]{1,0:T(8,128)(2,1)} %get-tuple-element.156), channel_id=1, source_target_pairs={{0,8},{1,9},{2,10},{3,11},{4,12},{5,13},{6,14},{7,15},{8,0},{9,1},... | collective-permute-start | bytes 3440648 | tf_op jit(solution)/shard_map/ppermute | solution.py:65
  808.8 14.8 %copy-start.18 = (f32[1,2560]{1,0:T(1,128)S(1)}, f32[1,2560]{1,0:T(1,128)}, u32[]{:S(2)}) copy-start(f32[1,2560]{1,0:T(1,128)} %get-tuple-element.87) | copy-start | bytes 30724
  808.8 25.6 %collective-permute-start.10 = (bf16[320,1792]{1,0:T(8,128)(2,1)}, bf16[320,1792]{1,0:T(8,128)(2,1)}, u32[]{:S(2)}, u32[]{:S(2)}) collective-permute-start(bf16[320,1792]{1,0:T(8,128)(2,1)} %get-tuple-element.157), channel_id=1, source_target_pairs={{0,16},{1,17},{2,18},{3,19},{4,20},{5,21},{6,22},{7,23},{8,24},{9,... | collective-permute-start | bytes 3440648 | tf_op jit(solution)/shard_map/ppermute | solution.py:65
  (15 other events, 65.5 us)
